TPU v7x, 256 devices: a whole 4x4x8 slice. The times are simulated.
256 devices in a mesh: space: 32 (over y, z_lo, core), edge: 8 (over z_hi, x).
Axes of the slice: x: 4, y: 4, z: 8 (z_hi: 2, z_lo: 4; z = z_hi * 4 + z_lo), core: 2. Of those that a mesh axis runs over, the one named last changes fastest.
Arguments:
- embeddings: bfloat16 [2048, 49, 128], P(('space', 'edge')), may hold values from -6 to 6
- species: int32 [2048], P(('space', 'edge')), may hold values from 0 to 99
- species_gain: float32 [100, 128], replicated, may hold values from 0.5 to 2
- sources: int32 [32768], P(('space', 'edge')), may hold values from 0 to 127
- targets: int32 [32768], P(('space', 'edge')), may hold values from 0 to 63
- counts: int32 [32], P('space'), may hold values from 512 to 1024, as said below
- send_left: int32 [32, 32], P('space'), may hold values from 0 to 63, as said below
- send_right: int32 [32, 32], P('space'), may hold values from 0 to 63, as said below
- rotations: bfloat16 [235, 32768], P(None, ('space', 'edge')), may hold values from -3 to 3
- radial_basis: bfloat16 [32768, 128], P(('space', 'edge')), may hold values from 0 to 1
- weight_radial: bfloat16 [128, 128], replicated, may hold values from -0.5 to 0.5
- weight_zero: bfloat16 [896, 896], replicated, may hold values from -0.1875 to 0.1875
- weight_one_real: bfloat16 [768, 768], replicated, may hold values from -0.15625 to 0.15625
- weight_one_imag: bfloat16 [768, 768], replicated, may hold values from -0.15625 to 0.15625
- weight_two_real: bfloat16 [640, 640], replicated, may hold values from -0.15625 to 0.15625
- weight_two_imag: bfloat16 [640, 640], replicated, may hold values from -0.15625 to 0.15625
- cotangent: bfloat16 [2048, 49, 128], P(('space', 'edge')), may hold values from -6 to 6
Outputs:
- updated: bfloat16 [2048, 49, 128], P(('space', 'edge'))
- grad_embeddings: float32 [2048, 49, 128], P(('space', 'edge'))
- grad_basis: float32 [32768, 128], P(('space', 'edge'))
Inputs may be any that keep to these rules, and one draw needn't show every extreme that they name: Each block's live slots are its first counts[b] slots; at least one block has all 1024 slots live. `send_left`: each row holds 32 distinct atom indices of its block. `send_right`: each row holds 32 distinct atom indices of its block.
All inputs are finite; a program needn't handle non-finite values.
Results may differ from a plain program's by a relative error of at most 0.0065.
Values may be sent and summed in bfloat16 or wider, within the bound.
No kernel may reach another device: no remote copies, remote signals or barrier semaphores. Data moves between devices by JAX's collectives and lax.ppermute only.
A program may use at most 128 MiB of HBM per device.

v0:
```python
import math

import jax
import jax.numpy as jnp
from jax import lax
from jax.sharding import PartitionSpec as P

MOMENTS = (0, 1, -1, 2, -2)


def from_behind(value, axis, steps):
    count = lax.axis_size(axis)
    pairs = [(source, (source + steps) % count) for source in range(count)]
    return lax.ppermute(value, axis, pairs)


def structure(coefficients):
    top_degree = math.isqrt(coefficients) - 1
    result = []
    offset = 0
    for degree in range(top_degree + 1):
        order_cap = min(degree, 2)
        rows_kept = 2 * order_cap + 1
        result.append((degree, order_cap, rows_kept, offset))
        offset += rows_kept * (2 * degree + 1)
    return result


def rotation_blocks(rotations, coefficients):
    blocks = []
    edge_total = rotations.shape[1]
    for degree, order_cap, rows_kept, offset in structure(coefficients):
        columns = 2 * degree + 1
        blocks.append(
            rotations[offset : offset + rows_kept * columns].reshape(rows_kept, columns, edge_total)
        )
    return blocks


def rotate_into(blocks, values):
    pieces = []
    for degree, rotation in enumerate(blocks):
        window = values[:, degree * degree : (degree + 1) * (degree + 1), :]
        pieces.append(
            jnp.einsum("ije,ejc->eic", rotation, window, preferred_element_type=jnp.float32)
        )
    return pieces


def rotate_back_major(blocks, pieces):
    outcome = [
        jnp.einsum("ije,eic->jec", rotation, fragment, preferred_element_type=jnp.float32)
        for rotation, fragment in zip(blocks, pieces)
    ]
    return jnp.concatenate(outcome, axis=0)


def split_orders(pieces):
    result = []
    for moment in MOMENTS:
        picked = []
        for fragment in pieces:
            center = (fragment.shape[1] - 1) // 2
            if center >= abs(moment):
                picked.append(fragment[:, center + moment])
        result.append(jnp.stack(picked, axis=1))
    return tuple(result)


def join_orders(orders):
    pieces = []
    for degree in range(orders[0].shape[1]):
        order_cap = min(degree, 2)
        picked = [
            orders[MOMENTS.index(moment)][:, degree - abs(moment)]
            for moment in range(-order_cap, order_cap + 1)
        ]
        pieces.append(jnp.stack(picked, axis=1))
    return pieces


def flatten(matrix):
    return matrix.reshape(matrix.shape[0], -1)


def product(left_side, right_side):
    return jnp.dot(left_side, right_side, preferred_element_type=jnp.float32)


def product_transposed(left_side, right_side):
    return lax.dot_general(
        left_side, right_side, (((1,), (1,)), ((), ())), preferred_element_type=jnp.float32
    )


def frame_mix(orders, weights):
    order_zero, one_up, one_down, two_up, two_down = [flatten(fragment) for fragment in orders]
    weight_zero, one_real, one_imag, two_real, two_imag = weights
    result = (
        product(order_zero, weight_zero),
        product(one_up, one_real) - product(one_down, one_imag),
        product(one_down, one_real) + product(one_up, one_imag),
        product(two_up, two_real) - product(two_down, two_imag),
        product(two_down, two_real) + product(two_up, two_imag),
    )
    return tuple((fragment.reshape(initial.shape) for fragment, initial in zip(result, orders)))


def frame_mix_transposed(grads, weights):
    order_zero, one_up, one_down, two_up, two_down = [flatten(fragment) for fragment in grads]
    weight_zero, one_real, one_imag, two_real, two_imag = weights
    result = (
        product_transposed(order_zero, weight_zero),
        product_transposed(one_up, one_real) + product_transposed(one_down, one_imag),
        product_transposed(one_down, one_real) - product_transposed(one_up, one_imag),
        product_transposed(two_up, two_real) + product_transposed(two_down, two_imag),
        product_transposed(two_down, two_real) - product_transposed(two_up, two_imag),
    )
    return tuple((fragment.reshape(initial.shape) for fragment, initial in zip(result, grads)))


def gating_forward(outputs):
    scalar = outputs[0][:, 0, :]
    gating = jax.nn.sigmoid(scalar)
    leading = jnp.concatenate(
        [jax.nn.silu(scalar)[:, None, :], outputs[0][:, 1:, :] * gating[:, None, :]], axis=1
    )
    return (leading,) + tuple((fragment * gating[:, None, :] for fragment in outputs[1:]))


def gating_backward(grads, outputs):
    scalar = outputs[0][:, 0, :]
    gating = jax.nn.sigmoid(scalar)
    gate_slope = gating * (1.0 - gating)
    weighted = sum(
        (jnp.sum(upstream * output_part, axis=1) for upstream, output_part in zip(grads, outputs))
    )
    lead_grad = grads[0][:, 0, :]
    grad_scalar = lead_grad * (gating + scalar * gate_slope) + gate_slope * (
        weighted - lead_grad * scalar
    )
    leading = jnp.concatenate(
        [grad_scalar[:, None, :], grads[0][:, 1:, :] * gating[:, None, :]], axis=1
    )
    return (leading,) + tuple((upstream * gating[:, None, :] for upstream in grads[1:]))


def forward_edges(gathered, live_mask, blocks, basis_rows, weight_radial, weights):
    turned = split_orders(rotate_into(blocks, gathered))
    radial_pre = product(basis_rows, weight_radial)
    radial = jax.nn.silu(radial_pre)
    scaled = tuple(((fragment * radial[:, None, :]).astype(jnp.bfloat16) for fragment in turned))
    outputs = frame_mix(scaled, weights)
    gated = tuple((fragment.astype(jnp.bfloat16) for fragment in gating_forward(outputs)))
    messages = (rotate_back_major(blocks, join_orders(gated)) * live_mask[None, :, None]).astype(
        jnp.bfloat16
    )
    return (messages, (turned, radial_pre, radial, outputs))


def backward_edges(kept_state, grad_messages, blocks, weight_radial, weights):
    turned, radial_pre, radial, outputs = kept_state
    grad_gated = split_orders(rotate_into(blocks, grad_messages))
    grad_outputs = tuple(
        (fragment.astype(jnp.bfloat16) for fragment in gating_backward(grad_gated, outputs))
    )
    grad_scaled = frame_mix_transposed(grad_outputs, weights)
    grad_radial = sum(
        (jnp.sum(upstream * fragment, axis=1) for upstream, fragment in zip(grad_scaled, turned))
    )
    radial_gate = jax.nn.sigmoid(radial_pre)
    grad_pre = (grad_radial * (radial_gate * (1.0 + radial_pre * (1.0 - radial_gate)))).astype(
        jnp.bfloat16
    )
    grad_basis = product_transposed(grad_pre, weight_radial)
    grad_turned = tuple(
        ((upstream * radial[:, None, :]).astype(jnp.bfloat16) for upstream in grad_scaled)
    )
    grad_gathered = rotate_back_major(blocks, join_orders(grad_turned))
    return (grad_gathered, grad_basis)


def on_device(
    embeddings,
    species,
    species_gain,
    sources,
    targets,
    counts,
    send_left,
    send_right,
    rotations,
    radial_basis,
    weight_radial,
    weight_zero,
    weight_one_real,
    weight_one_imag,
    weight_two_real,
    weight_two_imag,
    cotangent,
):
    weights = (weight_zero, weight_one_real, weight_one_imag, weight_two_real, weight_two_imag)
    atoms_here = embeddings.shape[0]
    edges_here = sources.shape[0]
    members = lax.axis_size("edge")
    member = lax.axis_index("edge")
    halo_rows = send_left.shape[1]
    block_atoms = atoms_here * members
    degree_scale = (atoms_here / edges_here) ** 0.5
    left_list = send_left[0]
    right_list = send_right[0]
    whole_block = lax.all_gather(embeddings, "edge", axis=0, tiled=True)
    arrived_left = from_behind(jnp.take(whole_block, right_list, axis=0), "space", 1)
    arrived_right = from_behind(jnp.take(whole_block, left_list, axis=0), "space", -1)
    row_table = jnp.concatenate([whole_block, arrived_left, arrived_right], axis=0)
    slot_ids = member * edges_here + lax.iota(jnp.int32, edges_here)
    live_mask = (slot_ids < counts[0]).astype(jnp.float32)
    blocks = rotation_blocks(rotations, embeddings.shape[1])
    gathered = jnp.take(row_table, sources, axis=0)
    messages, kept_state = forward_edges(
        gathered, live_mask, blocks, radial_basis, weight_radial, weights
    )
    rows_wanted = lax.iota(jnp.int32, lax.axis_size("edge") * atoms_here)
    one_hot = (rows_wanted[:, None] == targets[None, :]).astype(jnp.bfloat16)
    aggregate = lax.psum_scatter(
        jnp.einsum("ae,jec->ajc", one_hot, messages, preferred_element_type=jnp.float32).astype(
            jnp.bfloat16
        ),
        "edge",
        scatter_dimension=0,
        tiled=True,
    ).astype(jnp.float32)
    species_count = species_gain.shape[0]
    onehot = (species[:, None] == lax.iota(jnp.int32, species_count)[None, :]).astype(jnp.float32)
    gain_rows = jnp.dot(onehot, species_gain, precision=lax.Precision.HIGHEST)
    updated = (
        embeddings.astype(jnp.float32) + gain_rows[:, None, :] * degree_scale * aggregate
    ).astype(jnp.bfloat16)
    grad_aggregate = (cotangent.astype(jnp.float32) * gain_rows[:, None, :] * degree_scale).astype(
        jnp.bfloat16
    )
    grad_block = lax.all_gather(grad_aggregate, "edge", axis=0, tiled=True)
    grad_messages = jnp.take(grad_block, targets, axis=0) * live_mask[:, None, None].astype(
        jnp.bfloat16
    )
    grad_gathered, grad_basis = backward_edges(
        kept_state, grad_messages, blocks, weight_radial, weights
    )
    table_rows = block_atoms + 2 * halo_rows
    source_hot = (lax.iota(jnp.int32, table_rows)[:, None] == sources[None, :]).astype(jnp.float32)
    partial_value = jnp.einsum(
        "ae,jec->ajc",
        source_hot,
        grad_gathered,
        precision=lax.Precision.HIGHEST,
        preferred_element_type=jnp.float32,
    )
    own_rows = partial_value[:block_atoms]
    back_left = partial_value[block_atoms : block_atoms + halo_rows]
    back_right = partial_value[block_atoms + halo_rows :]
    home_right = from_behind(back_left.astype(jnp.bfloat16), "space", -1).astype(back_left.dtype)
    home_left = from_behind(back_right.astype(jnp.bfloat16), "space", 1).astype(back_right.dtype)
    own_rows = own_rows.at[right_list].add(home_right).at[left_list].add(home_left)
    summed_rows = lax.psum_scatter(
        own_rows.astype(jnp.bfloat16), "edge", scatter_dimension=0, tiled=True
    ).astype(jnp.float32)
    grad_embeddings = cotangent.astype(jnp.float32) + summed_rows
    return (updated, grad_embeddings, grad_basis)


def solution(mesh):
    placed = (
        P(("space", "edge"), None, None),
        P(("space", "edge")),
        P(),
        P(("space", "edge")),
        P(("space", "edge")),
        P("space"),
        P("space", None),
        P("space", None),
        P(None, ("space", "edge")),
        P(("space", "edge"), None),
        P(),
        P(),
        P(),
        P(),
        P(),
        P(),
        P(("space", "edge"), None, None),
    )
    return jax.shard_map(
        on_device,
        mesh=mesh,
        in_specs=placed,
        out_specs=(
            P(("space", "edge"), None, None),
            P(("space", "edge"), None, None),
            P(("space", "edge"), None),
        ),
        check_vma=False,
    )
```

profile of v0, /device:TPU:8, one launch (start us, length us, event | category | flops | bytes accessed | tf_op | source)
XLA Modules:
  0.0 461.0 jit_solution(17522446726706933073)
XLA Ops:
  8.6 48.3 %all_gather.6 = bf16[64,49,128]{2,0,1:T(8,128)(2,1)S(1)} all-gather(bf16[8,49,128]{2,0,1:T(8,128)(2,1)} %param.19), channel_id=1, replica_groups=mesh['space'=32,'edge'=8] {'edge'}, dimensions={0}, use_global_device_ids=true | all-gather | bytes 903168 | tf_op jit(solution)/shard_map/all_gather | solution.py:212
  60.7 4.4 collective-permute-start.1
  65.6 45.7 %all_gather.7 = bf16[64,49,128]{2,0,1:T(8,128)(2,1)S(1)} all-gather(bf16[8,49,128]{2,0,1:T(8,128)(2,1)S(1)} %copy.295), channel_id=1, replica_groups=mesh['space'=32,'edge'=8] {'edge'}, dimensions={0}, use_global_device_ids=true | all-gather | bytes 903168 | tf_op jit(solution)/shard_map/all_gather | solution.py:242
  112.5 2.0 gather_fusion.1
  114.5 1.8 fusion.3
  116.4 1.2 copy-done.5
  130.4 3.6 copy.260
  134.8 2.6 pad_maximum_fusion
  137.5 2.4 gather_fusion
  140.2 1.9 copy-done.6
  148.5 1.8 copy.259
  155.3 2.3 multiply_reduce_fusion.1
  159.3 1.2 copy.332
  160.4 1.8 copy.331
  162.6 2.0 fusion.89
  164.7 1.1 convolution_add_fusion.2
  165.8 1.9 copy.335
  167.7 1.9 copy.336
  169.6 2.5 multiply_reduce_fusion.7
  172.1 1.1 copy.274
  174.2 2.2 convolution_subtract_fusion.2
  176.4 1.9 copy.333
  178.3 1.9 copy.334
  180.1 2.4 multiply_reduce_fusion.6
  183.4 2.1 fusion.85
  185.5 2.2 convolution_subtract_fusion.3
  187.7 1.9 copy.277
  189.5 1.9 copy.278
  191.4 2.3 multiply_reduce_fusion.9
  195.5 1.6 fusion.88
  197.0 1.3 fusion.87
  198.3 1.3 convolution_add_fusion
  199.6 1.9 copy.327
  201.5 1.9 copy.328
  203.4 2.6 multiply_reduce_fusion.3
  206.0 1.7 copy.264
  207.8 2.1 fusion.84
  209.9 1.3 convolution_subtract_fusion
  211.1 1.9 copy.325
  213.1 1.9 copy.326
  215.0 2.6 multiply_reduce_fusion.2
  217.5 1.7 copy.263
  219.3 2.1 fusion.83
  222.7 1.2 copy.269
  223.9 1.4 multiply_reduce_fusion.5
  225.3 1.4 convolution_add_fusion.1
  229.5 2.2 multiply_reduce_fusion.4
  232.9 2.8 multiply_reduce_fusion
  237.0 1.4 convolution_bitcast_fusion.1
  238.4 1.4 convolution_bitcast_fusion.2
  239.8 1.1 convolution_bitcast_fusion.4
  242.8 1.1 convolution_bitcast_fusion.3
  247.1 1.4 fusion.5
  248.9 25.4 %concatenate.19 = f32[49,128,128]{2,0,1:T(8,128)} concatenate(f32[1,128,128]{2,0,1:T(1,128)S(1)} %bitcast.281, f32[3,128,128]{2,0,1:T(4,128)S(1)} %copy-done.61, f32[5,128,128]{2,0,1:T(8,128)} %convolution_bitcast_fusion.4, f32[7,128,128]{2,0,1:T(8,128)} %convolution_bitcast_fusion.3, f32[9,128,128]{2,0,1:T(8,128)S(1)} %copy-done.19, f32[11,128,128]{2,0,1:T(8,128)S(1)} %copy-done.18, ...), dimensions={0} | concatenate | bytes 6422528 | tf_op jit(solution)/shard_map/concatenate | solution.py:55
  274.3 4.3 fusion.82
  280.4 4.8 %collective-permute-done.2 = bf16[32,49,128]{2,0,1:T(8,128)(2,1)S(1)} collective-permute-done((bf16[32,49,128]{2,0,1:T(8,128)(2,1)S(1)}, bf16[32,49,128]{2,0,1:T(8,128)(2,1)S(1)}, u32[]{:S(2)}, u32[]{:S(2)}) %collective-permute-start.2) | collective-permute-done | bytes 401440 | tf_op jit(solution)/shard_map/ppermute | solution.py:14
  285.3 2.5 scatter_fusion
  287.9 6.7 %collective-permute-done.3 = bf16[32,49,128]{2,0,1:T(8,128)(2,1)} collective-permute-done((bf16[32,49,128]{2,0,1:T(8,128)(2,1)S(1)}, bf16[32,49,128]{2,0,1:T(8,128)(2,1)}, u32[]{:S(2)}, u32[]{:S(2)}) %collective-permute-start.3) | collective-permute-done | bytes 401440 | tf_op jit(solution)/shard_map/ppermute | solution.py:14
  294.6 1.1 copy.351
  295.7 2.5 scatter_fusion.1
  300.8 1.6 fusion.71
  302.4 64.2 %all-reduce.3.cloned.1.call-done = bf16[64,49,128]{2,0,1:T(8,128)(2,1)} async-done(((bf16[64,49,128]{2,0,1:T(8,128)(2,1)}), bf16[64,49,128]{2,0,1:T(8,128)(2,1)}) %all-reduce.3.cloned.1.call-update) | async-done | bytes 802832
  366.6 1.6 add_convert_fusion
  368.2 84.3 %reduce-scatter.3.cloned.1.call-done = bf16[8,49,128]{2,1,0:T(8,128)(2,1)} async-done(((bf16[64,49,128]{2,1,0:T(8,128)(2,1)}), bf16[8,49,128]{2,1,0:T(8,128)(2,1)}) %reduce-scatter.3.cloned.1.call-update) | async-done | bytes 100368 | tf_op jit(solution)/shard_map/reduce_scatter | solution.py:264
  (375 shorter events, 53.3 us)
Async XLA Ops:
  7.2 188.3 %copy-start = (bf16[768,768]{1,0:T(8,128)(2,1)S(1)}, bf16[768,768]{1,0:T(8,128)(2,1)}, u32[]{:S(2)}) copy-start(bf16[768,768]{1,0:T(8,128)(2,1)} %param.31) | copy-start | bytes 3538948
  7.2 50.4 %copy-start.100 = (s32[1,32]{1,0:T(1,128)S(1)}, s32[1,32]{1,0:T(1,128)}, u32[]{:S(2)}) copy-start(s32[1,32]{1,0:T(1,128)} %param.25) | copy-start | bytes 388
  7.2 359.4 %all-reduce.3.cloned.1.call-start = ((), (), s32[]{:S(2)}) async-start(), calls=%async_computation.2 | async-start | bytes 1605632
  57.6 7.6 %copy-start.91 = (s32[128]{0:T(128)S(1)}, s32[128]{0:T(128)}, u32[]{:S(2)}) copy-start(s32[128]{0:T(128)} %param.23) | copy-start | bytes 1540
  57.6 7.6 %copy-start.89 = (bf16[235,128]{1,0:T(8,128)(2,1)S(1)}, bf16[235,128]{1,0:T(8,128)(2,1)}, u32[]{:S(2)}) copy-start(bf16[235,128]{1,0:T(8,128)(2,1)} %param.27) | copy-start | bytes 180484
  57.6 7.7 %copy-start.96 = (f32[100,128]{1,0:T(8,128)S(1)}, f32[100,128]{1,0:T(8,128)}, u32[]{:S(2)}) copy-start(f32[100,128]{1,0:T(8,128)} %param.21) | copy-start | bytes 153604
  57.6 7.7 %copy-start.98 = (s32[8]{0:T(128)S(1)}, s32[8]{0:T(128)}, u32[]{:S(2)}) copy-start(s32[8]{0:T(128)} %param.20) | copy-start | bytes 100
  57.6 7.9 %copy-start.78 = (bf16[8,49,128]{2,0,1:T(8,128)(2,1)S(1)}, bf16[8,49,128]{2,0,1:T(8,128)(2,1)}, u32[]{:S(2)}) copy-start(bf16[8,49,128]{2,0,1:T(8,128)(2,1)} %param.35) | copy-start | bytes 301060
  59.2 75.7 %collective-permute-start = (bf16[32,49,128]{2,1,0:T(8,128)(2,1)}, bf16[32,49,128]{2,1,0:T(8,128)(2,1)}, u32[]{:S(2)}, u32[]{:S(2)}) collective-permute-start(bf16[32,49,128]{2,1,0:T(8,128)(2,1)} %broadcast_select_fusion.1), channel_id=1, source_target_pairs={{0,8},{8,16},{16,24},{24,32},{32,40},{40,48},{48,56},{56,64},{64,7... | collective-permute-start | bytes 1204232 | tf_op jit(solution)/shard_map/ppermute | solution.py:14
  60.7 74.1 %collective-permute-start.1 = (bf16[32,49,128]{2,1,0:T(8,128)(2,1)}, bf16[32,49,128]{2,1,0:T(8,128)(2,1)}, u32[]{:S(2)}, u32[]{:S(2)}) collective-permute-start(bf16[32,49,128]{2,1,0:T(8,128)(2,1)} %broadcast_select_fusion), channel_id=1, source_target_pairs={{0,248},{8,0},{16,8},{24,16},{32,24},{40,32},{48,40},{56,48},{64,5... | collective-permute-start | bytes 1204232 | tf_op jit(solution)/shard_map/ppermute | solution.py:14
  116.3 4.6 copy-start.93
  117.6 6.2 %slice-start = ((bf16[128,49,128]{2,0,1:T(8,128)(2,1)}), bf16[128,3,128]{2,0,1:T(8,128)(2,1)S(1)}, s32[]{:S(2)}) async-start(bf16[128,49,128]{2,0,1:T(8,128)(2,1)} %copy-done.5), calls=%async_computation.3 | async-start | bytes 196608 | tf_op jit(solution)/shard_map/slice | solution.py:43
  117.6 7.2 %slice-start.1 = ((bf16[128,49,128]{2,0,1:T(8,128)(2,1)}), bf16[128,5,128]{2,0,1:T(8,128)(2,1)S(1)}, s32[]{:S(2)}) async-start(bf16[128,49,128]{2,0,1:T(8,128)(2,1)} %copy-done.5), calls=%async_computation.4 | async-start | bytes 327680 | tf_op jit(solution)/shard_map/slice | solution.py:43
  117.8 8.0 %copy-start.25 = (bf16[5,7,128]{1,0,2:T(8,128)(2,1)}, bf16[5,7,128]{1,0,2:T(8,128)(2,1)S(1)}, u32[]{:S(2)}) copy-start(bf16[5,7,128]{1,0,2:T(8,128)(2,1)S(1)} %copy.248) | copy-start | bytes 26884
  119.0 6.9 %copy-start.27 = (bf16[5,5,128]{1,0,2:T(8,128)(2,1)}, bf16[5,5,128]{1,0,2:T(8,128)(2,1)S(1)}, u32[]{:S(2)}) copy-start(bf16[5,5,128]{1,0,2:T(8,128)(2,1)S(1)} %copy.245) | copy-start | bytes 19204
  120.1 4.0 copy-start.59
  121.0 4.9 %slice-start.2 = ((bf16[128,49,128]{2,0,1:T(8,128)(2,1)}), bf16[128,7,128]{2,0,1:T(8,128)(2,1)S(1)}, s32[]{:S(2)}) async-start(bf16[128,49,128]{2,0,1:T(8,128)(2,1)} %copy-done.5), calls=%async_computation.5 | async-start | bytes 458752 | tf_op jit(solution)/shard_map/slice | solution.py:43
  129.6 4.4 copy-start.94
  129.6 4.4 copy-start.90
  129.6 4.4 copy-start.97
  134.8 45.3 %copy-start.29 = (f32[128,128]{1,0:T(8,128)}, f32[128,128]{1,0:T(8,128)S(1)}, u32[]{:S(2)}) copy-start(f32[128,128]{1,0:T(8,128)S(1)} %get-tuple-element.165) | copy-start | bytes 196612
  140.2 3.0 copy-start.17
  140.2 3.0 copy-start.28
  140.2 3.4 copy-start.26
  146.3 4.1 copy-start.63
  146.3 4.6 %copy-start.56 = (f32[128,128,5]{1,0,2:T(8,128)S(1)}, f32[128,128,5]{1,0,2:T(8,128)}, u32[]{:S(2)}) copy-start(f32[128,128,5]{1,0,2:T(8,128)} %copy.444) | copy-start | bytes 983044
  146.4 5.3 %copy-start.55 = (f32[128,128,5]{1,0,2:T(8,128)S(1)}, f32[128,128,5]{1,0,2:T(8,128)}, u32[]{:S(2)}) copy-start(f32[128,128,5]{1,0,2:T(8,128)} %copy.443) | copy-start | bytes 983044
  146.4 5.9 %copy-start.54 = (f32[128,128,5]{1,0,2:T(8,128)S(1)}, f32[128,128,5]{1,0,2:T(8,128)}, u32[]{:S(2)}) copy-start(f32[128,128,5]{1,0,2:T(8,128)} %copy.442) | copy-start | bytes 983044
  147.8 5.2 %copy-start.53 = (f32[128,128,5]{1,0,2:T(8,128)S(1)}, f32[128,128,5]{1,0,2:T(8,128)}, u32[]{:S(2)}) copy-start(f32[128,128,5]{1,0,2:T(8,128)} %copy.441) | copy-start | bytes 983044
  148.5 5.1 %copy-start.52 = (f32[128,128,5]{1,0,2:T(8,128)S(1)}, f32[128,128,5]{1,0,2:T(8,128)}, u32[]{:S(2)}) copy-start(f32[128,128,5]{1,0,2:T(8,128)} %copy.440) | copy-start | bytes 983044
  151.0 4.4 copy-start.16
  151.0 4.4 copy-start.62
  154.3 5.0 %copy-start.42 = (f32[128,5,128]{2,0,1:T(8,128)}, f32[128,5,128]{2,0,1:T(8,128)S(1)}, u32[]{:S(2)}) copy-start(f32[128,5,128]{2,0,1:T(8,128)S(1)} %get-tuple-element.37) | copy-start | bytes 983044
  154.3 5.0 %copy-start.44 = (f32[128,5,128]{2,0,1:T(8,128)}, f32[128,5,128]{2,0,1:T(8,128)S(1)}, u32[]{:S(2)}) copy-start(f32[128,5,128]{2,0,1:T(8,128)S(1)} %get-tuple-element.38) | copy-start | bytes 983044
  155.3 6.9 %copy-start.3 = (bf16[640,640]{1,0:T(8,128)(2,1)S(1)}, bf16[640,640]{1,0:T(8,128)(2,1)}, u32[]{:S(2)}) copy-start(bf16[640,640]{1,0:T(8,128)(2,1)} %param.33) | copy-start | bytes 2457604
  159.3 5.4 %copy-start.4 = (bf16[640,640]{1,0:T(8,128)(2,1)S(1)}, bf16[640,640]{1,0:T(8,128)(2,1)}, u32[]{:S(2)}) copy-start(bf16[640,640]{1,0:T(8,128)(2,1)} %param.34) | copy-start | bytes 2457604
  160.4 5.4 %copy-start.50 = (bf16[128,5,128]{0,2,1:T(8,128)(2,1)}, bf16[128,5,128]{0,2,1:T(8,128)(2,1)S(1)}, u32[]{:S(2)}) copy-start(bf16[128,5,128]{0,2,1:T(8,128)(2,1)S(1)} %copy.332) | copy-start | bytes 491524
  173.1 7.0 %copy-start.48 = (bf16[128,5,128]{0,2,1:T(8,128)(2,1)}, bf16[128,5,128]{0,2,1:T(8,128)(2,1)S(1)}, u32[]{:S(2)}) copy-start(bf16[128,5,128]{0,2,1:T(8,128)(2,1)S(1)} %copy.274) | copy-start | bytes 491524
  183.4 8.0 %copy-start.45 = (f32[128,5,128]{2,0,1:T(8,128)S(1)}, f32[128,5,128]{2,0,1:T(8,128)}, u32[]{:S(2)}) copy-start(f32[128,5,128]{2,0,1:T(8,128)} %copy-done.44) | copy-start | bytes 983044
  185.5 8.2 %copy-start.34 = (f32[128,6,128]{2,0,1:T(8,128)S(1)}, f32[128,6,128]{2,0,1:T(8,128)}, u32[]{:S(2)}) copy-start(f32[128,6,128]{2,0,1:T(8,128)} %copy-done.33) | copy-start | bytes 1179652
  185.5 8.2 %copy-start.36 = (f32[128,6,128]{2,0,1:T(8,128)S(1)}, f32[128,6,128]{2,0,1:T(8,128)}, u32[]{:S(2)}) copy-start(f32[128,6,128]{2,0,1:T(8,128)} %copy-done.35) | copy-start | bytes 1179652
  195.4 2.9 copy-start.2
  221.8 3.5 copy-start.38
  228.6 3.2 copy-start.7
  228.6 3.1 copy-start.85
  228.8 3.0 copy-start.86
  228.8 3.0 copy-start.87
  229.5 3.4 copy-start.30
  229.5 3.4 copy-start.32
  231.9 4.6 copy-start.67
  232.9 3.6 copy-start.64
  232.9 3.6 copy-start.69
  232.9 3.6 copy-start.15
  237.0 2.8 copy-start.71
  237.0 2.8 copy-start.24
  248.5 204.0 %reduce-scatter.3.cloned.1.call-start = ((), (), s32[]{:S(2)}) async-start(), calls=%async_computation.1 | async-start | bytes 1032192 | tf_op jit(solution)/shard_map/reduce_scatter | solution.py:264
  248.9 25.4 %copy-start.95 = (s32[128]{0:T(128)S(1)}, s32[128]{0:T(128)}, u32[]{:S(2)}) copy-start(s32[128]{0:T(128)} %param.22) | copy-start | bytes 1540
  274.3 5.0 %copy-start.99 = (s32[1,32]{1,0:T(1,128)S(1)}, s32[1,32]{1,0:T(1,128)}, u32[]{:S(2)}) copy-start(s32[1,32]{1,0:T(1,128)} %param.26) | copy-start | bytes 388
  274.3 5.0 %copy-start.101 = (s32[1,32]{1,0:T(1,128)S(1)}, s32[1,32]{1,0:T(1,128)}, u32[]{:S(2)}) copy-start(s32[1,32]{1,0:T(1,128)} %param.25) | copy-start | bytes 388
  278.7 6.5 %collective-permute-start.2 = (bf16[32,49,128]{2,0,1:T(8,128)(2,1)S(1)}, bf16[32,49,128]{2,0,1:T(8,128)(2,1)S(1)}, u32[]{:S(2)}, u32[]{:S(2)}) collective-permute-start(bf16[32,49,128]{2,0,1:T(8,128)(2,1)S(1)} %get-tuple-element.16), channel_id=1, source_target_pairs={{0,248},{8,0},{16,8},{24,16},{32,24},{40,32},{48,40},{56,48},{64,5... | collective-permute-start | bytes 1204232 | tf_op jit(solution)/shard_map/ppermute | solution.py:14
  278.8 15.8 %collective-permute-start.3 = (bf16[32,49,128]{2,0,1:T(8,128)(2,1)S(1)}, bf16[32,49,128]{2,0,1:T(8,128)(2,1)}, u32[]{:S(2)}, u32[]{:S(2)}) collective-permute-start(bf16[32,49,128]{2,0,1:T(8,128)(2,1)S(1)} %get-tuple-element.15), channel_id=1, source_target_pairs={{0,8},{8,16},{16,24},{24,32},{32,40},{40,48},{48,56},{56,64},{64,7... | collective-permute-start | bytes 1204232 | tf_op jit(solution)/shard_map/ppermute | solution.py:14
  298.3 68.3 %copy-start.77 = (bf16[8,49,128]{2,0,1:T(8,128)(2,1)S(1)}, bf16[8,49,128]{2,0,1:T(8,128)(2,1)}, u32[]{:S(2)}) copy-start(bf16[8,49,128]{2,0,1:T(8,128)(2,1)} %param.19) | copy-start | bytes 301060
  298.4 154.1 %copy-start.79 = (bf16[8,49,128]{2,0,1:T(8,128)(2,1)S(1)}, bf16[8,49,128]{2,0,1:T(8,128)(2,1)}, u32[]{:S(2)}) copy-start(bf16[8,49,128]{2,0,1:T(8,128)(2,1)} %param.35) | copy-start | bytes 301060
  298.4 155.8 %copy-start.1 = (bf16[768,768]{1,0:T(8,128)(2,1)S(1)}, bf16[768,768]{1,0:T(8,128)(2,1)}, u32[]{:S(2)}) copy-start(bf16[768,768]{1,0:T(8,128)(2,1)} %param.31) | copy-start | bytes 3538948
  (55 other events, 97.8 us)
Sparse Core Ops, SparseCore 0:
  248.6 117.9 all-reduce.2
  371.1 81.3 reduce-scatter.2
where the time goes:
time: 463 us; the launch traced here: 461 us
  waiting for transfers between devices  160 us (35%)
  local copies, waits for them, and re-layouts  99.1 us (21%)
  blocking collectives  94.1 us (20%)
  matrix products  48.4 us (10%)
  other arithmetic  37.3 us (8%)
  between operations  16.9 us (4%)
  starting transfers between devices  5.1 us (1%)
    reduce_scatter x1, waiting for transfers between devices, on_device(): lax.psum_scatter(own_rows.astype(jnp.bfloat16), 'edge', scatter_dimension...  84.3 us
    unnamed x3, waiting for transfers between devices  64.2 us
    all_gather x1, blocking collectives, on_device(): whole_block = lax.all_gather(embeddings, 'edge', axis=0, tiled=True)  48.3 us
    all_gather x1, blocking collectives, on_device(): grad_block = lax.all_gather(grad_aggregate, 'edge', axis=0, tiled=True)  45.7 us
    concatenate x2, local copies, waits for them, and re-layouts, rotate_back_major(): return jnp.concatenate(outcome, axis=0)  25.6 us
    unnamed x232, local copies, waits for them, and re-layouts  17.1 us
    dot_general x10, matrix products, product_transposed(): lax.dot_general(left_side, right_side, (((1,), (1,)), ((), ())), preferre...  15.5 us
    dot_general x10, matrix products, product(): return jnp.dot(left_side, right_side, preferred_element_type=jnp.float32)  15 us
  transfers between devices with their start and end apart: 6, of which 4 were waited for; matrix products, arithmetic and copies ran while one was open for 14% of the time, Pallas kernels for 0%

commit v1 on v0

v1 whole, which is shorter than its diff:
```python
import numpy as np

import jax
import jax.numpy as jnp
from jax import lax
from jax.experimental import pallas as pl
from jax.experimental.pallas import tpu as pltpu
from jax.sharding import PartitionSpec as P

F32 = jnp.float32
BF16 = jnp.bfloat16
LANES = 128
GROUP = 16
TOP = 6
COEFS = (TOP + 1) ** 2
ORDERS = 29
WIDE = COEFS * LANES
VMEM = 50 * 2**20

TILES = ((0, 1, 2, 3), (4,), (5,), (6,))


def place_of(degree, order):
    if order == 0:
        return degree
    start = {1: 7, -1: 13, 2: 19, -2: 24}[order]
    return start + degree - abs(order)


def tile_table():
    table = []
    row_start = 0
    for degrees in TILES:
        first = degrees[0] ** 2
        coefs = (degrees[-1] + 1) ** 2 - first
        pairs = [(d, m) for d in degrees for m in range(-min(d, 2), min(d, 2) + 1)]
        table.append((first, coefs, pairs, row_start))
        row_start += GROUP * len(pairs)
    return table, row_start


TABLE, TURN_ROWS = tile_table()
BACK_ROWS = GROUP * COEFS
ROT_ROWS = 235
ROT_PAD = 256


def selectors():
    pick_turn = np.zeros((TURN_ROWS, ROT_PAD), np.float32)
    pick_back = np.zeros((BACK_ROWS, ROT_PAD), np.float32)
    mask_turn = np.zeros((ROT_PAD, 256), np.float32)
    mask_back = np.zeros((ROT_PAD, 256), np.float32)
    offset = 0
    for degree in range(TOP + 1):
        cap = min(degree, 2)
        [(first, _, pairs, start)] = [
            e for e, d in zip(TABLE, TILES) if degree in d
        ]
        for order in range(-cap, cap + 1):
            row_block = pairs.index((degree, order))
            for column in range(2 * degree + 1):
                row = offset + (order + cap) * (2 * degree + 1) + column
                coef = degree * degree + column
                pick_turn[start + GROUP * row_block : start + GROUP * (row_block + 1), row] = 1
                pick_back[GROUP * coef : GROUP * (coef + 1), row] = 1
                mask_turn[row, GROUP * (coef - first) : GROUP * (coef - first + 1)] = 1
                mask_back[row, GROUP * row_block : GROUP * (row_block + 1)] = 1
        offset += (2 * cap + 1) * (2 * degree + 1)
    return pick_turn, pick_back, mask_turn, mask_back


def dot(a, b):
    return jnp.dot(a, b, preferred_element_type=F32)


def dot_nt(a, b):
    return lax.dot_general(a, b, (((1,), (1,)), ((), ())), preferred_element_type=F32)


def chunks(total, size):
    return [(s, min(size, total - s)) for s in range(0, total, size)]


def prep_kernel(rot, pick_turn, pick_back, mask_turn, mask_back, turn, back):
    row = lax.broadcasted_iota(jnp.int32, (LANES, 256), 0)
    lane = lax.broadcasted_iota(jnp.int32, (LANES, 256), 1) & (GROUP - 1)

    def keep(rows):
        r = lax.broadcasted_iota(jnp.int32, (rows, 256), 0) & (GROUP - 1)
        c = lax.broadcasted_iota(jnp.int32, (rows, 256), 1) & (GROUP - 1)
        return r == c

    keep_turn, keep_back = keep(TURN_ROWS), keep(BACK_ROWS)
    for g in range(LANES // GROUP):
        spread = (row == lane + GROUP * g).astype(F32).astype(BF16)
        laid = dot(rot[...], spread)
        for mask, pick, kept, out in (
            (mask_turn, pick_turn, keep_turn, turn),
            (mask_back, pick_back, keep_back, back),
        ):
            full = dot(pick[...], (laid * mask[...]).astype(BF16))
            out[g] = jnp.where(kept, full, 0.0).astype(BF16)


def rotate(turn, wide, use):
    for g in range(LANES // GROUP):
        rows = pl.ds(GROUP * g, GROUP)
        for first, coefs, pairs, start in TABLE:
            window = jnp.concatenate(
                [wide[rows, pl.ds((first + c) * LANES, LANES)] for c in range(coefs)], axis=0
            )
            block = turn[g, pl.ds(start, GROUP * len(pairs)), pl.ds(0, GROUP * coefs)]
            result = dot(block, window)
            for k, (degree, order) in enumerate(pairs):
                use(g, degree, order, result[GROUP * k : GROUP * (k + 1)])


def rotate_back(back, fragments, wide):
    for g in range(LANES // GROUP):
        rows = pl.ds(GROUP * g, GROUP)
        for first, coefs, pairs, _ in TABLE:
            window = jnp.concatenate(
                [fragments[rows, pl.ds(place_of(*p) * LANES, LANES)] for p in pairs], axis=0
            )
            block = back[g, pl.ds(GROUP * first, GROUP * coefs), pl.ds(0, GROUP * len(pairs))]
            result = dot(block, window)
            for c in range(coefs):
                wide[rows, pl.ds((first + c) * LANES, LANES)] = result[
                    GROUP * c : GROUP * (c + 1)
                ].astype(BF16)


def pick_rows(ids, pieces, wide):
    total = sum(p.shape[0] for p in pieces)
    hot = (ids[...] == lax.broadcasted_iota(jnp.int32, (LANES, total), 1)).astype(F32).astype(BF16)
    for start, size in chunks(WIDE, 256):
        lanes = pl.ds(start, size)
        table = jnp.concatenate([p[:, lanes] for p in pieces], axis=0)
        wide[:, lanes] = dot(hot, table).astype(BF16)


def add_rows(ids, wide, pieces):
    total = sum(p.shape[0] for p in pieces)
    hot = (ids[...] == lax.broadcasted_iota(jnp.int32, (total, LANES), 0)).astype(F32).astype(BF16)
    for start, size in chunks(WIDE, 256):
        lanes = pl.ds(start, size)
        summed = dot(hot, wide[:, lanes]).astype(BF16)
        offset = 0
        for p in pieces:
            p[:, lanes] = summed[offset : offset + p.shape[0]]
            offset += p.shape[0]


def put_order(zero, one, two, g, degree, order, value):
    where, lead = {0: (zero, 0), 1: (one, 1), 2: (two, 2)}[abs(order)]
    base = LANES if order < 0 else 0
    where[pl.ds(base + GROUP * g, GROUP), pl.ds((degree - lead) * LANES, LANES)] = value


def forward_kernel(
    own, partner, far0, far1, far2, far3, src, tgt, turn, back, basis, w_rad, w0, w1r, w1i, w2r, w2i,
    agg0, agg1, agg2, agg3, turned, outs, pre,
    wide, zero, one, two, gated, rad,
):
    value = dot(basis[...], w_rad[...])
    pre[...] = value
    rad[...] = value * jax.nn.sigmoid(value)
    pick_rows(src, (own, partner, far0, far1, far2, far3), wide)

    def use(g, degree, order, part):
        rows = pl.ds(GROUP * g, GROUP)
        turned[rows, pl.ds(place_of(degree, order) * LANES, LANES)] = part
        put_order(zero, one, two, g, degree, order, (part * rad[rows, :]).astype(BF16))

    rotate(turn, wide, use)
    for start, size in chunks(7 * LANES, 256):
        outs[:, pl.ds(start, size)] = dot(zero[...], w0[:, pl.ds(start, size)])
    for stacked, real, imag, up, down, count in (
        (one, w1r, w1i, 7, 13, 6),
        (two, w2r, w2i, 19, 24, 5),
    ):
        for start, size in chunks(count * LANES, 256):
            a = dot(stacked[...], real[:, pl.ds(start, size)])
            b = dot(stacked[...], imag[:, pl.ds(start, size)])
            outs[:, pl.ds(up * LANES + start, size)] = a[:LANES] - b[LANES:]
            outs[:, pl.ds(down * LANES + start, size)] = a[LANES:] + b[:LANES]
    gate = jax.nn.sigmoid(outs[:, pl.ds(0, LANES)])
    for q in range(ORDERS):
        lanes = pl.ds(q * LANES, LANES)
        gated[:, lanes] = (outs[:, lanes] * gate).astype(BF16)
    rotate_back(back, gated, wide)
    add_rows(tgt, wide, (agg0, agg1, agg2, agg3))


def backward_kernel(
    up0, up1, up2, up3, tgt, src, turn, back, turned, outs, pre, w_rad, w0, w1r, w1i, w2r, w2i,
    own, partner, far0, far1, far2, far3, grad_basis,
    wide, zero, one, two, grads, rad,
):
    pick_rows(tgt, (up0, up1, up2, up3), wide)

    def use(g, degree, order, part):
        grads[pl.ds(GROUP * g, GROUP), pl.ds(place_of(degree, order) * LANES, LANES)] = part

    rotate(turn, wide, use)
    scalar = outs[:, pl.ds(0, LANES)]
    gate = jax.nn.sigmoid(scalar)
    slope = gate * (1.0 - gate)
    lead = grads[:, pl.ds(0, LANES)]
    weighted = lead * scalar
    for q in range(1, ORDERS):
        lanes = pl.ds(q * LANES, LANES)
        weighted = weighted + grads[:, lanes] * outs[:, lanes]
    zero[:, pl.ds(0, LANES)] = (
        lead * (gate + scalar * slope) + slope * (weighted - lead * scalar)
    ).astype(BF16)
    for stacked, count, base, q0 in ((zero, 6, 0, 1), (one, 6, 0, 7), (one, 6, LANES, 13), (two, 5, 0, 19), (two, 5, LANES, 24)):
        for k in range(count):
            value = (grads[:, pl.ds((q0 + k) * LANES, LANES)] * gate).astype(BF16)
            column = k + 1 if stacked is zero else k
            stacked[pl.ds(base, LANES), pl.ds(column * LANES, LANES)] = value
    value = pre[...]
    gate = jax.nn.sigmoid(value)
    rad[...] = value * gate
    slope = gate * (1.0 + value * (1.0 - gate))
    total = jnp.zeros((LANES, LANES), F32)

    def take(total, q, scaled):
        lanes = pl.ds(q * LANES, LANES)
        wide[:, lanes] = (scaled * rad[...]).astype(BF16)
        return total + scaled * turned[:, lanes]

    for start, size in chunks(7 * LANES, 256):
        a = dot_nt(zero[...], w0[pl.ds(start, size), :])
        for k in range(size // LANES):
            total = take(total, start // LANES + k, a[:, k * LANES : (k + 1) * LANES])
    for stacked, real, imag, up, down, count in (
        (one, w1r, w1i, 7, 13, 6),
        (two, w2r, w2i, 19, 24, 5),
    ):
        for start, size in chunks(count * LANES, 256):
            a = dot_nt(stacked[...], real[pl.ds(start, size), :])
            b = dot_nt(stacked[...], imag[pl.ds(start, size), :])
            for k in range(size // LANES):
                cut = slice(k * LANES, (k + 1) * LANES)
                total = take(total, up + start // LANES + k, a[:LANES, cut] + b[LANES:, cut])
                total = take(total, down + start // LANES + k, a[LANES:, cut] - b[:LANES, cut])
    grad_basis[...] = dot_nt((total * slope).astype(BF16), w_rad[...])
    for q in range(ORDERS):
        lanes = pl.ds(q * LANES, LANES)
        zero_q = wide[:, lanes]
        grads[:, lanes] = zero_q.astype(F32)
    rotate_back_f32(back, grads, wide)
    add_rows(src, wide, (own, partner, far0, far1, far2, far3))


def rotate_back_f32(back, fragments, wide):
    for g in range(LANES // GROUP):
        rows = pl.ds(GROUP * g, GROUP)
        for first, coefs, pairs, _ in TABLE:
            window = jnp.concatenate(
                [fragments[rows, pl.ds(place_of(*p) * LANES, LANES)] for p in pairs], axis=0
            ).astype(BF16)
            block = back[g, pl.ds(GROUP * first, GROUP * coefs), pl.ds(0, GROUP * len(pairs))]
            result = dot(block, window)
            for c in range(coefs):
                wide[rows, pl.ds((first + c) * LANES, LANES)] = result[
                    GROUP * c : GROUP * (c + 1)
                ].astype(BF16)


def kernel_call(kernel, outs, scratch, flops, moved):
    return pl.pallas_call(
        kernel,
        out_shape=outs,
        scratch_shapes=scratch,
        compiler_params=pltpu.CompilerParams(vmem_limit_bytes=VMEM),
        cost_estimate=pl.CostEstimate(flops=flops, bytes_accessed=moved, transcendentals=0),
    )


def shaped(*dims, kind=BF16):
    return jax.ShapeDtypeStruct(dims, kind)


def on_device(
    embeddings, species, species_gain, sources, targets, counts, send_left, send_right, rotations,
    radial_basis, weight_radial, weight_zero, weight_one_real, weight_one_imag, weight_two_real,
    weight_two_imag, cotangent,
):
    weights = (weight_zero, weight_one_real, weight_one_imag, weight_two_real, weight_two_imag)
    atoms = embeddings.shape[0]
    edges = sources.shape[0]
    blocks = lax.axis_size("space")
    member = lax.axis_index("edge")
    block = lax.axis_index("space")
    half, along = member // 4, member % 4
    odd = block % 2
    scale = (atoms / edges) ** 0.5

    def across(v):
        return lax.ppermute(v, "edge", [(s, (s + 4) % 8) for s in range(8)])

    def shift(v, k):
        return lax.ppermute(v, "edge", [(s, s // 4 * 4 + (s + k) % 4) for s in range(8)])

    def swap_near(v):
        return lax.ppermute(v, "space", [(b, b ^ 1) for b in range(blocks)])

    def swap_far(v):
        return lax.ppermute(v, "space", [(b, (b + 2 * (b % 2) - 1) % blocks) for b in range(blocks)])

    def roll(v, k):
        return lax.ppermute(v, "space", [(b, (b + k) % blocks) for b in range(blocks)])

    def spread(v):
        return [v] + [shift(v, 4 - d) for d in (1, 2, 3)]

    def collect(parts):
        total = parts[0].astype(F32)
        for d in (1, 2, 3):
            total = total + shift(parts[d], d).astype(F32)
        return total

    gain = jnp.dot(
        (species[:, None] == lax.iota(jnp.int32, species_gain.shape[0])[None, :]).astype(F32),
        species_gain,
        precision=lax.Precision.HIGHEST,
    )
    flat = embeddings.reshape(atoms, WIDE)
    upstream = (cotangent.astype(F32) * gain[:, None, :] * scale).astype(BF16).reshape(atoms, WIDE)

    pair = jnp.concatenate([flat, across(flat)], axis=0)
    far_pair = swap_far(pair)
    own_pieces = spread(pair)
    own_table = jnp.concatenate(own_pieces, axis=0)
    partner_table = swap_near(own_table)
    far_pieces = spread(far_pair)
    up_pair = jnp.concatenate([upstream, across(upstream)], axis=0)
    up_pieces = spread(up_pair)

    def slot(atom):
        owner, row = atom // atoms, atom % atoms
        return (owner % 4 - along) % 4 * (2 * atoms) + (owner // 4 - half) % 2 * atoms + row

    lists = jnp.concatenate([roll(send_right, 1), roll(send_left, -1)], axis=1)[0]
    halo = send_left.shape[1]
    block_atoms = 8 * atoms
    halo_hot = (sources[:, None] - block_atoms) == lax.iota(jnp.int32, 2 * halo)[None, :]
    halo_atom = jnp.sum(jnp.where(halo_hot, lists[None, :], 0), axis=1)
    on_left = sources < block_atoms + halo
    near = jnp.where(on_left, odd == 1, odd == 0)
    src = jnp.where(
        sources < block_atoms,
        slot(sources),
        jnp.where(near, block_atoms, 2 * block_atoms) + slot(halo_atom),
    ).astype(jnp.int32)
    live = member * edges + lax.iota(jnp.int32, edges) < counts[0]
    tgt = jnp.where(live, slot(targets), -1).astype(jnp.int32)
    src_col, src_row = src[:, None], src[None, :]
    tgt_col, tgt_row = tgt[:, None], tgt[None, :]

    pick_turn, pick_back, mask_turn, mask_back = selectors()
    groups = LANES // GROUP
    turn, back = kernel_call(
        prep_kernel,
        (shaped(groups, TURN_ROWS, 256), shaped(groups, BACK_ROWS, 256)),
        [],
        2 * 10**9,
        6 * 10**6,
    )(
        jnp.pad(rotations, ((0, ROT_PAD - ROT_ROWS), (0, 0))),
        jnp.asarray(pick_turn, BF16),
        jnp.asarray(pick_back, BF16),
        jnp.asarray(mask_turn, F32),
        jnp.asarray(mask_back, F32),
    )

    def work():
        return [
            pltpu.VMEM((edges, WIDE), BF16),
            pltpu.VMEM((edges, 7 * LANES), BF16),
            pltpu.VMEM((2 * edges, 6 * LANES), BF16),
            pltpu.VMEM((2 * edges, 5 * LANES), BF16),
        ]

    piece = shaped(2 * atoms, WIDE)
    whole = shaped(block_atoms, WIDE)
    kept = shaped(edges, ORDERS * LANES, kind=F32)
    square = shaped(edges, LANES, kind=F32)
    *aggs, turned, outs, pre = kernel_call(
        forward_kernel,
        (piece, piece, piece, piece, kept, kept, square),
        work() + [pltpu.VMEM((edges, ORDERS * LANES), BF16), pltpu.VMEM((edges, LANES), F32)],
        4 * 10**9,
        20 * 10**6,
    )(own_table, partner_table, *far_pieces, src_col, tgt_row, turn, back, radial_basis, weight_radial, *weights)

    agg_pair = collect(aggs)
    aggregate = agg_pair[:atoms] + across(agg_pair[atoms:].astype(BF16)).astype(F32)
    updated = (
        embeddings.astype(F32) + gain[:, None, :] * scale * aggregate.reshape(embeddings.shape)
    ).astype(BF16)

    own_grad, near_grad, *far_grads, grad_basis = kernel_call(
        backward_kernel,
        (whole, whole, piece, piece, piece, piece, square),
        work() + [pltpu.VMEM((edges, ORDERS * LANES), F32), pltpu.VMEM((edges, LANES), F32)],
        5 * 10**9,
        20 * 10**6,
    )(*up_pieces, tgt_col, src_row, turn, back, turned, outs, pre, weight_radial, *weights)

    far_home = swap_far(collect(far_grads).astype(BF16)).astype(F32)
    summed = own_grad.astype(F32) + swap_near(near_grad).astype(F32)
    parts = [summed[2 * atoms * d : 2 * atoms * (d + 1)].astype(BF16) for d in range(4)]
    grad_pair = collect(parts) + far_home
    grad_rows = grad_pair[:atoms] + across(grad_pair[atoms:].astype(BF16)).astype(F32)
    grad_embeddings = cotangent.astype(F32) + grad_rows.reshape(cotangent.shape)
    return (updated, grad_embeddings, grad_basis)


def solution(mesh):
    both = ("space", "edge")
    placed = (
        P(both, None, None), P(both), P(), P(both), P(both), P("space"), P("space", None),
        P("space", None), P(None, both), P(both, None), P(), P(), P(), P(), P(), P(),
        P(both, None, None),
    )
    return jax.shard_map(
        on_device,
        mesh=mesh,
        in_specs=placed,
        out_specs=(P(both, None, None), P(both, None, None), P(both, None)),
        check_vma=False,
    )
```

time: 463 us -> 116 us (0.25)
  the two profiles are of different devices: /device:TPU:8 before, /device:TPU:1 now
where the time goes in v1:
time: 116 us
  starting transfers between devices  66.2 us (57%)
  Pallas kernels  22.5 us (19%)
  waiting for transfers between devices  12.3 us (11%)
  local copies, waits for them, and re-layouts  7.25 us (6%)
  other arithmetic  5.13 us (4%)
  between operations  1.45 us (1%)
    ppermute x4, starting transfers between devices, across(): return lax.ppermute(v, 'edge', [(s, (s + 4) % 8) for s in range(8)])  24.4 us
    ppermute x18, starting transfers between devices, shift(): lax.ppermute(v, 'edge', [(s, s // 4 * 4 + (s + k) % 4) for s in range(8)])  22.6 us
    ppermute x2, starting transfers between devices, swap_near(): return lax.ppermute(v, 'space', [(b, b ^ 1) for b in range(blocks)])  14.3 us
    ppermute x18, waiting for transfers between devices, shift(): lax.ppermute(v, 'edge', [(s, s // 4 * 4 + (s + k) % 4) for s in range(8)])  10.4 us
    pallas_call x1, Pallas kernels, on_device(): kernel_call(backward_kernel, (whole, whole, piece, piece, piece, piece, s...  9.86 us
    pallas_call x1, Pallas kernels, on_device(): kernel_call(forward_kernel, (piece, piece, piece, piece, kept, kept, squa...  8.16 us
    unnamed x26, local copies, waits for them, and re-layouts  6.1 us
    pallas_call x1, Pallas kernels, on_device(): kernel_call(prep_kernel, (shaped(groups, TURN_ROWS, 256), shaped(groups,...  4.48 us
  transfers between devices with their start and end apart: 28, of which 9 were waited for; matrix products, arithmetic and copies ran while one was open for 6% of the time, Pallas kernels for 11%

profile of v1, /device:TPU:1, one launch (start us, length us, event | category | flops | bytes accessed | tf_op | source)
XLA Modules:
  0.0 115.7 jit_solution(9708069541743280186)
XLA Ops:
  0.6 0.0 copy-start
  0.6 7.8 %collective-permute-start = (bf16[8,6272]{1,0:T(8,128)(2,1)}, bf16[8,6272]{1,0:T(8,128)(2,1)S(1)}, u32[]{:S(2)}, u32[]{:S(2)}) collective-permute-start(bf16[8,6272]{1,0:T(8,128)(2,1)} %bitcast.30), channel_id=1, source_target_pairs={{0,4},{1,5},{2,6},{3,7},{4,0},{5,1},{6,2},{7,3},{8,12},{9,13},{10,... | collective-permute-start | bytes 301064 | tf_op jit(solution)/shard_map/ppermute | solution.py:302
  8.5 1.0 collective-permute-start.10
  9.4 0.8 collective-permute-start.9
  10.2 0.8 broadcast_multiply_fusion
  11.1 0.9 fusion.7
  12.0 0.2 collective-permute-start.15
  12.2 0.9 constant_dynamic-update-slice_fusion.4
  13.1 0.7 broadcast_add_fusion
  14.4 0.7 fusion.35.tgt
  15.1 0.7 fusion.34
  15.8 0.8 pad.4.rot
  16.6 1.0 copy-done.3
  17.6 0.9 copy-done.4
  18.6 0.9 copy-done.5
  19.5 0.9 copy-done.6
  20.5 4.5 %shard_map.220 = (bf16[8,464,256]{2,1,0:T(8,128)(2,1)S(1)}, bf16[8,784,256]{2,1,0:T(8,128)(2,1)}) custom-call(bf16[256,128]{1,0:T(8,128)(2,1)S(1)} %pad.4.rot, bf16[464,256]{1,0:T(8,128)(2,1)S(1)} %copy-done.6, bf16[784,256]{1,0:T(8,128)(2,1)S(1)} %copy-done.3, f32[256,256]{1,0:T(8,128)S(1)} %copy-done.4, f32[256,256]{1,0:T(8,128)S(1)} %copy-done.5), custom_call_target="tpu_custom_call" | custom-call | flops 2000000000 | bytes 6000000 | tf_op jit(solution)/shard_map/pallas_call | solution.py:365
  24.9 1.3 %copy-done.7 = bf16[8,464,256]{2,1,0:T(8,128)(2,1)} copy-done((bf16[8,464,256]{2,1,0:T(8,128)(2,1)}, bf16[8,464,256]{2,1,0:T(8,128)(2,1)S(1)}, u32[]{:S(2)}) %copy-start.7) | copy-done | bytes 1900568
  26.2 0.1 copy.27.tgt
  26.4 0.1 add_bitcast_fusion
  26.4 0.1 select_reduce_fusion
  26.6 2.5 %collective-permute-start.1 = (bf16[16,6272]{1,0:T(8,128)(2,1)S(1)}, bf16[16,6272]{1,0:T(8,128)(2,1)S(1)}, u32[]{:S(2)}, u32[]{:S(2)}) collective-permute-start(bf16[16,6272]{1,0:T(8,128)(2,1)S(1)} %pad_maximum_fusion), channel_id=1, source_target_pairs={{0,3},{1,0},{2,1},{3,2},{4,7},{5,4},{6,5},{7,6},{8,11},{9,8},{10,9... | collective-permute-start | bytes 602120 | tf_op jit(solution)/shard_map/ppermute | solution.py:305
  29.1 0.5 collective-permute-start.2
  29.6 0.6 collective-permute-start.3
  30.2 1.3 %collective-permute-start.5 = (bf16[16,6272]{1,0:T(8,128)(2,1)S(1)}, bf16[16,6272]{1,0:T(8,128)(2,1)S(1)}, u32[]{:S(2)}, u32[]{:S(2)}) collective-permute-start(bf16[16,6272]{1,0:T(8,128)(2,1)S(1)} %pad_maximum_fusion), channel_id=1, source_target_pairs={{0,248},{8,16},{16,8},{24,32},{32,24},{40,48},{48,40},{56,64},{64,... | collective-permute-start | bytes 602120 | tf_op jit(solution)/shard_map/ppermute | solution.py:311
  31.5 2.4 %collective-permute-done.1 = bf16[16,6272]{1,0:T(8,128)(2,1)S(1)} collective-permute-done((bf16[16,6272]{1,0:T(8,128)(2,1)S(1)}, bf16[16,6272]{1,0:T(8,128)(2,1)S(1)}, u32[]{:S(2)}, u32[]{:S(2)}) %collective-permute-start.1) | collective-permute-done | bytes 200736 | tf_op jit(solution)/shard_map/ppermute | solution.py:305
  33.9 1.3 %collective-permute-done.2 = bf16[16,6272]{1,0:T(8,128)(2,1)S(1)} collective-permute-done((bf16[16,6272]{1,0:T(8,128)(2,1)S(1)}, bf16[16,6272]{1,0:T(8,128)(2,1)S(1)}, u32[]{:S(2)}, u32[]{:S(2)}) %collective-permute-start.2) | collective-permute-done | bytes 200736 | tf_op jit(solution)/shard_map/ppermute | solution.py:305
  35.3 2.0 %collective-permute-done.3 = bf16[16,6272]{1,0:T(8,128)(2,1)S(1)} collective-permute-done((bf16[16,6272]{1,0:T(8,128)(2,1)S(1)}, bf16[16,6272]{1,0:T(8,128)(2,1)S(1)}, u32[]{:S(2)}, u32[]{:S(2)}) %collective-permute-start.3) | collective-permute-done | bytes 200736 | tf_op jit(solution)/shard_map/ppermute | solution.py:305
  37.4 5.6 %collective-permute-start.4 = (bf16[64,6272]{1,0:T(8,128)(2,1)S(1)}, bf16[64,6272]{1,0:T(8,128)(2,1)S(1)}, u32[]{:S(2)}, u32[]{:S(2)}) collective-permute-start(bf16[64,6272]{1,0:T(8,128)(2,1)S(1)} %constant_dynamic-update-slice_fusion.own), channel_id=1, source_target_pairs={{0,8},{8,0},{16,24},{24,16},{32,40},{40,32},{48,56},{56,48},{64,72... | collective-permute-start | bytes 2408456 | tf_op jit(solution)/shard_map/ppermute | solution.py:308
  43.0 0.1 copy.26.src
  43.1 0.4 collective-permute-start.6
  43.5 0.5 collective-permute-start.7
  44.0 0.7 collective-permute-start.8
  44.7 2.5 %collective-permute-start.16 = (bf16[16,6272]{1,0:T(8,128)(2,1)S(1)}, bf16[16,6272]{1,0:T(8,128)(2,1)S(1)}, u32[]{:S(2)}, u32[]{:S(2)}) collective-permute-start(bf16[16,6272]{1,0:T(8,128)(2,1)S(1)} %pad_maximum_fusion.1.up0), channel_id=1, source_target_pairs={{0,3},{1,0},{2,1},{3,2},{4,7},{5,4},{6,5},{7,6},{8,11},{9,8},{10,9... | collective-permute-start | bytes 602120 | tf_op jit(solution)/shard_map/ppermute | solution.py:305
  47.2 1.5 %collective-permute-done.6.far1 = bf16[16,6272]{1,0:T(8,128)(2,1)S(1)} collective-permute-done((bf16[16,6272]{1,0:T(8,128)(2,1)S(1)}, bf16[16,6272]{1,0:T(8,128)(2,1)S(1)}, u32[]{:S(2)}, u32[]{:S(2)}) %collective-permute-start.6) | collective-permute-done | bytes 200736 | tf_op jit(solution)/shard_map/ppermute | solution.py:305
  48.6 0.0 collective-permute-start.17
  48.6 1.0 collective-permute-done.7.far2
  49.7 3.4 %collective-permute-start.18 = (bf16[16,6272]{1,0:T(8,128)(2,1)S(1)}, bf16[16,6272]{1,0:T(8,128)(2,1)S(1)}, u32[]{:S(2)}, u32[]{:S(2)}) collective-permute-start(bf16[16,6272]{1,0:T(8,128)(2,1)S(1)} %pad_maximum_fusion.1.up0), channel_id=1, source_target_pairs={{0,1},{1,2},{2,3},{3,0},{4,5},{5,6},{6,7},{7,4},{8,9},{9,10},{10,1... | collective-permute-start | bytes 602120 | tf_op jit(solution)/shard_map/ppermute | solution.py:305
  53.1 8.2 %shard_map.221 = (bf16[16,6272]{1,0:T(8,128)(2,1)S(1)}, bf16[16,6272]{1,0:T(8,128)(2,1)S(1)}, bf16[16,6272]{1,0:T(8,128)(2,1)S(1)}, bf16[16,6272]{1,0:T(8,128)(2...) custom-call(bf16[64,6272]{1,0:T(8,128)(2,1)S(1)} %constant_dynamic-update-slice_fusion.own, ...), custom_call_target="tpu_custom_call" | custom-call | flops 4000000000 | bytes 20000000 | tf_op jit(solution)/shard_map/pallas_call | solution.py:391
  61.3 9.9 %shard_map.222 = (bf16[64,6272]{1,0:T(8,128)(2,1)S(1)}, bf16[64,6272]{1,0:T(8,128)(2,1)S(1)}, bf16[16,6272]{1,0:T(8,128)(2,1)S(1)}, bf16[16,6272]{1,0:T(8,128)(2...) custom-call(bf16[16,6272]{1,0:T(8,128)(2,1)S(1)} %pad_maximum_fusion.1.up0, ...), custom_call_target="tpu_custom_call" | custom-call | flops 5000000000 | bytes 20000000 | tf_op jit(solution)/shard_map/pallas_call | solution.py:405
  71.2 2.4 %collective-permute-start.25 = (bf16[16,6272]{1,0:T(8,128)(2,1)S(1)}, bf16[16,6272]{1,0:T(8,128)(2,1)S(1)}, u32[]{:S(2)}, u32[]{:S(2)}) collective-permute-start(bf16[16,6272]{1,0:T(8,128)(2,1)S(1)} %get-tuple-element.33), channel_id=1, source_target_pairs={{0,3},{1,0},{2,1},{3,2},{4,7},{5,4},{6,5},{7,6},{8,11},{9,8},{10,9... | collective-permute-start | bytes 602120 | tf_op jit(solution)/shard_map/ppermute | solution.py:305
  73.5 1.3 %collective-permute-start.24 = (bf16[16,6272]{1,0:T(8,128)(2,1)S(1)}, bf16[16,6272]{1,0:T(8,128)(2,1)S(1)}, u32[]{:S(2)}, u32[]{:S(2)}) collective-permute-start(bf16[16,6272]{1,0:T(8,128)(2,1)S(1)} %get-tuple-element.32), channel_id=1, source_target_pairs={{0,2},{1,3},{2,0},{3,1},{4,6},{5,7},{6,4},{7,5},{8,10},{9,11},{10,... | collective-permute-start | bytes 602120 | tf_op jit(solution)/shard_map/ppermute | solution.py:305
  74.8 0.8 collective-permute-start.23
  75.6 1.9 %collective-permute-start.13 = (bf16[16,6272]{1,0:T(8,128)(2,1)S(1)}, bf16[16,6272]{1,0:T(8,128)(2,1)S(1)}, u32[]{:S(2)}, u32[]{:S(2)}) collective-permute-start(bf16[16,6272]{1,0:T(8,128)(2,1)S(1)} %get-tuple-element.24), channel_id=1, source_target_pairs={{0,3},{1,0},{2,1},{3,2},{4,7},{5,4},{6,5},{7,6},{8,11},{9,8},{10,9... | collective-permute-start | bytes 602120 | tf_op jit(solution)/shard_map/ppermute | solution.py:305
  77.5 0.5 collective-permute-start.12
  78.0 0.4 collective-permute-done.25
  78.3 0.0 collective-permute-start.11
  78.3 1.4 %collective-permute-done.24 = bf16[16,6272]{1,0:T(8,128)(2,1)S(1)} collective-permute-done((bf16[16,6272]{1,0:T(8,128)(2,1)S(1)}, bf16[16,6272]{1,0:T(8,128)(2,1)S(1)}, u32[]{:S(2)}, u32[]{:S(2)}) %collective-permute-start.24) | collective-permute-done | bytes 200736 | tf_op jit(solution)/shard_map/ppermute | solution.py:305
  79.7 8.7 %collective-permute-start.19 = (bf16[64,6272]{1,0:T(8,128)(2,1)S(1)}, bf16[64,6272]{1,0:T(8,128)(2,1)S(1)}, u32[]{:S(2)}, u32[]{:S(2)}) collective-permute-start(bf16[64,6272]{1,0:T(8,128)(2,1)S(1)} %get-tuple-element.29), channel_id=1, source_target_pairs={{0,8},{8,0},{16,24},{24,16},{32,40},{40,32},{48,56},{56,48},{64,72... | collective-permute-start | bytes 2408456 | tf_op jit(solution)/shard_map/ppermute | solution.py:308
  88.4 0.1 add_convert_fusion.1
  88.5 1.8 %collective-permute-start.26 = (bf16[16,6272]{1,0:T(8,128)(2,1)S(1)}, bf16[16,6272]{1,0:T(8,128)(2,1)S(1)}, u32[]{:S(2)}, u32[]{:S(2)}) collective-permute-start(bf16[16,6272]{1,0:T(8,128)(2,1)S(1)} %add_convert_fusion.1), channel_id=1, source_target_pairs={{0,248},{8,16},{16,8},{24,32},{32,24},{40,48},{48,40},{56,64},{64,... | collective-permute-start | bytes 602120 | tf_op jit(solution)/shard_map/ppermute | solution.py:311
  90.3 0.0 collective-permute-done.19
  90.4 0.2 add_convert_fusion
  90.6 2.4 %collective-permute-start.22 = (bf16[16,6272]{1,0:T(8,128)(2,1)S(1)}, bf16[16,6272]{1,0:T(8,128)(2,1)S(1)}, u32[]{:S(2)}, u32[]{:S(2)}) collective-permute-start(bf16[16,6272]{1,0:T(8,128)(2,1)S(1)} %get-tuple-element.36), channel_id=1, source_target_pairs={{0,3},{1,0},{2,1},{3,2},{4,7},{5,4},{6,5},{7,6},{8,11},{9,8},{10,9... | collective-permute-start | bytes 602120 | tf_op jit(solution)/shard_map/ppermute | solution.py:305
  93.0 1.6 %collective-permute-start.21 = (bf16[16,6272]{1,0:T(8,128)(2,1)S(1)}, bf16[16,6272]{1,0:T(8,128)(2,1)S(1)}, u32[]{:S(2)}, u32[]{:S(2)}) collective-permute-start(bf16[16,6272]{1,0:T(8,128)(2,1)S(1)} %get-tuple-element.37), channel_id=1, source_target_pairs={{0,2},{1,3},{2,0},{3,1},{4,6},{5,7},{6,4},{7,5},{8,10},{9,11},{10,... | collective-permute-start | bytes 602120 | tf_op jit(solution)/shard_map/ppermute | solution.py:305
  94.6 0.8 collective-permute-start.20
  95.3 0.1 convert_add_fusion.1
  95.5 5.3 %collective-permute-start.14 = (bf16[8,6272]{1,0:T(8,128)(2,1)S(1)}, bf16[8,6272]{1,0:T(8,128)(2,1)S(1)}, u32[]{:S(2)}, u32[]{:S(2)}) collective-permute-start(bf16[8,6272]{1,0:T(8,128)(2,1)S(1)} %slice.64), channel_id=1, source_target_pairs={{0,4},{1,5},{2,6},{3,7},{4,0},{5,1},{6,2},{7,3},{8,12},{9,13},{10,... | collective-permute-start | bytes 301064 | tf_op jit(solution)/shard_map/ppermute | solution.py:302
  100.8 0.4 collective-permute-done.20
  101.2 0.1 convert_add_fusion
  101.4 11.0 %collective-permute-start.27 = (bf16[8,6272]{1,0:T(8,128)(2,1)S(1)}, bf16[8,6272]{1,0:T(8,128)(2,1)S(1)}, u32[]{:S(2)}, u32[]{:S(2)}) collective-permute-start(bf16[8,6272]{1,0:T(8,128)(2,1)S(1)} %slice.63), channel_id=1, source_target_pairs={{0,4},{1,5},{2,6},{3,7},{4,0},{5,1},{6,2},{7,3},{8,12},{9,13},{10,... | collective-permute-start | bytes 301064 | tf_op jit(solution)/shard_map/ppermute | solution.py:302
  112.4 0.7 fusion.6
  113.1 1.8 %collective-permute-done.27 = bf16[8,6272]{1,0:T(8,128)(2,1)S(1)} collective-permute-done((bf16[8,6272]{1,0:T(8,128)(2,1)S(1)}, bf16[8,6272]{1,0:T(8,128)(2,1)S(1)}, u32[]{:S(2)}, u32[]{:S(2)}) %collective-permute-start.27) | collective-permute-done | bytes 100384 | tf_op jit(solution)/shard_map/ppermute | solution.py:302
  115.0 0.7 convert_add_fusion.2
  (44 shorter events, 0.3 us)
Async XLA Ops:
  0.6 9.6 %copy-start = (f32[100,128]{1,0:T(8,128)S(1)}, f32[100,128]{1,0:T(8,128)}, u32[]{:S(2)}) copy-start(f32[100,128]{1,0:T(8,128)} %param.23) | copy-start | bytes 153604
  0.6 25.9 %collective-permute-start = (bf16[8,6272]{1,0:T(8,128)(2,1)}, bf16[8,6272]{1,0:T(8,128)(2,1)S(1)}, u32[]{:S(2)}, u32[]{:S(2)}) collective-permute-start(bf16[8,6272]{1,0:T(8,128)(2,1)} %bitcast.30), channel_id=1, source_target_pairs={{0,4},{1,5},{2,6},{3,7},{4,0},{5,1},{6,2},{7,3},{8,12},{9,13},{10,... | collective-permute-start | bytes 301064 | tf_op jit(solution)/shard_map/ppermute | solution.py:302
  8.5 17.9 %collective-permute-start.10 = (s32[1,32]{1,0:T(1,128)}, s32[1,32]{1,0:T(1,128)S(1)}, u32[]{:S(2)}, u32[]{:S(2)}) collective-permute-start(s32[1,32]{1,0:T(1,128)} %param.27), channel_id=1, source_target_pairs={{0,248},{8,0},{16,8},{24,16},{32,24},{40,32},{48,40},{56,48},{64,5... | collective-permute-start | bytes 392 | tf_op jit(solution)/shard_map/ppermute | solution.py:314
  9.4 16.9 %collective-permute-start.9 = (s32[1,32]{1,0:T(1,128)}, s32[1,32]{1,0:T(1,128)S(1)}, u32[]{:S(2)}, u32[]{:S(2)}) collective-permute-start(s32[1,32]{1,0:T(1,128)} %param.28), channel_id=1, source_target_pairs={{0,8},{8,16},{16,24},{24,32},{32,40},{40,48},{48,56},{56,64},{64,7... | collective-permute-start | bytes 392 | tf_op jit(solution)/shard_map/ppermute | solution.py:314
  12.0 32.7 %collective-permute-start.15 = (bf16[8,6272]{1,0:T(8,128)(2,1)S(1)}, bf16[8,6272]{1,0:T(8,128)(2,1)S(1)}, u32[]{:S(2)}, u32[]{:S(2)}) collective-permute-start(bf16[8,6272]{1,0:T(8,128)(2,1)S(1)} %fusion.7), channel_id=1, source_target_pairs={{0,4},{1,5},{2,6},{3,7},{4,0},{5,1},{6,2},{7,3},{8,12},{9,13},{10,... | collective-permute-start | bytes 301064 | tf_op jit(solution)/shard_map/ppermute | solution.py:302
  16.6 1.0 copy-start.3
  17.6 0.9 copy-start.4
  18.6 0.9 copy-start.5
  19.5 0.9 copy-start.6
  20.5 6.1 %copy-start.8 = (bf16[8,49,128]{2,0,1:T(8,128)(2,1)S(1)}, bf16[8,49,128]{2,0,1:T(8,128)(2,1)}, u32[]{:S(2)}) copy-start(bf16[8,49,128]{2,0,1:T(8,128)(2,1)} %param.21) | copy-start | bytes 301060
  24.9 1.3 %copy-start.7 = (bf16[8,464,256]{2,1,0:T(8,128)(2,1)}, bf16[8,464,256]{2,1,0:T(8,128)(2,1)S(1)}, u32[]{:S(2)}) copy-start(bf16[8,464,256]{2,1,0:T(8,128)(2,1)S(1)} %get-tuple-element.19.turn) | copy-start | bytes 5701636
  26.2 16.7 %copy-start.10 = (s32[128]{0:T(128)S(1)}, s32[128]{0:T(128)}, u32[]{:S(2)}) copy-start(s32[128]{0:T(128)} %param.24) | copy-start | bytes 1540
  26.2 26.9 %copy-start.1 = (bf16[128,128]{1,0:T(8,128)(2,1)S(1)}, bf16[128,128]{1,0:T(8,128)(2,1)}, u32[]{:S(2)}) copy-start(bf16[128,128]{1,0:T(8,128)(2,1)} %basis.1) | copy-start | bytes 98308
  26.2 26.9 %copy-start.2 = (bf16[128,128]{1,0:T(8,128)(2,1)S(1)}, bf16[128,128]{1,0:T(8,128)(2,1)}, u32[]{:S(2)}) copy-start(bf16[128,128]{1,0:T(8,128)(2,1)} %w_rad.3) | copy-start | bytes 98308
  26.6 7.4 %collective-permute-start.1 = (bf16[16,6272]{1,0:T(8,128)(2,1)S(1)}, bf16[16,6272]{1,0:T(8,128)(2,1)S(1)}, u32[]{:S(2)}, u32[]{:S(2)}) collective-permute-start(bf16[16,6272]{1,0:T(8,128)(2,1)S(1)} %pad_maximum_fusion), channel_id=1, source_target_pairs={{0,3},{1,0},{2,1},{3,2},{4,7},{5,4},{6,5},{7,6},{8,11},{9,8},{10,9... | collective-permute-start | bytes 602120 | tf_op jit(solution)/shard_map/ppermute | solution.py:305
  29.1 6.2 %collective-permute-start.2 = (bf16[16,6272]{1,0:T(8,128)(2,1)S(1)}, bf16[16,6272]{1,0:T(8,128)(2,1)S(1)}, u32[]{:S(2)}, u32[]{:S(2)}) collective-permute-start(bf16[16,6272]{1,0:T(8,128)(2,1)S(1)} %pad_maximum_fusion), channel_id=1, source_target_pairs={{0,2},{1,3},{2,0},{3,1},{4,6},{5,7},{6,4},{7,5},{8,10},{9,11},{10,... | collective-permute-start | bytes 602120 | tf_op jit(solution)/shard_map/ppermute | solution.py:305
  29.6 7.7 %collective-permute-start.3 = (bf16[16,6272]{1,0:T(8,128)(2,1)S(1)}, bf16[16,6272]{1,0:T(8,128)(2,1)S(1)}, u32[]{:S(2)}, u32[]{:S(2)}) collective-permute-start(bf16[16,6272]{1,0:T(8,128)(2,1)S(1)} %pad_maximum_fusion), channel_id=1, source_target_pairs={{0,1},{1,2},{2,3},{3,0},{4,5},{5,6},{6,7},{7,4},{8,9},{9,10},{10,1... | collective-permute-start | bytes 602120 | tf_op jit(solution)/shard_map/ppermute | solution.py:305
  30.2 12.9 %collective-permute-start.5 = (bf16[16,6272]{1,0:T(8,128)(2,1)S(1)}, bf16[16,6272]{1,0:T(8,128)(2,1)S(1)}, u32[]{:S(2)}, u32[]{:S(2)}) collective-permute-start(bf16[16,6272]{1,0:T(8,128)(2,1)S(1)} %pad_maximum_fusion), channel_id=1, source_target_pairs={{0,248},{8,16},{16,8},{24,32},{32,24},{40,48},{48,40},{56,64},{64,... | collective-permute-start | bytes 602120 | tf_op jit(solution)/shard_map/ppermute | solution.py:311
  37.4 15.8 %collective-permute-start.4 = (bf16[64,6272]{1,0:T(8,128)(2,1)S(1)}, bf16[64,6272]{1,0:T(8,128)(2,1)S(1)}, u32[]{:S(2)}, u32[]{:S(2)}) collective-permute-start(bf16[64,6272]{1,0:T(8,128)(2,1)S(1)} %constant_dynamic-update-slice_fusion.own), channel_id=1, source_target_pairs={{0,8},{8,0},{16,24},{24,16},{32,40},{40,32},{48,56},{56,48},{64,72... | collective-permute-start | bytes 2408456 | tf_op jit(solution)/shard_map/ppermute | solution.py:308
  43.1 5.5 %collective-permute-start.6 = (bf16[16,6272]{1,0:T(8,128)(2,1)S(1)}, bf16[16,6272]{1,0:T(8,128)(2,1)S(1)}, u32[]{:S(2)}, u32[]{:S(2)}) collective-permute-start(bf16[16,6272]{1,0:T(8,128)(2,1)S(1)} %collective-permute-done.5.far0), channel_id=1, source_target_pairs={{0,3},{1,0},{2,1},{3,2},{4,7},{5,4},{6,5},{7,6},{8,11},{9,8},{10,9... | collective-permute-start | bytes 602120 | tf_op jit(solution)/shard_map/ppermute | solution.py:305
  43.5 6.2 %collective-permute-start.7 = (bf16[16,6272]{1,0:T(8,128)(2,1)S(1)}, bf16[16,6272]{1,0:T(8,128)(2,1)S(1)}, u32[]{:S(2)}, u32[]{:S(2)}) collective-permute-start(bf16[16,6272]{1,0:T(8,128)(2,1)S(1)} %collective-permute-done.5.far0), channel_id=1, source_target_pairs={{0,2},{1,3},{2,0},{3,1},{4,6},{5,7},{6,4},{7,5},{8,10},{9,11},{10,... | collective-permute-start | bytes 602120 | tf_op jit(solution)/shard_map/ppermute | solution.py:305
  44.0 9.1 %collective-permute-start.8 = (bf16[16,6272]{1,0:T(8,128)(2,1)S(1)}, bf16[16,6272]{1,0:T(8,128)(2,1)S(1)}, u32[]{:S(2)}, u32[]{:S(2)}) collective-permute-start(bf16[16,6272]{1,0:T(8,128)(2,1)S(1)} %collective-permute-done.5.far0), channel_id=1, source_target_pairs={{0,1},{1,2},{2,3},{3,0},{4,5},{5,6},{6,7},{7,4},{8,9},{9,10},{10,1... | collective-permute-start | bytes 602120 | tf_op jit(solution)/shard_map/ppermute | solution.py:305
  44.7 16.6 %collective-permute-start.16 = (bf16[16,6272]{1,0:T(8,128)(2,1)S(1)}, bf16[16,6272]{1,0:T(8,128)(2,1)S(1)}, u32[]{:S(2)}, u32[]{:S(2)}) collective-permute-start(bf16[16,6272]{1,0:T(8,128)(2,1)S(1)} %pad_maximum_fusion.1.up0), channel_id=1, source_target_pairs={{0,3},{1,0},{2,1},{3,2},{4,7},{5,4},{6,5},{7,6},{8,11},{9,8},{10,9... | collective-permute-start | bytes 602120 | tf_op jit(solution)/shard_map/ppermute | solution.py:305
  48.6 12.6 %collective-permute-start.17 = (bf16[16,6272]{1,0:T(8,128)(2,1)S(1)}, bf16[16,6272]{1,0:T(8,128)(2,1)S(1)}, u32[]{:S(2)}, u32[]{:S(2)}) collective-permute-start(bf16[16,6272]{1,0:T(8,128)(2,1)S(1)} %pad_maximum_fusion.1.up0), channel_id=1, source_target_pairs={{0,2},{1,3},{2,0},{3,1},{4,6},{5,7},{6,4},{7,5},{8,10},{9,11},{10,... | collective-permute-start | bytes 602120 | tf_op jit(solution)/shard_map/ppermute | solution.py:305
  49.7 11.6 %collective-permute-start.18 = (bf16[16,6272]{1,0:T(8,128)(2,1)S(1)}, bf16[16,6272]{1,0:T(8,128)(2,1)S(1)}, u32[]{:S(2)}, u32[]{:S(2)}) collective-permute-start(bf16[16,6272]{1,0:T(8,128)(2,1)S(1)} %pad_maximum_fusion.1.up0), channel_id=1, source_target_pairs={{0,1},{1,2},{2,3},{3,0},{4,5},{5,6},{6,7},{7,4},{8,9},{9,10},{10,1... | collective-permute-start | bytes 602120 | tf_op jit(solution)/shard_map/ppermute | solution.py:305
  71.2 7.2 %collective-permute-start.25 = (bf16[16,6272]{1,0:T(8,128)(2,1)S(1)}, bf16[16,6272]{1,0:T(8,128)(2,1)S(1)}, u32[]{:S(2)}, u32[]{:S(2)}) collective-permute-start(bf16[16,6272]{1,0:T(8,128)(2,1)S(1)} %get-tuple-element.33), channel_id=1, source_target_pairs={{0,3},{1,0},{2,1},{3,2},{4,7},{5,4},{6,5},{7,6},{8,11},{9,8},{10,9... | collective-permute-start | bytes 602120 | tf_op jit(solution)/shard_map/ppermute | solution.py:305
  73.5 6.2 %collective-permute-start.24 = (bf16[16,6272]{1,0:T(8,128)(2,1)S(1)}, bf16[16,6272]{1,0:T(8,128)(2,1)S(1)}, u32[]{:S(2)}, u32[]{:S(2)}) collective-permute-start(bf16[16,6272]{1,0:T(8,128)(2,1)S(1)} %get-tuple-element.32), channel_id=1, source_target_pairs={{0,2},{1,3},{2,0},{3,1},{4,6},{5,7},{6,4},{7,5},{8,10},{9,11},{10,... | collective-permute-start | bytes 602120 | tf_op jit(solution)/shard_map/ppermute | solution.py:305
  74.8 13.6 %collective-permute-start.23 = (bf16[16,6272]{1,0:T(8,128)(2,1)S(1)}, bf16[16,6272]{1,0:T(8,128)(2,1)S(1)}, u32[]{:S(2)}, u32[]{:S(2)}) collective-permute-start(bf16[16,6272]{1,0:T(8,128)(2,1)S(1)} %get-tuple-element.31), channel_id=1, source_target_pairs={{0,1},{1,2},{2,3},{3,0},{4,5},{5,6},{6,7},{7,4},{8,9},{9,10},{10,1... | collective-permute-start | bytes 602120 | tf_op jit(solution)/shard_map/ppermute | solution.py:305
  75.6 17.4 %collective-permute-start.13 = (bf16[16,6272]{1,0:T(8,128)(2,1)S(1)}, bf16[16,6272]{1,0:T(8,128)(2,1)S(1)}, u32[]{:S(2)}, u32[]{:S(2)}) collective-permute-start(bf16[16,6272]{1,0:T(8,128)(2,1)S(1)} %get-tuple-element.24), channel_id=1, source_target_pairs={{0,3},{1,0},{2,1},{3,2},{4,7},{5,4},{6,5},{7,6},{8,11},{9,8},{10,9... | collective-permute-start | bytes 602120 | tf_op jit(solution)/shard_map/ppermute | solution.py:305
  77.5 17.1 %collective-permute-start.12 = (bf16[16,6272]{1,0:T(8,128)(2,1)S(1)}, bf16[16,6272]{1,0:T(8,128)(2,1)S(1)}, u32[]{:S(2)}, u32[]{:S(2)}) collective-permute-start(bf16[16,6272]{1,0:T(8,128)(2,1)S(1)} %get-tuple-element.23), channel_id=1, source_target_pairs={{0,2},{1,3},{2,0},{3,1},{4,6},{5,7},{6,4},{7,5},{8,10},{9,11},{10,... | collective-permute-start | bytes 602120 | tf_op jit(solution)/shard_map/ppermute | solution.py:305
  78.3 17.0 %collective-permute-start.11 = (bf16[16,6272]{1,0:T(8,128)(2,1)S(1)}, bf16[16,6272]{1,0:T(8,128)(2,1)S(1)}, u32[]{:S(2)}, u32[]{:S(2)}) collective-permute-start(bf16[16,6272]{1,0:T(8,128)(2,1)S(1)} %get-tuple-element.22), channel_id=1, source_target_pairs={{0,1},{1,2},{2,3},{3,0},{4,5},{5,6},{6,7},{7,4},{8,9},{9,10},{10,1... | collective-permute-start | bytes 602120 | tf_op jit(solution)/shard_map/ppermute | solution.py:305
  79.7 10.7 %collective-permute-start.19 = (bf16[64,6272]{1,0:T(8,128)(2,1)S(1)}, bf16[64,6272]{1,0:T(8,128)(2,1)S(1)}, u32[]{:S(2)}, u32[]{:S(2)}) collective-permute-start(bf16[64,6272]{1,0:T(8,128)(2,1)S(1)} %get-tuple-element.29), channel_id=1, source_target_pairs={{0,8},{8,0},{16,24},{24,16},{32,40},{40,32},{48,56},{56,48},{64,72... | collective-permute-start | bytes 2408456 | tf_op jit(solution)/shard_map/ppermute | solution.py:308
  88.5 12.2 %collective-permute-start.26 = (bf16[16,6272]{1,0:T(8,128)(2,1)S(1)}, bf16[16,6272]{1,0:T(8,128)(2,1)S(1)}, u32[]{:S(2)}, u32[]{:S(2)}) collective-permute-start(bf16[16,6272]{1,0:T(8,128)(2,1)S(1)} %add_convert_fusion.1), channel_id=1, source_target_pairs={{0,248},{8,16},{16,8},{24,32},{32,24},{40,48},{48,40},{56,64},{64,... | collective-permute-start | bytes 602120 | tf_op jit(solution)/shard_map/ppermute | solution.py:311
  90.6 10.2 %collective-permute-start.22 = (bf16[16,6272]{1,0:T(8,128)(2,1)S(1)}, bf16[16,6272]{1,0:T(8,128)(2,1)S(1)}, u32[]{:S(2)}, u32[]{:S(2)}) collective-permute-start(bf16[16,6272]{1,0:T(8,128)(2,1)S(1)} %get-tuple-element.36), channel_id=1, source_target_pairs={{0,3},{1,0},{2,1},{3,2},{4,7},{5,4},{6,5},{7,6},{8,11},{9,8},{10,9... | collective-permute-start | bytes 602120 | tf_op jit(solution)/shard_map/ppermute | solution.py:305
  93.0 7.8 %collective-permute-start.21 = (bf16[16,6272]{1,0:T(8,128)(2,1)S(1)}, bf16[16,6272]{1,0:T(8,128)(2,1)S(1)}, u32[]{:S(2)}, u32[]{:S(2)}) collective-permute-start(bf16[16,6272]{1,0:T(8,128)(2,1)S(1)} %get-tuple-element.37), channel_id=1, source_target_pairs={{0,2},{1,3},{2,0},{3,1},{4,6},{5,7},{6,4},{7,5},{8,10},{9,11},{10,... | collective-permute-start | bytes 602120 | tf_op jit(solution)/shard_map/ppermute | solution.py:305
  94.6 6.6 %collective-permute-start.20 = (bf16[16,6272]{1,0:T(8,128)(2,1)S(1)}, bf16[16,6272]{1,0:T(8,128)(2,1)S(1)}, u32[]{:S(2)}, u32[]{:S(2)}) collective-permute-start(bf16[16,6272]{1,0:T(8,128)(2,1)S(1)} %get-tuple-element.35), channel_id=1, source_target_pairs={{0,1},{1,2},{2,3},{3,0},{4,5},{5,6},{6,7},{7,4},{8,9},{9,10},{10,1... | collective-permute-start | bytes 602120 | tf_op jit(solution)/shard_map/ppermute | solution.py:305
  95.3 19.6 %copy-start.9 = (bf16[8,49,128]{2,0,1:T(8,128)(2,1)S(1)}, bf16[8,49,128]{2,0,1:T(8,128)(2,1)}, u32[]{:S(2)}) copy-start(bf16[8,49,128]{2,0,1:T(8,128)(2,1)} %param.37) | copy-start | bytes 301060
  95.5 17.0 %collective-permute-start.14 = (bf16[8,6272]{1,0:T(8,128)(2,1)S(1)}, bf16[8,6272]{1,0:T(8,128)(2,1)S(1)}, u32[]{:S(2)}, u32[]{:S(2)}) collective-permute-start(bf16[8,6272]{1,0:T(8,128)(2,1)S(1)} %slice.64), channel_id=1, source_target_pairs={{0,4},{1,5},{2,6},{3,7},{4,0},{5,1},{6,2},{7,3},{8,12},{9,13},{10,... | collective-permute-start | bytes 301064 | tf_op jit(solution)/shard_map/ppermute | solution.py:302
  101.4 13.6 %collective-permute-start.27 = (bf16[8,6272]{1,0:T(8,128)(2,1)S(1)}, bf16[8,6272]{1,0:T(8,128)(2,1)S(1)}, u32[]{:S(2)}, u32[]{:S(2)}) collective-permute-start(bf16[8,6272]{1,0:T(8,128)(2,1)S(1)} %slice.63), channel_id=1, source_target_pairs={{0,4},{1,5},{2,6},{3,7},{4,0},{5,1},{6,2},{7,3},{8,12},{9,13},{10,... | collective-permute-start | bytes 301064 | tf_op jit(solution)/shard_map/ppermute | solution.py:302

commit v2 on v1

--- a/solution.py
+++ b/solution.py
@@ -46,27 +46,20 @@
 
 
 def selectors():
-    pick_turn = np.zeros((TURN_ROWS, ROT_PAD), np.float32)
-    pick_back = np.zeros((BACK_ROWS, ROT_PAD), np.float32)
-    mask_turn = np.zeros((ROT_PAD, 256), np.float32)
-    mask_back = np.zeros((ROT_PAD, 256), np.float32)
+    pair_all, coef_all, pair_tile, coef_tile = [np.full(ROT_PAD, -1, np.int32) for _ in range(4)]
     offset = 0
     for degree in range(TOP + 1):
         cap = min(degree, 2)
-        [(first, _, pairs, start)] = [
-            e for e, d in zip(TABLE, TILES) if degree in d
-        ]
+        [(first, _, pairs, start)] = [e for e, d in zip(TABLE, TILES) if degree in d]
         for order in range(-cap, cap + 1):
-            row_block = pairs.index((degree, order))
+            place = pairs.index((degree, order))
             for column in range(2 * degree + 1):
                 row = offset + (order + cap) * (2 * degree + 1) + column
                 coef = degree * degree + column
-                pick_turn[start + GROUP * row_block : start + GROUP * (row_block + 1), row] = 1
-                pick_back[GROUP * coef : GROUP * (coef + 1), row] = 1
-                mask_turn[row, GROUP * (coef - first) : GROUP * (coef - first + 1)] = 1
-                mask_back[row, GROUP * row_block : GROUP * (row_block + 1)] = 1
+                pair_all[row], coef_all[row] = start // GROUP + place, coef
+                pair_tile[row], coef_tile[row] = place, coef - first
         offset += (2 * cap + 1) * (2 * degree + 1)
-    return pick_turn, pick_back, mask_turn, mask_back
+    return pair_all[None, :], coef_all[None, :], pair_tile[:, None], coef_tile[:, None]
 
 
 def dot(a, b):
@@ -81,7 +74,7 @@
     return [(s, min(size, total - s)) for s in range(0, total, size)]
 
 
-def prep_kernel(rot, pick_turn, pick_back, mask_turn, mask_back, turn, back):
+def prep_kernel(rot, pair_all, coef_all, pair_tile, coef_tile, turn, back):
     row = lax.broadcasted_iota(jnp.int32, (LANES, 256), 0)
     lane = lax.broadcasted_iota(jnp.int32, (LANES, 256), 1) & (GROUP - 1)
 
@@ -90,15 +83,22 @@
         c = lax.broadcasted_iota(jnp.int32, (rows, 256), 1) & (GROUP - 1)
         return r == c
 
-    keep_turn, keep_back = keep(TURN_ROWS), keep(BACK_ROWS)
+    def pick(rows, ids):
+        group = lax.broadcasted_iota(jnp.int32, (rows, ROT_PAD), 0) // GROUP
+        return (group == ids[...]).astype(F32).astype(BF16)
+
+    def mask(ids):
+        return lax.broadcasted_iota(jnp.int32, (ROT_PAD, 256), 1) // GROUP == ids[...]
+
+    work = (
+        (mask(coef_tile), pick(TURN_ROWS, pair_all), keep(TURN_ROWS), turn),
+        (mask(pair_tile), pick(BACK_ROWS, coef_all), keep(BACK_ROWS), back),
+    )
     for g in range(LANES // GROUP):
         spread = (row == lane + GROUP * g).astype(F32).astype(BF16)
         laid = dot(rot[...], spread)
-        for mask, pick, kept, out in (
-            (mask_turn, pick_turn, keep_turn, turn),
-            (mask_back, pick_back, keep_back, back),
-        ):
-            full = dot(pick[...], (laid * mask[...]).astype(BF16))
+        for masked, picked, kept, out in work:
+            full = dot(picked, jnp.where(masked, laid, 0.0).astype(BF16))
             out[g] = jnp.where(kept, full, 0.0).astype(BF16)
 
 
@@ -195,7 +195,7 @@
 def backward_kernel(
     up0, up1, up2, up3, tgt, src, turn, back, turned, outs, pre, w_rad, w0, w1r, w1i, w2r, w2i,
     own, partner, far0, far1, far2, far3, grad_basis,
-    wide, zero, one, two, grads, rad,
+    wide, zero, one, two, grads, fragments, rad,
 ):
     pick_rows(tgt, (up0, up1, up2, up3), wide)
 
@@ -227,7 +227,7 @@
 
     def take(total, q, scaled):
         lanes = pl.ds(q * LANES, LANES)
-        wide[:, lanes] = (scaled * rad[...]).astype(BF16)
+        fragments[:, lanes] = (scaled * rad[...]).astype(BF16)
         return total + scaled * turned[:, lanes]
 
     for start, size in chunks(7 * LANES, 256):
@@ -246,27 +246,8 @@
                 total = take(total, up + start // LANES + k, a[:LANES, cut] + b[LANES:, cut])
                 total = take(total, down + start // LANES + k, a[LANES:, cut] - b[:LANES, cut])
     grad_basis[...] = dot_nt((total * slope).astype(BF16), w_rad[...])
-    for q in range(ORDERS):
-        lanes = pl.ds(q * LANES, LANES)
-        zero_q = wide[:, lanes]
-        grads[:, lanes] = zero_q.astype(F32)
-    rotate_back_f32(back, grads, wide)
+    rotate_back(back, fragments, wide)
     add_rows(src, wide, (own, partner, far0, far1, far2, far3))
-
-
-def rotate_back_f32(back, fragments, wide):
-    for g in range(LANES // GROUP):
-        rows = pl.ds(GROUP * g, GROUP)
-        for first, coefs, pairs, _ in TABLE:
-            window = jnp.concatenate(
-                [fragments[rows, pl.ds(place_of(*p) * LANES, LANES)] for p in pairs], axis=0
-            ).astype(BF16)
-            block = back[g, pl.ds(GROUP * first, GROUP * coefs), pl.ds(0, GROUP * len(pairs))]
-            result = dot(block, window)
-            for c in range(coefs):
-                wide[rows, pl.ds((first + c) * LANES, LANES)] = result[
-                    GROUP * c : GROUP * (c + 1)
-                ].astype(BF16)
 
 
 def kernel_call(kernel, outs, scratch, flops, moved):
@@ -313,6 +294,9 @@
     def roll(v, k):
         return lax.ppermute(v, "space", [(b, (b + k) % blocks) for b in range(blocks)])
 
+    def after(*values):
+        return lax.optimization_barrier(values)
+
     def spread(v):
         return [v] + [shift(v, 4 - d) for d in (1, 2, 3)]
 
@@ -322,21 +306,36 @@
             total = total + shift(parts[d], d).astype(F32)
         return total
 
+    groups = LANES // GROUP
+    turn, back = kernel_call(
+        prep_kernel,
+        (shaped(groups, TURN_ROWS, 256), shaped(groups, BACK_ROWS, 256)),
+        [],
+        2 * 10**9,
+        6 * 10**6,
+    )(
+        jnp.pad(rotations, ((0, ROT_PAD - ROT_ROWS), (0, 0))),
+        *[jnp.asarray(ids) for ids in selectors()],
+    )
+
+    flat = embeddings.reshape(atoms, WIDE)
+    beyond, turn, back = after(across(flat), turn, back)
+    pair = jnp.concatenate([flat, beyond], axis=0)
+    pair, species, upstream, targets = after(pair, species, cotangent, targets)
+    far_pair = swap_far(pair)
+    own_pieces = spread(pair)
     gain = jnp.dot(
         (species[:, None] == lax.iota(jnp.int32, species_gain.shape[0])[None, :]).astype(F32),
         species_gain,
         precision=lax.Precision.HIGHEST,
     )
-    flat = embeddings.reshape(atoms, WIDE)
-    upstream = (cotangent.astype(F32) * gain[:, None, :] * scale).astype(BF16).reshape(atoms, WIDE)
-
-    pair = jnp.concatenate([flat, across(flat)], axis=0)
-    far_pair = swap_far(pair)
-    own_pieces = spread(pair)
+    upstream = (upstream.astype(F32) * gain[:, None, :] * scale).astype(BF16).reshape(atoms, WIDE)
+    up_pair = jnp.concatenate([upstream, across(upstream)], axis=0)
+    *own_pieces, send_left, send_right, sources = after(*own_pieces, send_left, send_right, sources)
     own_table = jnp.concatenate(own_pieces, axis=0)
     partner_table = swap_near(own_table)
     far_pieces = spread(far_pair)
-    up_pair = jnp.concatenate([upstream, across(upstream)], axis=0)
+    *far_pieces, up_pair = after(*far_pieces, up_pair)
     up_pieces = spread(up_pair)
 
     def slot(atom):
@@ -360,22 +359,6 @@
     src_col, src_row = src[:, None], src[None, :]
     tgt_col, tgt_row = tgt[:, None], tgt[None, :]
 
-    pick_turn, pick_back, mask_turn, mask_back = selectors()
-    groups = LANES // GROUP
-    turn, back = kernel_call(
-        prep_kernel,
-        (shaped(groups, TURN_ROWS, 256), shaped(groups, BACK_ROWS, 256)),
-        [],
-        2 * 10**9,
-        6 * 10**6,
-    )(
-        jnp.pad(rotations, ((0, ROT_PAD - ROT_ROWS), (0, 0))),
-        jnp.asarray(pick_turn, BF16),
-        jnp.asarray(pick_back, BF16),
-        jnp.asarray(mask_turn, F32),
-        jnp.asarray(mask_back, F32),
-    )
-
     def work():
         return [
             pltpu.VMEM((edges, WIDE), BF16),
@@ -397,20 +380,25 @@
     )(own_table, partner_table, *far_pieces, src_col, tgt_row, turn, back, radial_basis, weight_radial, *weights)
 
     agg_pair = collect(aggs)
+    own_grad, near_grad, *far_grads, grad_basis = kernel_call(
+        backward_kernel,
+        (whole, whole, piece, piece, piece, piece, square),
+        work()
+        + [
+            pltpu.VMEM((edges, ORDERS * LANES), F32),
+            pltpu.VMEM((edges, ORDERS * LANES), BF16),
+            pltpu.VMEM((edges, LANES), F32),
+        ],
+        5 * 10**9,
+        20 * 10**6,
+    )(*up_pieces, tgt_col, src_row, turn, back, turned, outs, pre, weight_radial, *weights)
+
+    *far_grads, near_grad, agg_pair = after(*far_grads, near_grad, agg_pair)
+    far_home = swap_far(collect(far_grads).astype(BF16)).astype(F32)
     aggregate = agg_pair[:atoms] + across(agg_pair[atoms:].astype(BF16)).astype(F32)
     updated = (
         embeddings.astype(F32) + gain[:, None, :] * scale * aggregate.reshape(embeddings.shape)
     ).astype(BF16)
-
-    own_grad, near_grad, *far_grads, grad_basis = kernel_call(
-        backward_kernel,
-        (whole, whole, piece, piece, piece, piece, square),
-        work() + [pltpu.VMEM((edges, ORDERS * LANES), F32), pltpu.VMEM((edges, LANES), F32)],
-        5 * 10**9,
-        20 * 10**6,
-    )(*up_pieces, tgt_col, src_row, turn, back, turned, outs, pre, weight_radial, *weights)
-
-    far_home = swap_far(collect(far_grads).astype(BF16)).astype(F32)
     summed = own_grad.astype(F32) + swap_near(near_grad).astype(F32)
     parts = [summed[2 * atoms * d : 2 * atoms * (d + 1)].astype(BF16) for d in range(4)]
     grad_pair = collect(parts) + far_home

time: 116 us -> 116 us (level)
  the two profiles are of different devices: /device:TPU:1 before, /device:TPU:24 now
where the time goes in v2:
time: 116 us; the launch traced here: 115 us
  starting transfers between devices  48.3 us (42%)
  waiting for transfers between devices  35 us (30%)
  Pallas kernels  22.5 us (19%)
  local copies, waits for them, and re-layouts  5.7 us (5%)
  other arithmetic  2.29 us (2%)
  between operations  1.52 us (1%)
    ppermute x18, starting transfers between devices, shift(): lax.ppermute(v, 'edge', [(s, s // 4 * 4 + (s + k) % 4) for s in range(8)])  25.9 us
    ppermute x18, waiting for transfers between devices, shift(): lax.ppermute(v, 'edge', [(s, s // 4 * 4 + (s + k) % 4) for s in range(8)])  23.1 us
    ppermute x4, starting transfers between devices, across(): return lax.ppermute(v, 'edge', [(s, (s + 4) % 8) for s in range(8)])  15.9 us
    ppermute x4, waiting for transfers between devices, across(): return lax.ppermute(v, 'edge', [(s, (s + 4) % 8) for s in range(8)])  11.9 us
    pallas_call x1, Pallas kernels, on_device(): kernel_call(backward_kernel, (whole, whole, piece, piece, piece, piece, s...  9.87 us
    pallas_call x1, Pallas kernels, on_device(): kernel_call(forward_kernel, (piece, piece, piece, piece, kept, kept, squa...  8.21 us
    unnamed x33, local copies, waits for them, and re-layouts  4.54 us
    ppermute x2, starting transfers between devices, roll(): lax.ppermute(v, 'space', [(b, (b + k) % blocks) for b in range(blocks)])  4.51 us
  transfers between devices with their start and end apart: 28, of which 13 were waited for; matrix products, arithmetic and copies ran while one was open for 2% of the time, Pallas kernels for 19%

profile of v2, /device:TPU:24, one launch (start us, length us, event | category | flops | bytes accessed | tf_op | source)
XLA Modules:
  0.0 115.5 jit_solution(14194876386388023127)
XLA Ops:
  0.6 0.0 copy-start
  0.6 7.3 %collective-permute-start = (bf16[8,6272]{1,0:T(8,128)(2,1)}, bf16[8,6272]{1,0:T(8,128)(2,1)S(1)}, u32[]{:S(2)}, u32[]{:S(2)}) collective-permute-start(bf16[8,6272]{1,0:T(8,128)(2,1)} %bitcast.27), channel_id=1, source_target_pairs={{0,4},{1,5},{2,6},{3,7},{4,0},{5,1},{6,2},{7,3},{8,12},{9,13},{10,... | collective-permute-start | bytes 301064 | tf_op jit(solution)/shard_map/ppermute | solution.py:283
  8.6 0.8 pad.4.rot
  9.4 0.9 copy-done.3
  10.3 0.9 copy-done.4
  11.2 0.7 copy-done.5
  11.9 0.7 copy-done.6
  12.6 4.4 %shard_map.220 = (bf16[8,464,256]{2,1,0:T(8,128)(2,1)S(1)}, bf16[8,784,256]{2,1,0:T(8,128)(2,1)}) custom-call(bf16[256,128]{1,0:T(8,128)(2,1)S(1)} %pad.4.rot, s32[1,256]{1,0:T(1,128)S(1)} %copy-done.5, s32[1,256]{1,0:T(1,128)S(1)} %copy-done.6, s32[256,1]{1,0:T(8,128)S(1)} %copy-done.3, s32[256,1]{1,0:T(8,128)S(1)} %copy-done.4), custom_call_target="tpu_custom_call" | custom-call | flops 2000000000 | bytes 6000000 | tf_op jit(solution)/shard_map/pallas_call | solution.py:310
  17.0 1.3 %copy-done.7 = bf16[8,464,256]{2,1,0:T(8,128)(2,1)} copy-done((bf16[8,464,256]{2,1,0:T(8,128)(2,1)}, bf16[8,464,256]{2,1,0:T(8,128)(2,1)S(1)}, u32[]{:S(2)}) %copy-start.7) | copy-done | bytes 1900568
  18.3 0.0 copy-start.2
  18.4 3.1 %collective-permute-start.10 = (bf16[16,6272]{1,0:T(8,128)(2,1)S(1)}, bf16[16,6272]{1,0:T(8,128)(2,1)S(1)}, u32[]{:S(2)}, u32[]{:S(2)}) collective-permute-start(bf16[16,6272]{1,0:T(8,128)(2,1)S(1)} %pad_maximum_fusion), channel_id=1, source_target_pairs={{0,2},{1,3},{2,0},{3,1},{4,6},{5,7},{6,4},{7,5},{8,10},{9,11},{10,... | collective-permute-start | bytes 602120 | tf_op jit(solution)/shard_map/ppermute | solution.py:286
  21.5 0.6 collective-permute-start.11
  22.1 2.6 %collective-permute-start.9 = (bf16[16,6272]{1,0:T(8,128)(2,1)S(1)}, bf16[16,6272]{1,0:T(8,128)(2,1)S(1)}, u32[]{:S(2)}, u32[]{:S(2)}) collective-permute-start(bf16[16,6272]{1,0:T(8,128)(2,1)S(1)} %pad_maximum_fusion), channel_id=1, source_target_pairs={{0,3},{1,0},{2,1},{3,2},{4,7},{5,4},{6,5},{7,6},{8,11},{9,8},{10,9... | collective-permute-start | bytes 602120 | tf_op jit(solution)/shard_map/ppermute | solution.py:286
  24.7 0.4 collective-permute-start.1
  25.1 0.2 broadcast_multiply_fusion
  25.4 1.5 %collective-permute-start.5 = (bf16[8,6272]{1,0:T(8,128)(2,1)S(1)}, bf16[8,6272]{1,0:T(8,128)(2,1)S(1)}, u32[]{:S(2)}, u32[]{:S(2)}) collective-permute-start(bf16[8,6272]{1,0:T(8,128)(2,1)S(1)} %fusion.4), channel_id=1, source_target_pairs={{0,4},{1,5},{2,6},{3,7},{4,0},{5,1},{6,2},{7,3},{8,12},{9,13},{10,... | collective-permute-start | bytes 301064 | tf_op jit(solution)/shard_map/ppermute | solution.py:283
  26.9 0.1 copy.27.tgt
  27.1 0.8 collective-permute-done.10
  27.9 2.8 %collective-permute-done.11 = bf16[16,6272]{1,0:T(8,128)(2,1)S(1)} collective-permute-done((bf16[16,6272]{1,0:T(8,128)(2,1)S(1)}, bf16[16,6272]{1,0:T(8,128)(2,1)S(1)}, u32[]{:S(2)}, u32[]{:S(2)}) %collective-permute-start.11) | collective-permute-done | bytes 200736 | tf_op jit(solution)/shard_map/ppermute | solution.py:286
  30.7 0.1 collective-permute-done.9
  30.9 0.1 collective-permute-start.14
  31.0 4.5 %collective-permute-done.5 = bf16[8,6272]{1,0:T(8,128)(2,1)S(1)} collective-permute-done((bf16[8,6272]{1,0:T(8,128)(2,1)S(1)}, bf16[8,6272]{1,0:T(8,128)(2,1)S(1)}, u32[]{:S(2)}, u32[]{:S(2)}) %collective-permute-start.5) | collective-permute-done | bytes 100384 | tf_op jit(solution)/shard_map/ppermute | solution.py:283
  35.5 0.1 collective-permute-start.12
  35.6 4.4 %collective-permute-start.13 = (s32[1,32]{1,0:T(1,128)S(1)}, s32[1,32]{1,0:T(1,128)S(1)}, u32[]{:S(2)}, u32[]{:S(2)}) collective-permute-start(s32[1,32]{1,0:T(1,128)S(1)} %copy-done.14), channel_id=1, source_target_pairs={{0,248},{8,0},{16,8},{24,16},{32,24},{40,32},{48,40},{56,48},{64,5... | collective-permute-start | bytes 392 | tf_op jit(solution)/shard_map/ppermute | solution.py:295
  40.1 0.0 collective-permute-done.1.far0
  40.1 0.1 collective-permute-start.2
  40.1 1.4 %collective-permute-start.3 = (bf16[16,6272]{1,0:T(8,128)(2,1)S(1)}, bf16[16,6272]{1,0:T(8,128)(2,1)S(1)}, u32[]{:S(2)}, u32[]{:S(2)}) collective-permute-start(bf16[16,6272]{1,0:T(8,128)(2,1)S(1)} %collective-permute-done.1.far0), channel_id=1, source_target_pairs={{0,2},{1,3},{2,0},{3,1},{4,6},{5,7},{6,4},{7,5},{8,10},{9,11},{10,... | collective-permute-start | bytes 602120 | tf_op jit(solution)/shard_map/ppermute | solution.py:286
  41.6 0.0 collective-permute-done.12
  41.6 0.6 collective-permute-start.4
  42.2 0.0 collective-permute-done.13
  42.2 0.1 add_bitcast_fusion
  42.2 0.1 select_reduce_fusion
  42.4 0.1 copy.26.src
  42.5 4.6 %collective-permute-done.2.far1 = bf16[16,6272]{1,0:T(8,128)(2,1)S(1)} collective-permute-done((bf16[16,6272]{1,0:T(8,128)(2,1)S(1)}, bf16[16,6272]{1,0:T(8,128)(2,1)S(1)}, u32[]{:S(2)}, u32[]{:S(2)}) %collective-permute-start.2) | collective-permute-done | bytes 200736 | tf_op jit(solution)/shard_map/ppermute | solution.py:286
  47.1 1.6 %collective-permute-done.3.far2 = bf16[16,6272]{1,0:T(8,128)(2,1)S(1)} collective-permute-done((bf16[16,6272]{1,0:T(8,128)(2,1)S(1)}, bf16[16,6272]{1,0:T(8,128)(2,1)S(1)}, u32[]{:S(2)}, u32[]{:S(2)}) %collective-permute-start.3) | collective-permute-done | bytes 200736 | tf_op jit(solution)/shard_map/ppermute | solution.py:286
  48.7 2.1 %collective-permute-done.4.far3 = bf16[16,6272]{1,0:T(8,128)(2,1)S(1)} collective-permute-done((bf16[16,6272]{1,0:T(8,128)(2,1)S(1)}, bf16[16,6272]{1,0:T(8,128)(2,1)S(1)}, u32[]{:S(2)}, u32[]{:S(2)}) %collective-permute-start.4) | collective-permute-done | bytes 200736 | tf_op jit(solution)/shard_map/ppermute | solution.py:286
  50.8 1.1 collective-permute-start.6
  51.9 0.5 collective-permute-start.7
  52.4 0.8 collective-permute-start.8
  53.3 8.2 %shard_map.221 = (bf16[16,6272]{1,0:T(8,128)(2,1)S(1)}, bf16[16,6272]{1,0:T(8,128)(2,1)S(1)}, bf16[16,6272]{1,0:T(8,128)(2,1)S(1)}, bf16[16,6272]{1,0:T(8,128)(2...) custom-call(bf16[64,6272]{1,0:T(8,128)(2,1)S(1)} %constant_dynamic-update-slice_fusion.own, ...), custom_call_target="tpu_custom_call" | custom-call | flops 4000000000 | bytes 20000000 | tf_op jit(solution)/shard_map/pallas_call | solution.py:374
  61.5 2.2 %collective-permute-start.15 = (bf16[16,6272]{1,0:T(8,128)(2,1)S(1)}, bf16[16,6272]{1,0:T(8,128)(2,1)S(1)}, u32[]{:S(2)}, u32[]{:S(2)}) collective-permute-start(bf16[16,6272]{1,0:T(8,128)(2,1)S(1)} %get-tuple-element.74), channel_id=1, source_target_pairs={{0,1},{1,2},{2,3},{3,0},{4,5},{5,6},{6,7},{7,4},{8,9},{9,10},{10,1... | collective-permute-start | bytes 602120 | tf_op jit(solution)/shard_map/ppermute | solution.py:286
  63.6 1.7 %collective-permute-start.16 = (bf16[16,6272]{1,0:T(8,128)(2,1)S(1)}, bf16[16,6272]{1,0:T(8,128)(2,1)S(1)}, u32[]{:S(2)}, u32[]{:S(2)}) collective-permute-start(bf16[16,6272]{1,0:T(8,128)(2,1)S(1)} %get-tuple-element.75), channel_id=1, source_target_pairs={{0,2},{1,3},{2,0},{3,1},{4,6},{5,7},{6,4},{7,5},{8,10},{9,11},{10,... | collective-permute-start | bytes 602120 | tf_op jit(solution)/shard_map/ppermute | solution.py:286
  65.4 2.5 %collective-permute-start.17 = (bf16[16,6272]{1,0:T(8,128)(2,1)S(1)}, bf16[16,6272]{1,0:T(8,128)(2,1)S(1)}, u32[]{:S(2)}, u32[]{:S(2)}) collective-permute-start(bf16[16,6272]{1,0:T(8,128)(2,1)S(1)} %get-tuple-element.76), channel_id=1, source_target_pairs={{0,3},{1,0},{2,1},{3,2},{4,7},{5,4},{6,5},{7,6},{8,11},{9,8},{10,9... | collective-permute-start | bytes 602120 | tf_op jit(solution)/shard_map/ppermute | solution.py:286
  67.8 9.9 %shard_map.222 = (bf16[64,6272]{1,0:T(8,128)(2,1)S(1)}, bf16[64,6272]{1,0:T(8,128)(2,1)S(1)}, bf16[16,6272]{1,0:T(8,128)(2,1)S(1)}, bf16[16,6272]{1,0:T(8,128)(2...) custom-call(bf16[16,6272]{1,0:T(8,128)(2,1)S(1)} %pad_maximum_fusion.1.up0, ...), custom_call_target="tpu_custom_call" | custom-call | flops 5000000000 | bytes 20000000 | tf_op jit(solution)/shard_map/pallas_call | solution.py:383
  77.8 0.1 convert_add_fusion.1
  77.9 0.1 collective-permute-start.23
  77.9 1.5 %collective-permute-start.24 = (bf16[16,6272]{1,0:T(8,128)(2,1)S(1)}, bf16[16,6272]{1,0:T(8,128)(2,1)S(1)}, u32[]{:S(2)}, u32[]{:S(2)}) collective-permute-start(bf16[16,6272]{1,0:T(8,128)(2,1)S(1)} %get-tuple-element.82), channel_id=1, source_target_pairs={{0,2},{1,3},{2,0},{3,1},{4,6},{5,7},{6,4},{7,5},{8,10},{9,11},{10,... | collective-permute-start | bytes 602120 | tf_op jit(solution)/shard_map/ppermute | solution.py:286
  79.4 1.8 %collective-permute-start.25 = (bf16[16,6272]{1,0:T(8,128)(2,1)S(1)}, bf16[16,6272]{1,0:T(8,128)(2,1)S(1)}, u32[]{:S(2)}, u32[]{:S(2)}) collective-permute-start(bf16[16,6272]{1,0:T(8,128)(2,1)S(1)} %get-tuple-element.83), channel_id=1, source_target_pairs={{0,3},{1,0},{2,1},{3,2},{4,7},{5,4},{6,5},{7,6},{8,11},{9,8},{10,9... | collective-permute-start | bytes 602120 | tf_op jit(solution)/shard_map/ppermute | solution.py:286
  81.2 6.0 %collective-permute-done.23 = bf16[16,6272]{1,0:T(8,128)(2,1)S(1)} collective-permute-done((bf16[16,6272]{1,0:T(8,128)(2,1)S(1)}, bf16[16,6272]{1,0:T(8,128)(2,1)S(1)}, u32[]{:S(2)}, u32[]{:S(2)}) %collective-permute-start.23) | collective-permute-done | bytes 200736 | tf_op jit(solution)/shard_map/ppermute | solution.py:286
  87.2 0.7 collective-permute-done.25
  87.9 0.1 add_convert_fusion.1
  88.0 1.5 %collective-permute-start.26 = (bf16[16,6272]{1,0:T(8,128)(2,1)S(1)}, bf16[16,6272]{1,0:T(8,128)(2,1)S(1)}, u32[]{:S(2)}, u32[]{:S(2)}) collective-permute-start(bf16[16,6272]{1,0:T(8,128)(2,1)S(1)} %add_convert_fusion.1), channel_id=1, source_target_pairs={{0,248},{8,16},{16,8},{24,32},{32,24},{40,48},{48,40},{56,64},{64,... | collective-permute-start | bytes 602120 | tf_op jit(solution)/shard_map/ppermute | solution.py:292
  89.5 0.2 add_convert_fusion
  89.7 1.0 collective-permute-start.20
  90.8 4.3 %collective-permute-start.21 = (bf16[16,6272]{1,0:T(8,128)(2,1)S(1)}, bf16[16,6272]{1,0:T(8,128)(2,1)S(1)}, u32[]{:S(2)}, u32[]{:S(2)}) collective-permute-start(bf16[16,6272]{1,0:T(8,128)(2,1)S(1)} %get-tuple-element.87), channel_id=1, source_target_pairs={{0,2},{1,3},{2,0},{3,1},{4,6},{5,7},{6,4},{7,5},{8,10},{9,11},{10,... | collective-permute-start | bytes 602120 | tf_op jit(solution)/shard_map/ppermute | solution.py:286
  95.1 4.5 %collective-permute-start.18 = (bf16[8,6272]{1,0:T(8,128)(2,1)S(1)}, bf16[8,6272]{1,0:T(8,128)(2,1)S(1)}, u32[]{:S(2)}, u32[]{:S(2)}) collective-permute-start(bf16[8,6272]{1,0:T(8,128)(2,1)S(1)} %slice.55), channel_id=1, source_target_pairs={{0,4},{1,5},{2,6},{3,7},{4,0},{5,1},{6,2},{7,3},{8,12},{9,13},{10,... | collective-permute-start | bytes 301064 | tf_op jit(solution)/shard_map/ppermute | solution.py:283
  99.6 0.2 collective-permute-done.20
  99.9 4.1 %collective-permute-done.21 = bf16[16,6272]{1,0:T(8,128)(2,1)S(1)} collective-permute-done((bf16[16,6272]{1,0:T(8,128)(2,1)S(1)}, bf16[16,6272]{1,0:T(8,128)(2,1)S(1)}, u32[]{:S(2)}, u32[]{:S(2)}) %collective-permute-start.21) | collective-permute-done | bytes 200736 | tf_op jit(solution)/shard_map/ppermute | solution.py:286
  103.9 0.1 collective-permute-done.22
  104.0 0.1 convert_add_fusion
  104.1 2.6 %collective-permute-start.27 = (bf16[8,6272]{1,0:T(8,128)(2,1)S(1)}, bf16[8,6272]{1,0:T(8,128)(2,1)S(1)}, u32[]{:S(2)}, u32[]{:S(2)}) collective-permute-start(bf16[8,6272]{1,0:T(8,128)(2,1)S(1)} %slice.54), channel_id=1, source_target_pairs={{0,4},{1,5},{2,6},{3,7},{4,0},{5,1},{6,2},{7,3},{8,12},{9,13},{10,... | collective-permute-start | bytes 301064 | tf_op jit(solution)/shard_map/ppermute | solution.py:283
  106.7 0.7 fusion.3
  107.4 7.4 %collective-permute-done.27 = bf16[8,6272]{1,0:T(8,128)(2,1)S(1)} collective-permute-done((bf16[8,6272]{1,0:T(8,128)(2,1)S(1)}, bf16[8,6272]{1,0:T(8,128)(2,1)S(1)}, u32[]{:S(2)}, u32[]{:S(2)}) %collective-permute-start.27) | collective-permute-done | bytes 100384 | tf_op jit(solution)/shard_map/ppermute | solution.py:283
  114.7 0.7 fusion.1
  (51 shorter events, 0.4 us)
Async XLA Ops:
  0.6 24.5 %copy-start = (f32[100,128]{1,0:T(8,128)S(1)}, f32[100,128]{1,0:T(8,128)}, u32[]{:S(2)}) copy-start(f32[100,128]{1,0:T(8,128)} %param.23) | copy-start | bytes 153604
  0.6 17.7 %collective-permute-start = (bf16[8,6272]{1,0:T(8,128)(2,1)}, bf16[8,6272]{1,0:T(8,128)(2,1)S(1)}, u32[]{:S(2)}, u32[]{:S(2)}) collective-permute-start(bf16[8,6272]{1,0:T(8,128)(2,1)} %bitcast.27), channel_id=1, source_target_pairs={{0,4},{1,5},{2,6},{3,7},{4,0},{5,1},{6,2},{7,3},{8,12},{9,13},{10,... | collective-permute-start | bytes 301064 | tf_op jit(solution)/shard_map/ppermute | solution.py:283
  9.4 0.9 copy-start.3
  10.3 0.9 copy-start.4
  11.2 0.7 copy-start.5
  11.9 0.7 copy-start.6
  12.6 5.7 %copy-start.9 = (bf16[8,49,128]{2,0,1:T(8,128)(2,1)S(1)}, bf16[8,49,128]{2,0,1:T(8,128)(2,1)}, u32[]{:S(2)}) copy-start(bf16[8,49,128]{2,0,1:T(8,128)(2,1)} %param.21) | copy-start | bytes 301060
  12.6 12.6 %copy-start.12 = (s32[8]{0:T(128)S(1)}, s32[8]{0:T(128)}, u32[]{:S(2)}) copy-start(s32[8]{0:T(128)} %param.22) | copy-start | bytes 100
  12.6 12.7 %copy-start.8 = (bf16[8,49,128]{2,0,1:T(8,128)(2,1)S(1)}, bf16[8,49,128]{2,0,1:T(8,128)(2,1)}, u32[]{:S(2)}) copy-start(bf16[8,49,128]{2,0,1:T(8,128)(2,1)} %param.37) | copy-start | bytes 301060
  12.6 14.3 %copy-start.10 = (s32[128]{0:T(128)S(1)}, s32[128]{0:T(128)}, u32[]{:S(2)}) copy-start(s32[128]{0:T(128)} %param.25) | copy-start | bytes 1540
  17.0 1.3 %copy-start.7 = (bf16[8,464,256]{2,1,0:T(8,128)(2,1)}, bf16[8,464,256]{2,1,0:T(8,128)(2,1)S(1)}, u32[]{:S(2)}) copy-start(bf16[8,464,256]{2,1,0:T(8,128)(2,1)S(1)} %get-tuple-element.55.turn) | copy-start | bytes 5701636
  18.3 17.2 %copy-start.13 = (s32[1,32]{1,0:T(1,128)S(1)}, s32[1,32]{1,0:T(1,128)}, u32[]{:S(2)}) copy-start(s32[1,32]{1,0:T(1,128)} %param.28) | copy-start | bytes 388
  18.3 17.3 %copy-start.14 = (s32[1,32]{1,0:T(1,128)S(1)}, s32[1,32]{1,0:T(1,128)}, u32[]{:S(2)}) copy-start(s32[1,32]{1,0:T(1,128)} %param.27) | copy-start | bytes 388
  18.3 21.8 %copy-start.11 = (s32[128]{0:T(128)S(1)}, s32[128]{0:T(128)}, u32[]{:S(2)}) copy-start(s32[128]{0:T(128)} %param.24) | copy-start | bytes 1540
  18.3 35.0 %copy-start.1 = (bf16[128,128]{1,0:T(8,128)(2,1)S(1)}, bf16[128,128]{1,0:T(8,128)(2,1)}, u32[]{:S(2)}) copy-start(bf16[128,128]{1,0:T(8,128)(2,1)} %basis.1) | copy-start | bytes 98308
  18.3 35.0 %copy-start.2 = (bf16[128,128]{1,0:T(8,128)(2,1)S(1)}, bf16[128,128]{1,0:T(8,128)(2,1)}, u32[]{:S(2)}) copy-start(bf16[128,128]{1,0:T(8,128)(2,1)} %w_rad.3) | copy-start | bytes 98308
  18.4 9.5 %collective-permute-start.10 = (bf16[16,6272]{1,0:T(8,128)(2,1)S(1)}, bf16[16,6272]{1,0:T(8,128)(2,1)S(1)}, u32[]{:S(2)}, u32[]{:S(2)}) collective-permute-start(bf16[16,6272]{1,0:T(8,128)(2,1)S(1)} %pad_maximum_fusion), channel_id=1, source_target_pairs={{0,2},{1,3},{2,0},{3,1},{4,6},{5,7},{6,4},{7,5},{8,10},{9,11},{10,... | collective-permute-start | bytes 602120 | tf_op jit(solution)/shard_map/ppermute | solution.py:286
  21.5 9.2 %collective-permute-start.11 = (bf16[16,6272]{1,0:T(8,128)(2,1)S(1)}, bf16[16,6272]{1,0:T(8,128)(2,1)S(1)}, u32[]{:S(2)}, u32[]{:S(2)}) collective-permute-start(bf16[16,6272]{1,0:T(8,128)(2,1)S(1)} %pad_maximum_fusion), channel_id=1, source_target_pairs={{0,1},{1,2},{2,3},{3,0},{4,5},{5,6},{6,7},{7,4},{8,9},{9,10},{10,1... | collective-permute-start | bytes 602120 | tf_op jit(solution)/shard_map/ppermute | solution.py:286
  22.1 8.7 %collective-permute-start.9 = (bf16[16,6272]{1,0:T(8,128)(2,1)S(1)}, bf16[16,6272]{1,0:T(8,128)(2,1)S(1)}, u32[]{:S(2)}, u32[]{:S(2)}) collective-permute-start(bf16[16,6272]{1,0:T(8,128)(2,1)S(1)} %pad_maximum_fusion), channel_id=1, source_target_pairs={{0,3},{1,0},{2,1},{3,2},{4,7},{5,4},{6,5},{7,6},{8,11},{9,8},{10,9... | collective-permute-start | bytes 602120 | tf_op jit(solution)/shard_map/ppermute | solution.py:286
  24.7 15.4 %collective-permute-start.1 = (bf16[16,6272]{1,0:T(8,128)(2,1)S(1)}, bf16[16,6272]{1,0:T(8,128)(2,1)S(1)}, u32[]{:S(2)}, u32[]{:S(2)}) collective-permute-start(bf16[16,6272]{1,0:T(8,128)(2,1)S(1)} %pad_maximum_fusion), channel_id=1, source_target_pairs={{0,248},{8,16},{16,8},{24,32},{32,24},{40,48},{48,40},{56,64},{64,... | collective-permute-start | bytes 602120 | tf_op jit(solution)/shard_map/ppermute | solution.py:292
  25.4 10.1 %collective-permute-start.5 = (bf16[8,6272]{1,0:T(8,128)(2,1)S(1)}, bf16[8,6272]{1,0:T(8,128)(2,1)S(1)}, u32[]{:S(2)}, u32[]{:S(2)}) collective-permute-start(bf16[8,6272]{1,0:T(8,128)(2,1)S(1)} %fusion.4), channel_id=1, source_target_pairs={{0,4},{1,5},{2,6},{3,7},{4,0},{5,1},{6,2},{7,3},{8,12},{9,13},{10,... | collective-permute-start | bytes 301064 | tf_op jit(solution)/shard_map/ppermute | solution.py:283
  30.9 22.4 %collective-permute-start.14 = (bf16[64,6272]{1,0:T(8,128)(2,1)S(1)}, bf16[64,6272]{1,0:T(8,128)(2,1)S(1)}, u32[]{:S(2)}, u32[]{:S(2)}) collective-permute-start(bf16[64,6272]{1,0:T(8,128)(2,1)S(1)} %constant_dynamic-update-slice_fusion.own), channel_id=1, source_target_pairs={{0,8},{8,0},{16,24},{24,16},{32,40},{40,32},{48,56},{56,48},{64,72... | collective-permute-start | bytes 2408456 | tf_op jit(solution)/shard_map/ppermute | solution.py:289
  35.5 6.0 %collective-permute-start.12 = (s32[1,32]{1,0:T(1,128)S(1)}, s32[1,32]{1,0:T(1,128)S(1)}, u32[]{:S(2)}, u32[]{:S(2)}) collective-permute-start(s32[1,32]{1,0:T(1,128)S(1)} %copy-done.13), channel_id=1, source_target_pairs={{0,8},{8,16},{16,24},{24,32},{32,40},{40,48},{48,56},{56,64},{64,7... | collective-permute-start | bytes 392 | tf_op jit(solution)/shard_map/ppermute | solution.py:295
  35.6 6.5 %collective-permute-start.13 = (s32[1,32]{1,0:T(1,128)S(1)}, s32[1,32]{1,0:T(1,128)S(1)}, u32[]{:S(2)}, u32[]{:S(2)}) collective-permute-start(s32[1,32]{1,0:T(1,128)S(1)} %copy-done.14), channel_id=1, source_target_pairs={{0,248},{8,0},{16,8},{24,16},{32,24},{40,32},{48,40},{56,48},{64,5... | collective-permute-start | bytes 392 | tf_op jit(solution)/shard_map/ppermute | solution.py:295
  40.1 7.0 %collective-permute-start.2 = (bf16[16,6272]{1,0:T(8,128)(2,1)S(1)}, bf16[16,6272]{1,0:T(8,128)(2,1)S(1)}, u32[]{:S(2)}, u32[]{:S(2)}) collective-permute-start(bf16[16,6272]{1,0:T(8,128)(2,1)S(1)} %collective-permute-done.1.far0), channel_id=1, source_target_pairs={{0,3},{1,0},{2,1},{3,2},{4,7},{5,4},{6,5},{7,6},{8,11},{9,8},{10,9... | collective-permute-start | bytes 602120 | tf_op jit(solution)/shard_map/ppermute | solution.py:286
  40.1 8.6 %collective-permute-start.3 = (bf16[16,6272]{1,0:T(8,128)(2,1)S(1)}, bf16[16,6272]{1,0:T(8,128)(2,1)S(1)}, u32[]{:S(2)}, u32[]{:S(2)}) collective-permute-start(bf16[16,6272]{1,0:T(8,128)(2,1)S(1)} %collective-permute-done.1.far0), channel_id=1, source_target_pairs={{0,2},{1,3},{2,0},{3,1},{4,6},{5,7},{6,4},{7,5},{8,10},{9,11},{10,... | collective-permute-start | bytes 602120 | tf_op jit(solution)/shard_map/ppermute | solution.py:286
  41.6 9.2 %collective-permute-start.4 = (bf16[16,6272]{1,0:T(8,128)(2,1)S(1)}, bf16[16,6272]{1,0:T(8,128)(2,1)S(1)}, u32[]{:S(2)}, u32[]{:S(2)}) collective-permute-start(bf16[16,6272]{1,0:T(8,128)(2,1)S(1)} %collective-permute-done.1.far0), channel_id=1, source_target_pairs={{0,1},{1,2},{2,3},{3,0},{4,5},{5,6},{6,7},{7,4},{8,9},{9,10},{10,1... | collective-permute-start | bytes 602120 | tf_op jit(solution)/shard_map/ppermute | solution.py:286
  50.8 14.6 %collective-permute-start.6 = (bf16[16,6272]{1,0:T(8,128)(2,1)S(1)}, bf16[16,6272]{1,0:T(8,128)(2,1)S(1)}, u32[]{:S(2)}, u32[]{:S(2)}) collective-permute-start(bf16[16,6272]{1,0:T(8,128)(2,1)S(1)} %pad_maximum_fusion.1.up0), channel_id=1, source_target_pairs={{0,3},{1,0},{2,1},{3,2},{4,7},{5,4},{6,5},{7,6},{8,11},{9,8},{10,9... | collective-permute-start | bytes 602120 | tf_op jit(solution)/shard_map/ppermute | solution.py:286
  51.9 15.9 %collective-permute-start.7 = (bf16[16,6272]{1,0:T(8,128)(2,1)S(1)}, bf16[16,6272]{1,0:T(8,128)(2,1)S(1)}, u32[]{:S(2)}, u32[]{:S(2)}) collective-permute-start(bf16[16,6272]{1,0:T(8,128)(2,1)S(1)} %pad_maximum_fusion.1.up0), channel_id=1, source_target_pairs={{0,2},{1,3},{2,0},{3,1},{4,6},{5,7},{6,4},{7,5},{8,10},{9,11},{10,... | collective-permute-start | bytes 602120 | tf_op jit(solution)/shard_map/ppermute | solution.py:286
  52.4 15.4 %collective-permute-start.8 = (bf16[16,6272]{1,0:T(8,128)(2,1)S(1)}, bf16[16,6272]{1,0:T(8,128)(2,1)S(1)}, u32[]{:S(2)}, u32[]{:S(2)}) collective-permute-start(bf16[16,6272]{1,0:T(8,128)(2,1)S(1)} %pad_maximum_fusion.1.up0), channel_id=1, source_target_pairs={{0,1},{1,2},{2,3},{3,0},{4,5},{5,6},{6,7},{7,4},{8,9},{9,10},{10,1... | collective-permute-start | bytes 602120 | tf_op jit(solution)/shard_map/ppermute | solution.py:286
  61.5 16.2 %collective-permute-start.15 = (bf16[16,6272]{1,0:T(8,128)(2,1)S(1)}, bf16[16,6272]{1,0:T(8,128)(2,1)S(1)}, u32[]{:S(2)}, u32[]{:S(2)}) collective-permute-start(bf16[16,6272]{1,0:T(8,128)(2,1)S(1)} %get-tuple-element.74), channel_id=1, source_target_pairs={{0,1},{1,2},{2,3},{3,0},{4,5},{5,6},{6,7},{7,4},{8,9},{9,10},{10,1... | collective-permute-start | bytes 602120 | tf_op jit(solution)/shard_map/ppermute | solution.py:286
  63.6 14.1 %collective-permute-start.16 = (bf16[16,6272]{1,0:T(8,128)(2,1)S(1)}, bf16[16,6272]{1,0:T(8,128)(2,1)S(1)}, u32[]{:S(2)}, u32[]{:S(2)}) collective-permute-start(bf16[16,6272]{1,0:T(8,128)(2,1)S(1)} %get-tuple-element.75), channel_id=1, source_target_pairs={{0,2},{1,3},{2,0},{3,1},{4,6},{5,7},{6,4},{7,5},{8,10},{9,11},{10,... | collective-permute-start | bytes 602120 | tf_op jit(solution)/shard_map/ppermute | solution.py:286
  65.4 12.4 %collective-permute-start.17 = (bf16[16,6272]{1,0:T(8,128)(2,1)S(1)}, bf16[16,6272]{1,0:T(8,128)(2,1)S(1)}, u32[]{:S(2)}, u32[]{:S(2)}) collective-permute-start(bf16[16,6272]{1,0:T(8,128)(2,1)S(1)} %get-tuple-element.76), channel_id=1, source_target_pairs={{0,3},{1,0},{2,1},{3,2},{4,7},{5,4},{6,5},{7,6},{8,11},{9,8},{10,9... | collective-permute-start | bytes 602120 | tf_op jit(solution)/shard_map/ppermute | solution.py:286
  77.9 9.3 %collective-permute-start.23 = (bf16[16,6272]{1,0:T(8,128)(2,1)S(1)}, bf16[16,6272]{1,0:T(8,128)(2,1)S(1)}, u32[]{:S(2)}, u32[]{:S(2)}) collective-permute-start(bf16[16,6272]{1,0:T(8,128)(2,1)S(1)} %get-tuple-element.81), channel_id=1, source_target_pairs={{0,1},{1,2},{2,3},{3,0},{4,5},{5,6},{6,7},{7,4},{8,9},{9,10},{10,1... | collective-permute-start | bytes 602120 | tf_op jit(solution)/shard_map/ppermute | solution.py:286
  77.9 9.2 %collective-permute-start.24 = (bf16[16,6272]{1,0:T(8,128)(2,1)S(1)}, bf16[16,6272]{1,0:T(8,128)(2,1)S(1)}, u32[]{:S(2)}, u32[]{:S(2)}) collective-permute-start(bf16[16,6272]{1,0:T(8,128)(2,1)S(1)} %get-tuple-element.82), channel_id=1, source_target_pairs={{0,2},{1,3},{2,0},{3,1},{4,6},{5,7},{6,4},{7,5},{8,10},{9,11},{10,... | collective-permute-start | bytes 602120 | tf_op jit(solution)/shard_map/ppermute | solution.py:286
  79.4 8.5 %collective-permute-start.25 = (bf16[16,6272]{1,0:T(8,128)(2,1)S(1)}, bf16[16,6272]{1,0:T(8,128)(2,1)S(1)}, u32[]{:S(2)}, u32[]{:S(2)}) collective-permute-start(bf16[16,6272]{1,0:T(8,128)(2,1)S(1)} %get-tuple-element.83), channel_id=1, source_target_pairs={{0,3},{1,0},{2,1},{3,2},{4,7},{5,4},{6,5},{7,6},{8,11},{9,8},{10,9... | collective-permute-start | bytes 602120 | tf_op jit(solution)/shard_map/ppermute | solution.py:286
  81.2 8.3 %collective-permute-start.19 = (bf16[64,6272]{1,0:T(8,128)(2,1)S(1)}, bf16[64,6272]{1,0:T(8,128)(2,1)S(1)}, u32[]{:S(2)}, u32[]{:S(2)}) collective-permute-start(bf16[64,6272]{1,0:T(8,128)(2,1)S(1)} %get-tuple-element.79), channel_id=1, source_target_pairs={{0,8},{8,0},{16,24},{24,16},{32,40},{40,32},{48,56},{56,48},{64,72... | collective-permute-start | bytes 2408456 | tf_op jit(solution)/shard_map/ppermute | solution.py:289
  88.0 11.6 %collective-permute-start.26 = (bf16[16,6272]{1,0:T(8,128)(2,1)S(1)}, bf16[16,6272]{1,0:T(8,128)(2,1)S(1)}, u32[]{:S(2)}, u32[]{:S(2)}) collective-permute-start(bf16[16,6272]{1,0:T(8,128)(2,1)S(1)} %add_convert_fusion.1), channel_id=1, source_target_pairs={{0,248},{8,16},{16,8},{24,32},{32,24},{40,48},{48,40},{56,64},{64,... | collective-permute-start | bytes 602120 | tf_op jit(solution)/shard_map/ppermute | solution.py:292
  89.7 10.1 %collective-permute-start.20 = (bf16[16,6272]{1,0:T(8,128)(2,1)S(1)}, bf16[16,6272]{1,0:T(8,128)(2,1)S(1)}, u32[]{:S(2)}, u32[]{:S(2)}) collective-permute-start(bf16[16,6272]{1,0:T(8,128)(2,1)S(1)} %get-tuple-element.85), channel_id=1, source_target_pairs={{0,1},{1,2},{2,3},{3,0},{4,5},{5,6},{6,7},{7,4},{8,9},{9,10},{10,1... | collective-permute-start | bytes 602120 | tf_op jit(solution)/shard_map/ppermute | solution.py:286
  90.8 13.1 %collective-permute-start.21 = (bf16[16,6272]{1,0:T(8,128)(2,1)S(1)}, bf16[16,6272]{1,0:T(8,128)(2,1)S(1)}, u32[]{:S(2)}, u32[]{:S(2)}) collective-permute-start(bf16[16,6272]{1,0:T(8,128)(2,1)S(1)} %get-tuple-element.87), channel_id=1, source_target_pairs={{0,2},{1,3},{2,0},{3,1},{4,6},{5,7},{6,4},{7,5},{8,10},{9,11},{10,... | collective-permute-start | bytes 602120 | tf_op jit(solution)/shard_map/ppermute | solution.py:286
  95.1 8.9 %collective-permute-start.22 = (bf16[16,6272]{1,0:T(8,128)(2,1)S(1)}, bf16[16,6272]{1,0:T(8,128)(2,1)S(1)}, u32[]{:S(2)}, u32[]{:S(2)}) collective-permute-start(bf16[16,6272]{1,0:T(8,128)(2,1)S(1)} %get-tuple-element.86), channel_id=1, source_target_pairs={{0,3},{1,0},{2,1},{3,2},{4,7},{5,4},{6,5},{7,6},{8,11},{9,8},{10,9... | collective-permute-start | bytes 602120 | tf_op jit(solution)/shard_map/ppermute | solution.py:286
  95.1 11.6 %collective-permute-start.18 = (bf16[8,6272]{1,0:T(8,128)(2,1)S(1)}, bf16[8,6272]{1,0:T(8,128)(2,1)S(1)}, u32[]{:S(2)}, u32[]{:S(2)}) collective-permute-start(bf16[8,6272]{1,0:T(8,128)(2,1)S(1)} %slice.55), channel_id=1, source_target_pairs={{0,4},{1,5},{2,6},{3,7},{4,0},{5,1},{6,2},{7,3},{8,12},{9,13},{10,... | collective-permute-start | bytes 301064 | tf_op jit(solution)/shard_map/ppermute | solution.py:283
  104.1 10.6 %collective-permute-start.27 = (bf16[8,6272]{1,0:T(8,128)(2,1)S(1)}, bf16[8,6272]{1,0:T(8,128)(2,1)S(1)}, u32[]{:S(2)}, u32[]{:S(2)}) collective-permute-start(bf16[8,6272]{1,0:T(8,128)(2,1)S(1)} %slice.54), channel_id=1, source_target_pairs={{0,4},{1,5},{2,6},{3,7},{4,0},{5,1},{6,2},{7,3},{8,12},{9,13},{10,... | collective-permute-start | bytes 301064 | tf_op jit(solution)/shard_map/ppermute | solution.py:283

commit v3 on v2

--- a/solution.py
+++ b/solution.py
@@ -1,5 +1,3 @@
-import numpy as np
-
 import jax
 import jax.numpy as jnp
 from jax import lax
@@ -46,20 +44,22 @@
 
 
 def selectors():
-    pair_all, coef_all, pair_tile, coef_tile = [np.full(ROT_PAD, -1, np.int32) for _ in range(4)]
+    row = lax.broadcasted_iota(jnp.int32, (8, ROT_PAD), 1)
+    pair_all, coef_all, pair_tile, coef_tile = [jnp.full(row.shape, -1, jnp.int32) for _ in range(4)]
     offset = 0
     for degree in range(TOP + 1):
-        cap = min(degree, 2)
+        cap, columns = min(degree, 2), 2 * degree + 1
         [(first, _, pairs, start)] = [e for e, d in zip(TABLE, TILES) if degree in d]
         for order in range(-cap, cap + 1):
             place = pairs.index((degree, order))
-            for column in range(2 * degree + 1):
-                row = offset + (order + cap) * (2 * degree + 1) + column
-                coef = degree * degree + column
-                pair_all[row], coef_all[row] = start // GROUP + place, coef
-                pair_tile[row], coef_tile[row] = place, coef - first
-        offset += (2 * cap + 1) * (2 * degree + 1)
-    return pair_all[None, :], coef_all[None, :], pair_tile[:, None], coef_tile[:, None]
+            inside = (row >= offset) & (row < offset + columns)
+            coef = row - offset + degree * degree
+            pair_all = jnp.where(inside, start // GROUP + place, pair_all)
+            coef_all = jnp.where(inside, coef, coef_all)
+            pair_tile = jnp.where(inside, place, pair_tile)
+            coef_tile = jnp.where(inside, coef - first, coef_tile)
+            offset += columns
+    return pair_all[:1], coef_all[:1], pair_tile.astype(F32).T[:, :1], coef_tile.astype(F32).T[:, :1]
 
 
 def dot(a, b):
@@ -74,7 +74,10 @@
     return [(s, min(size, total - s)) for s in range(0, total, size)]
 
 
-def prep_kernel(rot, pair_all, coef_all, pair_tile, coef_tile, turn, back):
+def prep_kernel(rot, turn, back, rows_all):
+    pair_all, coef_all, pair_tile, coef_tile = selectors()
+    rows_all[...] = jnp.zeros_like(rows_all)
+    rows_all[pl.ds(0, ROT_ROWS), :] = rot[...]
     row = lax.broadcasted_iota(jnp.int32, (LANES, 256), 0)
     lane = lax.broadcasted_iota(jnp.int32, (LANES, 256), 1) & (GROUP - 1)
 
@@ -85,10 +88,10 @@
 
     def pick(rows, ids):
         group = lax.broadcasted_iota(jnp.int32, (rows, ROT_PAD), 0) // GROUP
-        return (group == ids[...]).astype(F32).astype(BF16)
+        return (group == ids).astype(F32).astype(BF16)
 
     def mask(ids):
-        return lax.broadcasted_iota(jnp.int32, (ROT_PAD, 256), 1) // GROUP == ids[...]
+        return lax.broadcasted_iota(jnp.int32, (ROT_PAD, 256), 1) // GROUP == ids.astype(jnp.int32)
 
     work = (
         (mask(coef_tile), pick(TURN_ROWS, pair_all), keep(TURN_ROWS), turn),
@@ -96,7 +99,7 @@
     )
     for g in range(LANES // GROUP):
         spread = (row == lane + GROUP * g).astype(F32).astype(BF16)
-        laid = dot(rot[...], spread)
+        laid = dot(rows_all[...], spread)
         for masked, picked, kept, out in work:
             full = dot(picked, jnp.where(masked, laid, 0.0).astype(BF16))
             out[g] = jnp.where(kept, full, 0.0).astype(BF16)
@@ -310,18 +313,15 @@
     turn, back = kernel_call(
         prep_kernel,
         (shaped(groups, TURN_ROWS, 256), shaped(groups, BACK_ROWS, 256)),
-        [],
+        [pltpu.VMEM((ROT_PAD, LANES), BF16)],
         2 * 10**9,
         6 * 10**6,
-    )(
-        jnp.pad(rotations, ((0, ROT_PAD - ROT_ROWS), (0, 0))),
-        *[jnp.asarray(ids) for ids in selectors()],
-    )
+    )(rotations)
 
     flat = embeddings.reshape(atoms, WIDE)
-    beyond, turn, back = after(across(flat), turn, back)
+    beyond, back = after(across(flat), back)
     pair = jnp.concatenate([flat, beyond], axis=0)
-    pair, species, upstream, targets = after(pair, species, cotangent, targets)
+    pair, species, cot, targets = after(pair, species, cotangent, targets)
     far_pair = swap_far(pair)
     own_pieces = spread(pair)
     gain = jnp.dot(
@@ -329,13 +329,15 @@
         species_gain,
         precision=lax.Precision.HIGHEST,
     )
-    upstream = (upstream.astype(F32) * gain[:, None, :] * scale).astype(BF16).reshape(atoms, WIDE)
-    up_pair = jnp.concatenate([upstream, across(upstream)], axis=0)
-    *own_pieces, send_left, send_right, sources = after(*own_pieces, send_left, send_right, sources)
+    upstream = (cot.astype(F32) * gain[:, None, :] * scale).astype(BF16).reshape(atoms, WIDE)
+    far_pair, upstream, send_left, send_right, sources = after(
+        far_pair, upstream, send_left, send_right, sources
+    )
+    far_pieces = spread(far_pair)
     own_table = jnp.concatenate(own_pieces, axis=0)
     partner_table = swap_near(own_table)
-    far_pieces = spread(far_pair)
-    *far_pieces, up_pair = after(*far_pieces, up_pair)
+    *far_pieces, up_far = after(*far_pieces, across(upstream))
+    up_pair = jnp.concatenate([upstream, up_far], axis=0)
     up_pieces = spread(up_pair)
 
     def slot(atom):
@@ -394,12 +396,13 @@
     )(*up_pieces, tgt_col, src_row, turn, back, turned, outs, pre, weight_radial, *weights)
 
     *far_grads, near_grad, agg_pair = after(*far_grads, near_grad, agg_pair)
+    near_home, agg_far = after(swap_near(near_grad), across(agg_pair[atoms:].astype(BF16)))
     far_home = swap_far(collect(far_grads).astype(BF16)).astype(F32)
-    aggregate = agg_pair[:atoms] + across(agg_pair[atoms:].astype(BF16)).astype(F32)
+    aggregate = agg_pair[:atoms] + agg_far.astype(F32)
     updated = (
         embeddings.astype(F32) + gain[:, None, :] * scale * aggregate.reshape(embeddings.shape)
     ).astype(BF16)
-    summed = own_grad.astype(F32) + swap_near(near_grad).astype(F32)
+    summed = own_grad.astype(F32) + near_home.astype(F32)
     parts = [summed[2 * atoms * d : 2 * atoms * (d + 1)].astype(BF16) for d in range(4)]
     grad_pair = collect(parts) + far_home
     grad_rows = grad_pair[:atoms] + across(grad_pair[atoms:].astype(BF16)).astype(F32)

time: 116 us -> 111 us (0.957)
  the two profiles are of different devices: /device:TPU:24 before, /device:TPU:8 now
where the time goes in v3:
time: 111 us; the launch traced here: 110 us
  starting transfers between devices  51.6 us (46%)
  waiting for transfers between devices  29.2 us (26%)
  Pallas kernels  22.6 us (20%)
  local copies, waits for them, and re-layouts  2.55 us (2%)
  other arithmetic  2.26 us (2%)
  between operations  1.54 us (1%)
    ppermute x18, starting transfers between devices, shift(): lax.ppermute(v, 'edge', [(s, s // 4 * 4 + (s + k) % 4) for s in range(8)])  26.6 us
    ppermute x4, starting transfers between devices, across(): return lax.ppermute(v, 'edge', [(s, (s + 4) % 8) for s in range(8)])  18.2 us
    ppermute x18, waiting for transfers between devices, shift(): lax.ppermute(v, 'edge', [(s, s // 4 * 4 + (s + k) % 4) for s in range(8)])  14.2 us
    ppermute x4, waiting for transfers between devices, across(): return lax.ppermute(v, 'edge', [(s, (s + 4) % 8) for s in range(8)])  10 us
    pallas_call x1, Pallas kernels, on_device(): kernel_call(backward_kernel, (whole, whole, piece, piece, piece, piece, s...  9.86 us
    pallas_call x1, Pallas kernels, on_device(): kernel_call(forward_kernel, (piece, piece, piece, piece, kept, kept, squa...  8.18 us
    ppermute x2, starting transfers between devices, swap_far(): lax.ppermute(v, 'space', [(b, (b + 2 * (b % 2) - 1) % blocks) for b in ra...  4.67 us
    pallas_call x1, Pallas kernels, on_device(): kernel_call(prep_kernel, (shaped(groups, TURN_ROWS, 256), shaped(groups,...  4.57 us
  transfers between devices with their start and end apart: 28, of which 11 were waited for; matrix products, arithmetic and copies ran while one was open for 2% of the time, Pallas kernels for 21%

profile of v3, /device:TPU:8, one launch (start us, length us, event | category | flops | bytes accessed | tf_op | source)
XLA Modules:
  0.0 109.9 jit_solution(14175809418763043593)
XLA Ops:
  0.6 0.0 copy-start
  0.6 7.3 %collective-permute-start = (bf16[8,6272]{1,0:T(8,128)(2,1)}, bf16[8,6272]{1,0:T(8,128)(2,1)S(1)}, u32[]{:S(2)}, u32[]{:S(2)}) collective-permute-start(bf16[8,6272]{1,0:T(8,128)(2,1)} %bitcast.27), channel_id=1, source_target_pairs={{0,4},{1,5},{2,6},{3,7},{4,0},{5,1},{6,2},{7,3},{8,12},{9,13},{10,... | collective-permute-start | bytes 301064 | tf_op jit(solution)/shard_map/ppermute | solution.py:286
  8.6 0.8 copy-done.1
  9.4 4.6 %shard_map.184 = (bf16[8,464,256]{2,1,0:T(8,128)(2,1)S(1)}, bf16[8,784,256]{2,1,0:T(8,128)(2,1)}) custom-call(bf16[235,128]{1,0:T(8,128)(2,1)S(1)} %copy-done.1), custom_call_target="tpu_custom_call" | custom-call | flops 2000000000 | bytes 6000000 | tf_op jit(solution)/shard_map/pallas_call | solution.py:313
  14.0 1.3 %copy-done.4 = bf16[8,464,256]{2,1,0:T(8,128)(2,1)} copy-done((bf16[8,464,256]{2,1,0:T(8,128)(2,1)}, bf16[8,464,256]{2,1,0:T(8,128)(2,1)S(1)}, u32[]{:S(2)}) %copy-start.4) | copy-done | bytes 1900568
  15.3 0.0 collective-permute-done
  15.4 1.1 collective-permute-start.1
  16.4 2.8 %collective-permute-start.11 = (bf16[16,6272]{1,0:T(8,128)(2,1)S(1)}, bf16[16,6272]{1,0:T(8,128)(2,1)S(1)}, u32[]{:S(2)}, u32[]{:S(2)}) collective-permute-start(bf16[16,6272]{1,0:T(8,128)(2,1)S(1)} %pad_maximum_fusion), channel_id=1, source_target_pairs={{0,3},{1,0},{2,1},{3,2},{4,7},{5,4},{6,5},{7,6},{8,11},{9,8},{10,9... | collective-permute-start | bytes 602120 | tf_op jit(solution)/shard_map/ppermute | solution.py:289
  19.3 0.8 collective-permute-start.12
  20.1 0.9 collective-permute-start.13
  21.0 0.1 copy.23.tgt
  21.1 0.2 broadcast_multiply_fusion
  21.4 1.9 %collective-permute-done.1.far0 = bf16[16,6272]{1,0:T(8,128)(2,1)S(1)} collective-permute-done((bf16[16,6272]{1,0:T(8,128)(2,1)S(1)}, bf16[16,6272]{1,0:T(8,128)(2,1)S(1)}, u32[]{:S(2)}, u32[]{:S(2)}) %collective-permute-start.1) | collective-permute-done | bytes 200736 | tf_op jit(solution)/shard_map/ppermute | solution.py:295
  23.3 2.8 %collective-permute-start.2 = (bf16[16,6272]{1,0:T(8,128)(2,1)S(1)}, bf16[16,6272]{1,0:T(8,128)(2,1)S(1)}, u32[]{:S(2)}, u32[]{:S(2)}) collective-permute-start(bf16[16,6272]{1,0:T(8,128)(2,1)S(1)} %collective-permute-done.1.far0), channel_id=1, source_target_pairs={{0,3},{1,0},{2,1},{3,2},{4,7},{5,4},{6,5},{7,6},{8,11},{9,8},{10,9... | collective-permute-start | bytes 602120 | tf_op jit(solution)/shard_map/ppermute | solution.py:289
  26.0 0.8 collective-permute-start.3
  26.8 1.9 %collective-permute-done.11 = bf16[16,6272]{1,0:T(8,128)(2,1)S(1)} collective-permute-done((bf16[16,6272]{1,0:T(8,128)(2,1)S(1)}, bf16[16,6272]{1,0:T(8,128)(2,1)S(1)}, u32[]{:S(2)}, u32[]{:S(2)}) %collective-permute-start.11) | collective-permute-done | bytes 200736 | tf_op jit(solution)/shard_map/ppermute | solution.py:289
  28.8 0.0 collective-permute-start.4
  28.8 0.0 collective-permute-done.12
  28.8 2.1 %collective-permute-start.10 = (s32[1,32]{1,0:T(1,128)S(1)}, s32[1,32]{1,0:T(1,128)S(1)}, u32[]{:S(2)}, u32[]{:S(2)}) collective-permute-start(s32[1,32]{1,0:T(1,128)S(1)} %copy-done.10), channel_id=1, source_target_pairs={{0,248},{8,0},{16,8},{24,16},{32,24},{40,32},{48,40},{56,48},{64,5... | collective-permute-start | bytes 392 | tf_op jit(solution)/shard_map/ppermute | solution.py:298
  30.9 2.1 %collective-permute-done.13 = bf16[16,6272]{1,0:T(8,128)(2,1)S(1)} collective-permute-done((bf16[16,6272]{1,0:T(8,128)(2,1)S(1)}, bf16[16,6272]{1,0:T(8,128)(2,1)S(1)}, u32[]{:S(2)}, u32[]{:S(2)}) %collective-permute-start.13) | collective-permute-done | bytes 200736 | tf_op jit(solution)/shard_map/ppermute | solution.py:289
  33.1 0.0 collective-permute-done.10
  33.1 2.6 %collective-permute-start.5 = (bf16[8,6272]{1,0:T(8,128)(2,1)S(1)}, bf16[8,6272]{1,0:T(8,128)(2,1)S(1)}, u32[]{:S(2)}, u32[]{:S(2)}) collective-permute-start(bf16[8,6272]{1,0:T(8,128)(2,1)S(1)} %fusion.4), channel_id=1, source_target_pairs={{0,4},{1,5},{2,6},{3,7},{4,0},{5,1},{6,2},{7,3},{8,12},{9,13},{10,... | collective-permute-start | bytes 301064 | tf_op jit(solution)/shard_map/ppermute | solution.py:286
  35.7 3.0 %collective-permute-done.9 = s32[1,32]{1,0:T(1,128)S(1)} collective-permute-done((s32[1,32]{1,0:T(1,128)S(1)}, s32[1,32]{1,0:T(1,128)S(1)}, u32[]{:S(2)}, u32[]{:S(2)}) %collective-permute-start.9) | collective-permute-done | bytes 160 | tf_op jit(solution)/shard_map/ppermute | solution.py:298
  38.7 0.1 add_bitcast_fusion
  38.8 0.1 select_reduce_fusion
  38.9 0.1 copy.22.src
  39.1 4.1 %collective-permute-done.5 = bf16[8,6272]{1,0:T(8,128)(2,1)S(1)} collective-permute-done((bf16[8,6272]{1,0:T(8,128)(2,1)S(1)}, bf16[8,6272]{1,0:T(8,128)(2,1)S(1)}, u32[]{:S(2)}, u32[]{:S(2)}) %collective-permute-start.5) | collective-permute-done | bytes 100384 | tf_op jit(solution)/shard_map/ppermute | solution.py:286
  43.1 0.0 collective-permute-done.2.far1
  43.1 0.0 collective-permute-done.3.far2
  43.1 0.0 collective-permute-done.4.far3
  43.2 2.4 %collective-permute-start.6 = (bf16[16,6272]{1,0:T(8,128)(2,1)S(1)}, bf16[16,6272]{1,0:T(8,128)(2,1)S(1)}, u32[]{:S(2)}, u32[]{:S(2)}) collective-permute-start(bf16[16,6272]{1,0:T(8,128)(2,1)S(1)} %constant_dynamic-update-slice_fusion.up0), channel_id=1, source_target_pairs={{0,3},{1,0},{2,1},{3,2},{4,7},{5,4},{6,5},{7,6},{8,11},{9,8},{10,9... | collective-permute-start | bytes 602120 | tf_op jit(solution)/shard_map/ppermute | solution.py:289
  45.5 1.8 %collective-permute-start.7 = (bf16[16,6272]{1,0:T(8,128)(2,1)S(1)}, bf16[16,6272]{1,0:T(8,128)(2,1)S(1)}, u32[]{:S(2)}, u32[]{:S(2)}) collective-permute-start(bf16[16,6272]{1,0:T(8,128)(2,1)S(1)} %constant_dynamic-update-slice_fusion.up0), channel_id=1, source_target_pairs={{0,2},{1,3},{2,0},{3,1},{4,6},{5,7},{6,4},{7,5},{8,10},{9,11},{10,... | collective-permute-start | bytes 602120 | tf_op jit(solution)/shard_map/ppermute | solution.py:289
  47.3 1.1 %collective-permute-start.8 = (bf16[16,6272]{1,0:T(8,128)(2,1)S(1)}, bf16[16,6272]{1,0:T(8,128)(2,1)S(1)}, u32[]{:S(2)}, u32[]{:S(2)}) collective-permute-start(bf16[16,6272]{1,0:T(8,128)(2,1)S(1)} %constant_dynamic-update-slice_fusion.up0), channel_id=1, source_target_pairs={{0,1},{1,2},{2,3},{3,0},{4,5},{5,6},{6,7},{7,4},{8,9},{9,10},{10,1... | collective-permute-start | bytes 602120 | tf_op jit(solution)/shard_map/ppermute | solution.py:289
  48.5 8.2 %shard_map.185 = (bf16[16,6272]{1,0:T(8,128)(2,1)S(1)}, bf16[16,6272]{1,0:T(8,128)(2,1)S(1)}, bf16[16,6272]{1,0:T(8,128)(2,1)S(1)}, bf16[16,6272]{1,0:T(8,128)(2...) custom-call(bf16[64,6272]{1,0:T(8,128)(2,1)S(1)} %constant_dynamic-update-slice_fusion.2.own, ...), custom_call_target="tpu_custom_call" | custom-call | flops 4000000000 | bytes 20000000 | tf_op jit(solution)/shard_map/pallas_call | solution.py:376
  56.6 0.6 collective-permute-start.15
  57.2 3.0 %collective-permute-start.16 = (bf16[16,6272]{1,0:T(8,128)(2,1)S(1)}, bf16[16,6272]{1,0:T(8,128)(2,1)S(1)}, u32[]{:S(2)}, u32[]{:S(2)}) collective-permute-start(bf16[16,6272]{1,0:T(8,128)(2,1)S(1)} %get-tuple-element.71), channel_id=1, source_target_pairs={{0,2},{1,3},{2,0},{3,1},{4,6},{5,7},{6,4},{7,5},{8,10},{9,11},{10,... | collective-permute-start | bytes 602120 | tf_op jit(solution)/shard_map/ppermute | solution.py:289
  60.2 0.0 collective-permute-start.17
  60.3 0.0 collective-permute-done.8.up3
  60.3 9.9 %shard_map.186 = (bf16[64,6272]{1,0:T(8,128)(2,1)S(1)}, bf16[64,6272]{1,0:T(8,128)(2,1)S(1)}, bf16[16,6272]{1,0:T(8,128)(2,1)S(1)}, bf16[16,6272]{1,0:T(8,128)(2...) custom-call(bf16[16,6272]{1,0:T(8,128)(2,1)S(1)} %constant_dynamic-update-slice_fusion.up0, ...), custom_call_target="tpu_custom_call" | custom-call | flops 5000000000 | bytes 20000000 | tf_op jit(solution)/shard_map/pallas_call | solution.py:385
  70.1 0.0 collective-permute-done.15
  70.1 0.0 collective-permute-done.16
  70.2 0.1 convert_add_fusion.1
  70.3 2.1 %collective-permute-start.23 = (bf16[16,6272]{1,0:T(8,128)(2,1)S(1)}, bf16[16,6272]{1,0:T(8,128)(2,1)S(1)}, u32[]{:S(2)}, u32[]{:S(2)}) collective-permute-start(bf16[16,6272]{1,0:T(8,128)(2,1)S(1)} %get-tuple-element.79), channel_id=1, source_target_pairs={{0,1},{1,2},{2,3},{3,0},{4,5},{5,6},{6,7},{7,4},{8,9},{9,10},{10,1... | collective-permute-start | bytes 602120 | tf_op jit(solution)/shard_map/ppermute | solution.py:289
  72.3 0.7 collective-permute-start.24
  73.0 2.5 %collective-permute-start.25 = (bf16[16,6272]{1,0:T(8,128)(2,1)S(1)}, bf16[16,6272]{1,0:T(8,128)(2,1)S(1)}, u32[]{:S(2)}, u32[]{:S(2)}) collective-permute-start(bf16[16,6272]{1,0:T(8,128)(2,1)S(1)} %get-tuple-element.81), channel_id=1, source_target_pairs={{0,3},{1,0},{2,1},{3,2},{4,7},{5,4},{6,5},{7,6},{8,11},{9,8},{10,9... | collective-permute-start | bytes 602120 | tf_op jit(solution)/shard_map/ppermute | solution.py:289
  75.5 0.0 collective-permute-start.18
  75.5 4.0 %collective-permute-start.19 = (bf16[8,6272]{1,0:T(8,128)(2,1)S(1)}, bf16[8,6272]{1,0:T(8,128)(2,1)S(1)}, u32[]{:S(2)}, u32[]{:S(2)}) collective-permute-start(bf16[8,6272]{1,0:T(8,128)(2,1)S(1)} %slice.55), channel_id=1, source_target_pairs={{0,4},{1,5},{2,6},{3,7},{4,0},{5,1},{6,2},{7,3},{8,12},{9,13},{10,... | collective-permute-start | bytes 301064 | tf_op jit(solution)/shard_map/ppermute | solution.py:286
  79.5 0.8 collective-permute-done.23
  80.3 0.0 collective-permute-done.24
  80.3 0.6 collective-permute-done.25
  80.9 0.1 add_convert_fusion.1
  81.0 3.6 %collective-permute-start.26 = (bf16[16,6272]{1,0:T(8,128)(2,1)S(1)}, bf16[16,6272]{1,0:T(8,128)(2,1)S(1)}, u32[]{:S(2)}, u32[]{:S(2)}) collective-permute-start(bf16[16,6272]{1,0:T(8,128)(2,1)S(1)} %add_convert_fusion.1), channel_id=1, source_target_pairs={{0,248},{8,16},{16,8},{24,32},{32,24},{40,48},{48,40},{56,64},{64,... | collective-permute-start | bytes 602120 | tf_op jit(solution)/shard_map/ppermute | solution.py:295
  84.6 1.2 %collective-permute-done.19 = bf16[8,6272]{1,0:T(8,128)(2,1)S(1)} collective-permute-done((bf16[8,6272]{1,0:T(8,128)(2,1)S(1)}, bf16[8,6272]{1,0:T(8,128)(2,1)S(1)}, u32[]{:S(2)}, u32[]{:S(2)}) %collective-permute-start.19) | collective-permute-done | bytes 100384 | tf_op jit(solution)/shard_map/ppermute | solution.py:286
  85.8 0.2 add_convert_fusion
  86.1 0.1 collective-permute-start.20
  86.2 4.0 %collective-permute-start.21 = (bf16[16,6272]{1,0:T(8,128)(2,1)S(1)}, bf16[16,6272]{1,0:T(8,128)(2,1)S(1)}, u32[]{:S(2)}, u32[]{:S(2)}) collective-permute-start(bf16[16,6272]{1,0:T(8,128)(2,1)S(1)} %get-tuple-element.85), channel_id=1, source_target_pairs={{0,2},{1,3},{2,0},{3,1},{4,6},{5,7},{6,4},{7,5},{8,10},{9,11},{10,... | collective-permute-start | bytes 602120 | tf_op jit(solution)/shard_map/ppermute | solution.py:289
  90.1 0.3 collective-permute-start.22
  90.5 8.2 %collective-permute-done.20 = bf16[16,6272]{1,0:T(8,128)(2,1)S(1)} collective-permute-done((bf16[16,6272]{1,0:T(8,128)(2,1)S(1)}, bf16[16,6272]{1,0:T(8,128)(2,1)S(1)}, u32[]{:S(2)}, u32[]{:S(2)}) %collective-permute-start.20) | collective-permute-done | bytes 200736 | tf_op jit(solution)/shard_map/ppermute | solution.py:289
  98.6 0.6 collective-permute-done.22
  99.2 0.1 convert_add_fusion
  99.4 4.4 %collective-permute-start.27 = (bf16[8,6272]{1,0:T(8,128)(2,1)S(1)}, bf16[8,6272]{1,0:T(8,128)(2,1)S(1)}, u32[]{:S(2)}, u32[]{:S(2)}) collective-permute-start(bf16[8,6272]{1,0:T(8,128)(2,1)S(1)} %slice.54), channel_id=1, source_target_pairs={{0,4},{1,5},{2,6},{3,7},{4,0},{5,1},{6,2},{7,3},{8,12},{9,13},{10,... | collective-permute-start | bytes 301064 | tf_op jit(solution)/shard_map/ppermute | solution.py:286
  103.8 0.7 fusion.3
  104.4 4.8 %collective-permute-done.27 = bf16[8,6272]{1,0:T(8,128)(2,1)S(1)} collective-permute-done((bf16[8,6272]{1,0:T(8,128)(2,1)S(1)}, bf16[8,6272]{1,0:T(8,128)(2,1)S(1)}, u32[]{:S(2)}, u32[]{:S(2)}) %collective-permute-start.27) | collective-permute-done | bytes 100384 | tf_op jit(solution)/shard_map/ppermute | solution.py:286
  109.2 0.7 fusion.1
  (45 shorter events, 0.4 us)
Async XLA Ops:
  0.6 20.5 %copy-start = (f32[100,128]{1,0:T(8,128)S(1)}, f32[100,128]{1,0:T(8,128)}, u32[]{:S(2)}) copy-start(f32[100,128]{1,0:T(8,128)} %param.19) | copy-start | bytes 153604
  0.6 14.7 %collective-permute-start = (bf16[8,6272]{1,0:T(8,128)(2,1)}, bf16[8,6272]{1,0:T(8,128)(2,1)S(1)}, u32[]{:S(2)}, u32[]{:S(2)}) collective-permute-start(bf16[8,6272]{1,0:T(8,128)(2,1)} %bitcast.27), channel_id=1, source_target_pairs={{0,4},{1,5},{2,6},{3,7},{4,0},{5,1},{6,2},{7,3},{8,12},{9,13},{10,... | collective-permute-start | bytes 301064 | tf_op jit(solution)/shard_map/ppermute | solution.py:286
  8.6 0.8 copy-start.1
  9.4 5.9 %copy-start.6 = (bf16[8,49,128]{2,0,1:T(8,128)(2,1)S(1)}, bf16[8,49,128]{2,0,1:T(8,128)(2,1)}, u32[]{:S(2)}) copy-start(bf16[8,49,128]{2,0,1:T(8,128)(2,1)} %param.17) | copy-start | bytes 301060
  9.4 11.5 %copy-start.7 = (s32[128]{0:T(128)S(1)}, s32[128]{0:T(128)}, u32[]{:S(2)}) copy-start(s32[128]{0:T(128)} %param.21) | copy-start | bytes 1540
  9.4 11.7 %copy-start.9 = (s32[8]{0:T(128)S(1)}, s32[8]{0:T(128)}, u32[]{:S(2)}) copy-start(s32[8]{0:T(128)} %param.18) | copy-start | bytes 100
  9.4 11.9 %copy-start.5 = (bf16[8,49,128]{2,0,1:T(8,128)(2,1)S(1)}, bf16[8,49,128]{2,0,1:T(8,128)(2,1)}, u32[]{:S(2)}) copy-start(bf16[8,49,128]{2,0,1:T(8,128)(2,1)} %param.33) | copy-start | bytes 301060
  9.4 19.4 %copy-start.10 = (s32[1,32]{1,0:T(1,128)S(1)}, s32[1,32]{1,0:T(1,128)}, u32[]{:S(2)}) copy-start(s32[1,32]{1,0:T(1,128)} %param.23) | copy-start | bytes 388
  14.0 1.3 %copy-start.4 = (bf16[8,464,256]{2,1,0:T(8,128)(2,1)}, bf16[8,464,256]{2,1,0:T(8,128)(2,1)S(1)}, u32[]{:S(2)}) copy-start(bf16[8,464,256]{2,1,0:T(8,128)(2,1)S(1)} %get-tuple-element.55.turn) | copy-start | bytes 5701636
  15.3 17.8 %copy-start.11 = (s32[1,32]{1,0:T(1,128)S(1)}, s32[1,32]{1,0:T(1,128)}, u32[]{:S(2)}) copy-start(s32[1,32]{1,0:T(1,128)} %param.24) | copy-start | bytes 388
  15.3 17.8 %copy-start.8 = (s32[128]{0:T(128)S(1)}, s32[128]{0:T(128)}, u32[]{:S(2)}) copy-start(s32[128]{0:T(128)} %param.20) | copy-start | bytes 1540
  15.3 33.1 %copy-start.2 = (bf16[128,128]{1,0:T(8,128)(2,1)S(1)}, bf16[128,128]{1,0:T(8,128)(2,1)}, u32[]{:S(2)}) copy-start(bf16[128,128]{1,0:T(8,128)(2,1)} %basis.1) | copy-start | bytes 98308
  15.3 33.1 %copy-start.3 = (bf16[128,128]{1,0:T(8,128)(2,1)S(1)}, bf16[128,128]{1,0:T(8,128)(2,1)}, u32[]{:S(2)}) copy-start(bf16[128,128]{1,0:T(8,128)(2,1)} %w_rad.3) | copy-start | bytes 98308
  15.4 7.9 %collective-permute-start.1 = (bf16[16,6272]{1,0:T(8,128)(2,1)S(1)}, bf16[16,6272]{1,0:T(8,128)(2,1)S(1)}, u32[]{:S(2)}, u32[]{:S(2)}) collective-permute-start(bf16[16,6272]{1,0:T(8,128)(2,1)S(1)} %pad_maximum_fusion), channel_id=1, source_target_pairs={{0,248},{8,16},{16,8},{24,32},{32,24},{40,48},{48,40},{56,64},{64,... | collective-permute-start | bytes 602120 | tf_op jit(solution)/shard_map/ppermute | solution.py:295
  16.4 12.3 %collective-permute-start.11 = (bf16[16,6272]{1,0:T(8,128)(2,1)S(1)}, bf16[16,6272]{1,0:T(8,128)(2,1)S(1)}, u32[]{:S(2)}, u32[]{:S(2)}) collective-permute-start(bf16[16,6272]{1,0:T(8,128)(2,1)S(1)} %pad_maximum_fusion), channel_id=1, source_target_pairs={{0,3},{1,0},{2,1},{3,2},{4,7},{5,4},{6,5},{7,6},{8,11},{9,8},{10,9... | collective-permute-start | bytes 602120 | tf_op jit(solution)/shard_map/ppermute | solution.py:289
  19.3 9.5 %collective-permute-start.12 = (bf16[16,6272]{1,0:T(8,128)(2,1)S(1)}, bf16[16,6272]{1,0:T(8,128)(2,1)S(1)}, u32[]{:S(2)}, u32[]{:S(2)}) collective-permute-start(bf16[16,6272]{1,0:T(8,128)(2,1)S(1)} %pad_maximum_fusion), channel_id=1, source_target_pairs={{0,2},{1,3},{2,0},{3,1},{4,6},{5,7},{6,4},{7,5},{8,10},{9,11},{10,... | collective-permute-start | bytes 602120 | tf_op jit(solution)/shard_map/ppermute | solution.py:289
  20.1 13.0 %collective-permute-start.13 = (bf16[16,6272]{1,0:T(8,128)(2,1)S(1)}, bf16[16,6272]{1,0:T(8,128)(2,1)S(1)}, u32[]{:S(2)}, u32[]{:S(2)}) collective-permute-start(bf16[16,6272]{1,0:T(8,128)(2,1)S(1)} %pad_maximum_fusion), channel_id=1, source_target_pairs={{0,1},{1,2},{2,3},{3,0},{4,5},{5,6},{6,7},{7,4},{8,9},{9,10},{10,1... | collective-permute-start | bytes 602120 | tf_op jit(solution)/shard_map/ppermute | solution.py:289
  23.3 19.9 %collective-permute-start.2 = (bf16[16,6272]{1,0:T(8,128)(2,1)S(1)}, bf16[16,6272]{1,0:T(8,128)(2,1)S(1)}, u32[]{:S(2)}, u32[]{:S(2)}) collective-permute-start(bf16[16,6272]{1,0:T(8,128)(2,1)S(1)} %collective-permute-done.1.far0), channel_id=1, source_target_pairs={{0,3},{1,0},{2,1},{3,2},{4,7},{5,4},{6,5},{7,6},{8,11},{9,8},{10,9... | collective-permute-start | bytes 602120 | tf_op jit(solution)/shard_map/ppermute | solution.py:289
  26.0 17.1 %collective-permute-start.3 = (bf16[16,6272]{1,0:T(8,128)(2,1)S(1)}, bf16[16,6272]{1,0:T(8,128)(2,1)S(1)}, u32[]{:S(2)}, u32[]{:S(2)}) collective-permute-start(bf16[16,6272]{1,0:T(8,128)(2,1)S(1)} %collective-permute-done.1.far0), channel_id=1, source_target_pairs={{0,2},{1,3},{2,0},{3,1},{4,6},{5,7},{6,4},{7,5},{8,10},{9,11},{10,... | collective-permute-start | bytes 602120 | tf_op jit(solution)/shard_map/ppermute | solution.py:289
  28.8 14.4 %collective-permute-start.4 = (bf16[16,6272]{1,0:T(8,128)(2,1)S(1)}, bf16[16,6272]{1,0:T(8,128)(2,1)S(1)}, u32[]{:S(2)}, u32[]{:S(2)}) collective-permute-start(bf16[16,6272]{1,0:T(8,128)(2,1)S(1)} %collective-permute-done.1.far0), channel_id=1, source_target_pairs={{0,1},{1,2},{2,3},{3,0},{4,5},{5,6},{6,7},{7,4},{8,9},{9,10},{10,1... | collective-permute-start | bytes 602120 | tf_op jit(solution)/shard_map/ppermute | solution.py:289
  28.8 4.3 %collective-permute-start.10 = (s32[1,32]{1,0:T(1,128)S(1)}, s32[1,32]{1,0:T(1,128)S(1)}, u32[]{:S(2)}, u32[]{:S(2)}) collective-permute-start(s32[1,32]{1,0:T(1,128)S(1)} %copy-done.10), channel_id=1, source_target_pairs={{0,248},{8,0},{16,8},{24,16},{32,24},{40,32},{48,40},{56,48},{64,5... | collective-permute-start | bytes 392 | tf_op jit(solution)/shard_map/ppermute | solution.py:298
  33.1 5.7 %collective-permute-start.9 = (s32[1,32]{1,0:T(1,128)S(1)}, s32[1,32]{1,0:T(1,128)S(1)}, u32[]{:S(2)}, u32[]{:S(2)}) collective-permute-start(s32[1,32]{1,0:T(1,128)S(1)} %copy-done.11), channel_id=1, source_target_pairs={{0,8},{8,16},{16,24},{24,32},{32,40},{40,48},{48,56},{56,64},{64,7... | collective-permute-start | bytes 392 | tf_op jit(solution)/shard_map/ppermute | solution.py:298
  33.1 10.0 %collective-permute-start.5 = (bf16[8,6272]{1,0:T(8,128)(2,1)S(1)}, bf16[8,6272]{1,0:T(8,128)(2,1)S(1)}, u32[]{:S(2)}, u32[]{:S(2)}) collective-permute-start(bf16[8,6272]{1,0:T(8,128)(2,1)S(1)} %fusion.4), channel_id=1, source_target_pairs={{0,4},{1,5},{2,6},{3,7},{4,0},{5,1},{6,2},{7,3},{8,12},{9,13},{10,... | collective-permute-start | bytes 301064 | tf_op jit(solution)/shard_map/ppermute | solution.py:286
  38.7 9.7 %collective-permute-start.14 = (bf16[64,6272]{1,0:T(8,128)(2,1)S(1)}, bf16[64,6272]{1,0:T(8,128)(2,1)S(1)}, u32[]{:S(2)}, u32[]{:S(2)}) collective-permute-start(bf16[64,6272]{1,0:T(8,128)(2,1)S(1)} %constant_dynamic-update-slice_fusion.2.own), channel_id=1, source_target_pairs={{0,8},{8,0},{16,24},{24,16},{32,40},{40,32},{48,56},{56,48},{64,72... | collective-permute-start | bytes 2408456 | tf_op jit(solution)/shard_map/ppermute | solution.py:292
  43.2 17.1 %collective-permute-start.6 = (bf16[16,6272]{1,0:T(8,128)(2,1)S(1)}, bf16[16,6272]{1,0:T(8,128)(2,1)S(1)}, u32[]{:S(2)}, u32[]{:S(2)}) collective-permute-start(bf16[16,6272]{1,0:T(8,128)(2,1)S(1)} %constant_dynamic-update-slice_fusion.up0), channel_id=1, source_target_pairs={{0,3},{1,0},{2,1},{3,2},{4,7},{5,4},{6,5},{7,6},{8,11},{9,8},{10,9... | collective-permute-start | bytes 602120 | tf_op jit(solution)/shard_map/ppermute | solution.py:289
  45.5 14.7 %collective-permute-start.7 = (bf16[16,6272]{1,0:T(8,128)(2,1)S(1)}, bf16[16,6272]{1,0:T(8,128)(2,1)S(1)}, u32[]{:S(2)}, u32[]{:S(2)}) collective-permute-start(bf16[16,6272]{1,0:T(8,128)(2,1)S(1)} %constant_dynamic-update-slice_fusion.up0), channel_id=1, source_target_pairs={{0,2},{1,3},{2,0},{3,1},{4,6},{5,7},{6,4},{7,5},{8,10},{9,11},{10,... | collective-permute-start | bytes 602120 | tf_op jit(solution)/shard_map/ppermute | solution.py:289
  47.3 13.0 %collective-permute-start.8 = (bf16[16,6272]{1,0:T(8,128)(2,1)S(1)}, bf16[16,6272]{1,0:T(8,128)(2,1)S(1)}, u32[]{:S(2)}, u32[]{:S(2)}) collective-permute-start(bf16[16,6272]{1,0:T(8,128)(2,1)S(1)} %constant_dynamic-update-slice_fusion.up0), channel_id=1, source_target_pairs={{0,1},{1,2},{2,3},{3,0},{4,5},{5,6},{6,7},{7,4},{8,9},{9,10},{10,1... | collective-permute-start | bytes 602120 | tf_op jit(solution)/shard_map/ppermute | solution.py:289
  56.6 13.5 %collective-permute-start.15 = (bf16[16,6272]{1,0:T(8,128)(2,1)S(1)}, bf16[16,6272]{1,0:T(8,128)(2,1)S(1)}, u32[]{:S(2)}, u32[]{:S(2)}) collective-permute-start(bf16[16,6272]{1,0:T(8,128)(2,1)S(1)} %get-tuple-element.70), channel_id=1, source_target_pairs={{0,1},{1,2},{2,3},{3,0},{4,5},{5,6},{6,7},{7,4},{8,9},{9,10},{10,1... | collective-permute-start | bytes 602120 | tf_op jit(solution)/shard_map/ppermute | solution.py:289
  57.2 12.9 %collective-permute-start.16 = (bf16[16,6272]{1,0:T(8,128)(2,1)S(1)}, bf16[16,6272]{1,0:T(8,128)(2,1)S(1)}, u32[]{:S(2)}, u32[]{:S(2)}) collective-permute-start(bf16[16,6272]{1,0:T(8,128)(2,1)S(1)} %get-tuple-element.71), channel_id=1, source_target_pairs={{0,2},{1,3},{2,0},{3,1},{4,6},{5,7},{6,4},{7,5},{8,10},{9,11},{10,... | collective-permute-start | bytes 602120 | tf_op jit(solution)/shard_map/ppermute | solution.py:289
  60.2 9.9 %collective-permute-start.17 = (bf16[16,6272]{1,0:T(8,128)(2,1)S(1)}, bf16[16,6272]{1,0:T(8,128)(2,1)S(1)}, u32[]{:S(2)}, u32[]{:S(2)}) collective-permute-start(bf16[16,6272]{1,0:T(8,128)(2,1)S(1)} %get-tuple-element.72), channel_id=1, source_target_pairs={{0,3},{1,0},{2,1},{3,2},{4,7},{5,4},{6,5},{7,6},{8,11},{9,8},{10,9... | collective-permute-start | bytes 602120 | tf_op jit(solution)/shard_map/ppermute | solution.py:289
  70.3 10.1 %collective-permute-start.23 = (bf16[16,6272]{1,0:T(8,128)(2,1)S(1)}, bf16[16,6272]{1,0:T(8,128)(2,1)S(1)}, u32[]{:S(2)}, u32[]{:S(2)}) collective-permute-start(bf16[16,6272]{1,0:T(8,128)(2,1)S(1)} %get-tuple-element.79), channel_id=1, source_target_pairs={{0,1},{1,2},{2,3},{3,0},{4,5},{5,6},{6,7},{7,4},{8,9},{9,10},{10,1... | collective-permute-start | bytes 602120 | tf_op jit(solution)/shard_map/ppermute | solution.py:289
  72.3 8.0 %collective-permute-start.24 = (bf16[16,6272]{1,0:T(8,128)(2,1)S(1)}, bf16[16,6272]{1,0:T(8,128)(2,1)S(1)}, u32[]{:S(2)}, u32[]{:S(2)}) collective-permute-start(bf16[16,6272]{1,0:T(8,128)(2,1)S(1)} %get-tuple-element.80), channel_id=1, source_target_pairs={{0,2},{1,3},{2,0},{3,1},{4,6},{5,7},{6,4},{7,5},{8,10},{9,11},{10,... | collective-permute-start | bytes 602120 | tf_op jit(solution)/shard_map/ppermute | solution.py:289
  73.0 7.9 %collective-permute-start.25 = (bf16[16,6272]{1,0:T(8,128)(2,1)S(1)}, bf16[16,6272]{1,0:T(8,128)(2,1)S(1)}, u32[]{:S(2)}, u32[]{:S(2)}) collective-permute-start(bf16[16,6272]{1,0:T(8,128)(2,1)S(1)} %get-tuple-element.81), channel_id=1, source_target_pairs={{0,3},{1,0},{2,1},{3,2},{4,7},{5,4},{6,5},{7,6},{8,11},{9,8},{10,9... | collective-permute-start | bytes 602120 | tf_op jit(solution)/shard_map/ppermute | solution.py:289
  75.5 10.3 %collective-permute-start.18 = (bf16[64,6272]{1,0:T(8,128)(2,1)S(1)}, bf16[64,6272]{1,0:T(8,128)(2,1)S(1)}, u32[]{:S(2)}, u32[]{:S(2)}) collective-permute-start(bf16[64,6272]{1,0:T(8,128)(2,1)S(1)} %get-tuple-element.74), channel_id=1, source_target_pairs={{0,8},{8,0},{16,24},{24,16},{32,40},{40,32},{48,56},{56,48},{64,72... | collective-permute-start | bytes 2408456 | tf_op jit(solution)/shard_map/ppermute | solution.py:292
  75.5 10.3 %collective-permute-start.19 = (bf16[8,6272]{1,0:T(8,128)(2,1)S(1)}, bf16[8,6272]{1,0:T(8,128)(2,1)S(1)}, u32[]{:S(2)}, u32[]{:S(2)}) collective-permute-start(bf16[8,6272]{1,0:T(8,128)(2,1)S(1)} %slice.55), channel_id=1, source_target_pairs={{0,4},{1,5},{2,6},{3,7},{4,0},{5,1},{6,2},{7,3},{8,12},{9,13},{10,... | collective-permute-start | bytes 301064 | tf_op jit(solution)/shard_map/ppermute | solution.py:286
  81.0 9.4 %collective-permute-start.26 = (bf16[16,6272]{1,0:T(8,128)(2,1)S(1)}, bf16[16,6272]{1,0:T(8,128)(2,1)S(1)}, u32[]{:S(2)}, u32[]{:S(2)}) collective-permute-start(bf16[16,6272]{1,0:T(8,128)(2,1)S(1)} %add_convert_fusion.1), channel_id=1, source_target_pairs={{0,248},{8,16},{16,8},{24,32},{32,24},{40,48},{48,40},{56,64},{64,... | collective-permute-start | bytes 602120 | tf_op jit(solution)/shard_map/ppermute | solution.py:295
  86.1 12.6 %collective-permute-start.20 = (bf16[16,6272]{1,0:T(8,128)(2,1)S(1)}, bf16[16,6272]{1,0:T(8,128)(2,1)S(1)}, u32[]{:S(2)}, u32[]{:S(2)}) collective-permute-start(bf16[16,6272]{1,0:T(8,128)(2,1)S(1)} %get-tuple-element.83), channel_id=1, source_target_pairs={{0,1},{1,2},{2,3},{3,0},{4,5},{5,6},{6,7},{7,4},{8,9},{9,10},{10,1... | collective-permute-start | bytes 602120 | tf_op jit(solution)/shard_map/ppermute | solution.py:289
  86.2 12.5 %collective-permute-start.21 = (bf16[16,6272]{1,0:T(8,128)(2,1)S(1)}, bf16[16,6272]{1,0:T(8,128)(2,1)S(1)}, u32[]{:S(2)}, u32[]{:S(2)}) collective-permute-start(bf16[16,6272]{1,0:T(8,128)(2,1)S(1)} %get-tuple-element.85), channel_id=1, source_target_pairs={{0,2},{1,3},{2,0},{3,1},{4,6},{5,7},{6,4},{7,5},{8,10},{9,11},{10,... | collective-permute-start | bytes 602120 | tf_op jit(solution)/shard_map/ppermute | solution.py:289
  90.1 9.1 %collective-permute-start.22 = (bf16[16,6272]{1,0:T(8,128)(2,1)S(1)}, bf16[16,6272]{1,0:T(8,128)(2,1)S(1)}, u32[]{:S(2)}, u32[]{:S(2)}) collective-permute-start(bf16[16,6272]{1,0:T(8,128)(2,1)S(1)} %get-tuple-element.84), channel_id=1, source_target_pairs={{0,3},{1,0},{2,1},{3,2},{4,7},{5,4},{6,5},{7,6},{8,11},{9,8},{10,9... | collective-permute-start | bytes 602120 | tf_op jit(solution)/shard_map/ppermute | solution.py:289
  99.4 9.8 %collective-permute-start.27 = (bf16[8,6272]{1,0:T(8,128)(2,1)S(1)}, bf16[8,6272]{1,0:T(8,128)(2,1)S(1)}, u32[]{:S(2)}, u32[]{:S(2)}) collective-permute-start(bf16[8,6272]{1,0:T(8,128)(2,1)S(1)} %slice.54), channel_id=1, source_target_pairs={{0,4},{1,5},{2,6},{3,7},{4,0},{5,1},{6,2},{7,3},{8,12},{9,13},{10,... | collective-permute-start | bytes 301064 | tf_op jit(solution)/shard_map/ppermute | solution.py:286

commit v4 on v3

--- a/solution.py
+++ b/solution.py
@@ -74,6 +74,12 @@
     return [(s, min(size, total - s)) for s in range(0, total, size)]
 
 
+def copies(sources, places, sems, first):
+    return [
+        pltpu.make_async_copy(a, b, sems.at[first + k]) for k, (a, b) in enumerate(zip(sources, places))
+    ]
+
+
 def prep_kernel(rot, turn, back, rows_all):
     pair_all, coef_all, pair_tile, coef_tile = selectors()
     rows_all[...] = jnp.zeros_like(rows_all)
@@ -161,10 +167,17 @@
 
 
 def forward_kernel(
-    own, partner, far0, far1, far2, far3, src, tgt, turn, back, basis, w_rad, w0, w1r, w1i, w2r, w2i,
-    agg0, agg1, agg2, agg3, turned, outs, pre,
-    wide, zero, one, two, gated, rad,
+    own, partner, far0, far1, far2, far3, src, tgt, turn, basis, w_rad,
+    w0_far, w1r_far, w1i_far, w2r_far, w2i_far, back_far,
+    agg0, agg1, agg2, agg3, pre, turned_far, outs_far,
+    wide, zero, one, two, w0, w1r, w1i, w2r, w2i, back, turned, outs, gated, rad, sems,
 ):
+    loads = copies(
+        (w0_far, w1r_far, w1i_far, w2r_far, w2i_far, back_far), (w0, w1r, w1i, w2r, w2i, back), sems, 0
+    )
+    stores = copies((turned, outs), (turned_far, outs_far), sems, 6)
+    for c in loads:
+        c.start()
     value = dot(basis[...], w_rad[...])
     pre[...] = value
     rad[...] = value * jax.nn.sigmoid(value)
@@ -176,6 +189,9 @@
         put_order(zero, one, two, g, degree, order, (part * rad[rows, :]).astype(BF16))
 
     rotate(turn, wide, use)
+    stores[0].start()
+    for c in loads[:5]:
+        c.wait()
     for start, size in chunks(7 * LANES, 256):
         outs[:, pl.ds(start, size)] = dot(zero[...], w0[:, pl.ds(start, size)])
     for stacked, real, imag, up, down, count in (
@@ -187,25 +203,39 @@
             b = dot(stacked[...], imag[:, pl.ds(start, size)])
             outs[:, pl.ds(up * LANES + start, size)] = a[:LANES] - b[LANES:]
             outs[:, pl.ds(down * LANES + start, size)] = a[LANES:] + b[:LANES]
+    stores[1].start()
     gate = jax.nn.sigmoid(outs[:, pl.ds(0, LANES)])
     for q in range(ORDERS):
         lanes = pl.ds(q * LANES, LANES)
         gated[:, lanes] = (outs[:, lanes] * gate).astype(BF16)
+    loads[5].wait()
     rotate_back(back, gated, wide)
     add_rows(tgt, wide, (agg0, agg1, agg2, agg3))
+    for c in stores:
+        c.wait()
 
 
 def backward_kernel(
-    up0, up1, up2, up3, tgt, src, turn, back, turned, outs, pre, w_rad, w0, w1r, w1i, w2r, w2i,
+    up0, up1, up2, up3, tgt, src, turn, pre, w_rad,
+    outs_far, w0_far, w1r_far, w1i_far, w2r_far, w2i_far, turned_far, back_far,
     own, partner, far0, far1, far2, far3, grad_basis,
-    wide, zero, one, two, grads, fragments, rad,
+    wide, zero, one, two, w0, w1r, w1i, w2r, w2i, back, turned, outs, grads, fragments, rad, sems,
 ):
+    loads = copies(
+        (outs_far, w0_far, w1r_far, w1i_far, w2r_far, w2i_far, turned_far, back_far),
+        (outs, w0, w1r, w1i, w2r, w2i, turned, back),
+        sems,
+        0,
+    )
+    for c in loads:
+        c.start()
     pick_rows(tgt, (up0, up1, up2, up3), wide)
 
     def use(g, degree, order, part):
         grads[pl.ds(GROUP * g, GROUP), pl.ds(place_of(degree, order) * LANES, LANES)] = part
 
     rotate(turn, wide, use)
+    loads[0].wait()
     scalar = outs[:, pl.ds(0, LANES)]
     gate = jax.nn.sigmoid(scalar)
     slope = gate * (1.0 - gate)
@@ -233,6 +263,8 @@
         fragments[:, lanes] = (scaled * rad[...]).astype(BF16)
         return total + scaled * turned[:, lanes]
 
+    for c in loads[1:7]:
+        c.wait()
     for start, size in chunks(7 * LANES, 256):
         a = dot_nt(zero[...], w0[pl.ds(start, size), :])
         for k in range(size // LANES):
@@ -249,14 +281,18 @@
                 total = take(total, up + start // LANES + k, a[:LANES, cut] + b[LANES:, cut])
                 total = take(total, down + start // LANES + k, a[LANES:, cut] - b[:LANES, cut])
     grad_basis[...] = dot_nt((total * slope).astype(BF16), w_rad[...])
+    loads[7].wait()
     rotate_back(back, fragments, wide)
     add_rows(src, wide, (own, partner, far0, far1, far2, far3))
 
 
-def kernel_call(kernel, outs, scratch, flops, moved):
+def kernel_call(kernel, near, far, outs, far_outs, scratch, flops, moved):
+    inside, outside = pl.BlockSpec(memory_space=pltpu.VMEM), pl.BlockSpec(memory_space=pl.ANY)
     return pl.pallas_call(
         kernel,
-        out_shape=outs,
+        out_shape=outs + far_outs,
+        in_specs=[inside] * near + [outside] * far,
+        out_specs=(inside,) * len(outs) + (outside,) * len(far_outs),
         scratch_shapes=scratch,
         compiler_params=pltpu.CompilerParams(vmem_limit_bytes=VMEM),
         cost_estimate=pl.CostEstimate(flops=flops, bytes_accessed=moved, transcendentals=0),
@@ -309,34 +345,38 @@
             total = total + shift(parts[d], d).astype(F32)
         return total
 
+    flat = embeddings.reshape(atoms, WIDE)
+    pair = jnp.concatenate([flat, across(flat)], axis=0)
+    gain = jnp.dot(
+        (species[:, None] == lax.iota(jnp.int32, species_gain.shape[0])[None, :]).astype(F32),
+        species_gain,
+        precision=lax.Precision.HIGHEST,
+    )
+    upstream = (cotangent.astype(F32) * gain[:, None, :] * scale).astype(BF16).reshape(atoms, WIDE)
+    up_far = across(upstream)
+    pair, rotations, targets = after(pair, rotations, targets)
+    far_pair = swap_far(pair)
+    own_pieces = spread(pair)
     groups = LANES // GROUP
     turn, back = kernel_call(
         prep_kernel,
+        1,
+        0,
         (shaped(groups, TURN_ROWS, 256), shaped(groups, BACK_ROWS, 256)),
+        (),
         [pltpu.VMEM((ROT_PAD, LANES), BF16)],
         2 * 10**9,
         6 * 10**6,
     )(rotations)
 
-    flat = embeddings.reshape(atoms, WIDE)
-    beyond, back = after(across(flat), back)
-    pair = jnp.concatenate([flat, beyond], axis=0)
-    pair, species, cot, targets = after(pair, species, cotangent, targets)
-    far_pair = swap_far(pair)
-    own_pieces = spread(pair)
-    gain = jnp.dot(
-        (species[:, None] == lax.iota(jnp.int32, species_gain.shape[0])[None, :]).astype(F32),
-        species_gain,
-        precision=lax.Precision.HIGHEST,
-    )
-    upstream = (cot.astype(F32) * gain[:, None, :] * scale).astype(BF16).reshape(atoms, WIDE)
-    far_pair, upstream, send_left, send_right, sources = after(
-        far_pair, upstream, send_left, send_right, sources
-    )
+    far_pair, back, send_left, send_right, sources = after(
+        far_pair, back, send_left, send_right, sources
+    )
+    *own_pieces, back = after(*own_pieces, back)
     far_pieces = spread(far_pair)
     own_table = jnp.concatenate(own_pieces, axis=0)
     partner_table = swap_near(own_table)
-    *far_pieces, up_far = after(*far_pieces, across(upstream))
+    *far_pieces, up_far = after(*far_pieces, up_far)
     up_pair = jnp.concatenate([upstream, up_far], axis=0)
     up_pieces = spread(up_pair)
 
@@ -367,33 +407,52 @@
             pltpu.VMEM((edges, 7 * LANES), BF16),
             pltpu.VMEM((2 * edges, 6 * LANES), BF16),
             pltpu.VMEM((2 * edges, 5 * LANES), BF16),
+            *[pltpu.VMEM(w.shape, BF16) for w in weights],
+            pltpu.VMEM(back.shape, BF16),
+            pltpu.VMEM((edges, ORDERS * LANES), F32),
+            pltpu.VMEM((edges, ORDERS * LANES), F32),
         ]
 
     piece = shaped(2 * atoms, WIDE)
     whole = shaped(block_atoms, WIDE)
     kept = shaped(edges, ORDERS * LANES, kind=F32)
     square = shaped(edges, LANES, kind=F32)
-    *aggs, turned, outs, pre = kernel_call(
+    *aggs, pre, turned, outs = kernel_call(
         forward_kernel,
-        (piece, piece, piece, piece, kept, kept, square),
-        work() + [pltpu.VMEM((edges, ORDERS * LANES), BF16), pltpu.VMEM((edges, LANES), F32)],
+        11,
+        6,
+        (piece, piece, piece, piece, square),
+        (kept, kept),
+        work()
+        + [
+            pltpu.VMEM((edges, ORDERS * LANES), BF16),
+            pltpu.VMEM((edges, LANES), F32),
+            pltpu.SemaphoreType.DMA((8,)),
+        ],
         4 * 10**9,
         20 * 10**6,
-    )(own_table, partner_table, *far_pieces, src_col, tgt_row, turn, back, radial_basis, weight_radial, *weights)
+    )(
+        own_table, partner_table, *far_pieces, src_col, tgt_row, turn, radial_basis, weight_radial,
+        *weights, back,
+    )
 
     agg_pair = collect(aggs)
     own_grad, near_grad, *far_grads, grad_basis = kernel_call(
         backward_kernel,
+        9,
+        8,
         (whole, whole, piece, piece, piece, piece, square),
+        (),
         work()
         + [
             pltpu.VMEM((edges, ORDERS * LANES), F32),
             pltpu.VMEM((edges, ORDERS * LANES), BF16),
             pltpu.VMEM((edges, LANES), F32),
+            pltpu.SemaphoreType.DMA((8,)),
         ],
         5 * 10**9,
         20 * 10**6,
-    )(*up_pieces, tgt_col, src_row, turn, back, turned, outs, pre, weight_radial, *weights)
+    )(*up_pieces, tgt_col, src_row, turn, pre, weight_radial, outs, *weights, turned, back)
 
     *far_grads, near_grad, agg_pair = after(*far_grads, near_grad, agg_pair)
     near_home, agg_far = after(swap_near(near_grad), across(agg_pair[atoms:].astype(BF16)))

time: 111 us -> 110 us (level)
  waiting for transfers between devices: 29.2 us -> 23.8 us
  other arithmetic: 2.26 us -> 5.37 us
    ppermute x4, waiting for transfers between devices: 10 us -> 4.37 us  [across(): return lax.ppermute(v, 'edge', [(s, (s + 4) % 8) for s in range(8)])]
    ppermute x4, starting transfers between devices: 18.2 us -> 21.4 us  [across(): return lax.ppermute(v, 'edge', [(s, (s + 4) % 8) for s in range(8)])]
    ppermute x2, starting transfers between devices: 4.67 us -> 1.74 us  [swap_far(): lax.ppermute(v, 'space', [(b, (b + 2 * (b % 2) - 1) % blocks) for b in ra...]
    ppermute x2, waiting for transfers between devices: 3.04 us -> 4.67 us  [roll(): lax.ppermute(v, 'space', [(b, (b + k) % blocks) for b in range(blocks)])]
    ppermute x2, waiting for transfers between devices: 1.89 us -> 0.57 us  [swap_far(): lax.ppermute(v, 'space', [(b, (b + 2 * (b % 2) - 1) % blocks) for b in ra...]
    broadcast_in_dim x2, other arithmetic: 0.06 us -> 1.37 us  [on_device(): tgt_col, tgt_row = (tgt[:, None], tgt[None, :])]
    unnamed x28 -> x23, local copies, waits for them, and re-layouts: 2.22 us -> 2.21 us
  transfers between devices with their start and end apart: 28 -> 28, of which waited for: 11 -> 11; matrix products, arithmetic and copies ran while one was open for 2% -> 5% of each run, Pallas kernels for 21% -> 21%
where the time goes in v4:
time: 110 us; the launch traced here: 109 us
  starting transfers between devices  51.8 us (47%)
  waiting for transfers between devices  23.8 us (22%)
  Pallas kernels  23.1 us (21%)
  other arithmetic  5.37 us (5%)
  local copies, waits for them, and re-layouts  2.52 us (2%)
  between operations  1.52 us (1%)
    ppermute x18, starting transfers between devices, shift(): lax.ppermute(v, 'edge', [(s, s // 4 * 4 + (s + k) % 4) for s in range(8)])  26.8 us
    ppermute x4, starting transfers between devices, across(): return lax.ppermute(v, 'edge', [(s, (s + 4) % 8) for s in range(8)])  21.4 us
    ppermute x18, waiting for transfers between devices, shift(): lax.ppermute(v, 'edge', [(s, s // 4 * 4 + (s + k) % 4) for s in range(8)])  14.1 us
    pallas_call x1, Pallas kernels, on_device(): kernel_call(backward_kernel, 9, 8, (whole, whole, piece, piece, piece, pi...  9.49 us
    pallas_call x1, Pallas kernels, on_device(): kernel_call(forward_kernel, 11, 6, (piece, piece, piece, piece, square),...  9.01 us
    ppermute x2, waiting for transfers between devices, roll(): lax.ppermute(v, 'space', [(b, (b + k) % blocks) for b in range(blocks)])  4.67 us
    pallas_call x1, Pallas kernels, on_device(): kernel_call(prep_kernel, 1, 0, (shaped(groups, TURN_ROWS, 256), shaped(gr...  4.57 us
    ppermute x4, waiting for transfers between devices, across(): return lax.ppermute(v, 'edge', [(s, (s + 4) % 8) for s in range(8)])  4.37 us
  transfers between devices with their start and end apart: 28, of which 11 were waited for; matrix products, arithmetic and copies ran while one was open for 5% of the time, Pallas kernels for 21%

profile of v4, /device:TPU:8, one launch (start us, length us, event | category | flops | bytes accessed | tf_op | source)
XLA Modules:
  0.0 108.9 jit_solution(11495661713343745966)
XLA Ops:
  0.6 0.0 copy-start
  0.6 7.3 %collective-permute-start = (bf16[8,6272]{1,0:T(8,128)(2,1)}, bf16[8,6272]{1,0:T(8,128)(2,1)S(1)}, u32[]{:S(2)}, u32[]{:S(2)}) collective-permute-start(bf16[8,6272]{1,0:T(8,128)(2,1)} %bitcast.27), channel_id=1, source_target_pairs={{0,4},{1,5},{2,6},{3,7},{4,0},{5,1},{6,2},{7,3},{8,12},{9,13},{10,... | collective-permute-start | bytes 301064 | tf_op jit(solution)/shard_map/ppermute | solution.py:322
  7.9 0.8 broadcast_multiply_fusion
  8.8 0.9 fusion.5
  9.7 0.8 collective-permute-start.5
  11.2 0.9 pad_maximum_fusion
  12.1 1.6 %collective-permute-start.1 = (bf16[16,6272]{1,0:T(8,128)(2,1)S(1)}, bf16[16,6272]{1,0:T(8,128)(2,1)S(1)}, u32[]{:S(2)}, u32[]{:S(2)}) collective-permute-start(bf16[16,6272]{1,0:T(8,128)(2,1)S(1)} %pad_maximum_fusion), channel_id=1, source_target_pairs={{0,248},{8,16},{16,8},{24,32},{32,24},{40,48},{48,40},{56,64},{64,... | collective-permute-start | bytes 602120 | tf_op jit(solution)/shard_map/ppermute | solution.py:331
  13.7 2.8 %collective-permute-start.11 = (bf16[16,6272]{1,0:T(8,128)(2,1)S(1)}, bf16[16,6272]{1,0:T(8,128)(2,1)S(1)}, u32[]{:S(2)}, u32[]{:S(2)}) collective-permute-start(bf16[16,6272]{1,0:T(8,128)(2,1)S(1)} %pad_maximum_fusion), channel_id=1, source_target_pairs={{0,3},{1,0},{2,1},{3,2},{4,7},{5,4},{6,5},{7,6},{8,11},{9,8},{10,9... | collective-permute-start | bytes 602120 | tf_op jit(solution)/shard_map/ppermute | solution.py:325
  16.4 0.8 collective-permute-start.12
  17.2 0.9 collective-permute-start.13
  18.1 0.7 fusion.32.tgt
  18.8 0.7 fusion.33
  19.5 0.1 copy.23.tgt
  19.6 0.8 copy-done.1
  20.4 4.6 %shard_map.184 = (bf16[8,464,256]{2,1,0:T(8,128)(2,1)S(1)}, bf16[8,784,256]{2,1,0:T(8,128)(2,1)}) custom-call(bf16[235,128]{1,0:T(8,128)(2,1)S(1)} %copy-done.1), custom_call_target="tpu_custom_call" | custom-call | flops 2000000000 | bytes 6000000 | tf_op jit(solution)/shard_map/pallas_call | solution.py:361
  25.0 1.3 %copy-done.4 = bf16[8,464,256]{2,1,0:T(8,128)(2,1)} copy-done((bf16[8,464,256]{2,1,0:T(8,128)(2,1)}, bf16[8,464,256]{2,1,0:T(8,128)(2,1)S(1)}, u32[]{:S(2)}) %copy-start.4) | copy-done | bytes 1900568
  26.3 0.0 collective-permute-done.1.far0
  26.3 2.4 %collective-permute-start.2 = (bf16[16,6272]{1,0:T(8,128)(2,1)S(1)}, bf16[16,6272]{1,0:T(8,128)(2,1)S(1)}, u32[]{:S(2)}, u32[]{:S(2)}) collective-permute-start(bf16[16,6272]{1,0:T(8,128)(2,1)S(1)} %collective-permute-done.1.far0), channel_id=1, source_target_pairs={{0,3},{1,0},{2,1},{3,2},{4,7},{5,4},{6,5},{7,6},{8,11},{9,8},{10,9... | collective-permute-start | bytes 602120 | tf_op jit(solution)/shard_map/ppermute | solution.py:325
  28.7 0.0 collective-permute-done.11
  28.7 1.5 %collective-permute-start.3 = (bf16[16,6272]{1,0:T(8,128)(2,1)S(1)}, bf16[16,6272]{1,0:T(8,128)(2,1)S(1)}, u32[]{:S(2)}, u32[]{:S(2)}) collective-permute-start(bf16[16,6272]{1,0:T(8,128)(2,1)S(1)} %collective-permute-done.1.far0), channel_id=1, source_target_pairs={{0,2},{1,3},{2,0},{3,1},{4,6},{5,7},{6,4},{7,5},{8,10},{9,11},{10,... | collective-permute-start | bytes 602120 | tf_op jit(solution)/shard_map/ppermute | solution.py:325
  30.2 0.0 collective-permute-done.12
  30.2 1.6 %collective-permute-start.10 = (s32[1,32]{1,0:T(1,128)S(1)}, s32[1,32]{1,0:T(1,128)S(1)}, u32[]{:S(2)}, u32[]{:S(2)}) collective-permute-start(s32[1,32]{1,0:T(1,128)S(1)} %copy-done.8), channel_id=1, source_target_pairs={{0,248},{8,0},{16,8},{24,16},{32,24},{40,32},{48,40},{56,48},{64,5... | collective-permute-start | bytes 392 | tf_op jit(solution)/shard_map/ppermute | solution.py:334
  31.8 0.0 collective-permute-done.13
  31.8 0.3 collective-permute-start.9
  32.2 0.8 collective-permute-done.10
  33.1 0.5 collective-permute-start.4
  33.6 3.8 %collective-permute-done.9 = s32[1,32]{1,0:T(1,128)S(1)} collective-permute-done((s32[1,32]{1,0:T(1,128)S(1)}, s32[1,32]{1,0:T(1,128)S(1)}, u32[]{:S(2)}, u32[]{:S(2)}) %collective-permute-start.9) | collective-permute-done | bytes 160 | tf_op jit(solution)/shard_map/ppermute | solution.py:334
  37.5 0.1 add_bitcast_fusion
  37.5 0.1 select_reduce_fusion
  37.7 0.1 copy.22.src
  37.8 4.3 %collective-permute-done.4.far3 = bf16[16,6272]{1,0:T(8,128)(2,1)S(1)} collective-permute-done((bf16[16,6272]{1,0:T(8,128)(2,1)S(1)}, bf16[16,6272]{1,0:T(8,128)(2,1)S(1)}, u32[]{:S(2)}, u32[]{:S(2)}) %collective-permute-start.4) | collective-permute-done | bytes 200736 | tf_op jit(solution)/shard_map/ppermute | solution.py:325
  42.1 0.1 collective-permute-start.6
  42.2 1.6 %collective-permute-start.7 = (bf16[16,6272]{1,0:T(8,128)(2,1)S(1)}, bf16[16,6272]{1,0:T(8,128)(2,1)S(1)}, u32[]{:S(2)}, u32[]{:S(2)}) collective-permute-start(bf16[16,6272]{1,0:T(8,128)(2,1)S(1)} %pad_maximum_fusion.1.up0), channel_id=1, source_target_pairs={{0,2},{1,3},{2,0},{3,1},{4,6},{5,7},{6,4},{7,5},{8,10},{9,11},{10,... | collective-permute-start | bytes 602120 | tf_op jit(solution)/shard_map/ppermute | solution.py:325
  43.8 1.1 collective-permute-start.8
  44.9 9.0 %shard_map.185 = (bf16[16,6272]{1,0:T(8,128)(2,1)S(1)}, bf16[16,6272]{1,0:T(8,128)(2,1)S(1)}, bf16[16,6272]{1,0:T(8,128)(2,1)S(1)}, bf16[16,6272]{1,0:T(8,128)(2...) custom-call(bf16[64,6272]{1,0:T(8,128)(2,1)S(1)} %constant_dynamic-update-slice_fusion.own, ...), custom_call_target="tpu_custom_call" | custom-call | flops 4000000000 | bytes 20000000 | tf_op jit(solution)/shard_map/pallas_call | solution.py:420
  53.9 1.2 %collective-permute-start.15 = (bf16[16,6272]{1,0:T(8,128)(2,1)S(1)}, bf16[16,6272]{1,0:T(8,128)(2,1)S(1)}, u32[]{:S(2)}, u32[]{:S(2)}) collective-permute-start(bf16[16,6272]{1,0:T(8,128)(2,1)S(1)} %get-tuple-element.74), channel_id=1, source_target_pairs={{0,1},{1,2},{2,3},{3,0},{4,5},{5,6},{6,7},{7,4},{8,9},{9,10},{10,1... | collective-permute-start | bytes 602120 | tf_op jit(solution)/shard_map/ppermute | solution.py:325
  55.1 2.5 %collective-permute-start.16 = (bf16[16,6272]{1,0:T(8,128)(2,1)S(1)}, bf16[16,6272]{1,0:T(8,128)(2,1)S(1)}, u32[]{:S(2)}, u32[]{:S(2)}) collective-permute-start(bf16[16,6272]{1,0:T(8,128)(2,1)S(1)} %get-tuple-element.75), channel_id=1, source_target_pairs={{0,2},{1,3},{2,0},{3,1},{4,6},{5,7},{6,4},{7,5},{8,10},{9,11},{10,... | collective-permute-start | bytes 602120 | tf_op jit(solution)/shard_map/ppermute | solution.py:325
  57.6 2.5 %collective-permute-start.17 = (bf16[16,6272]{1,0:T(8,128)(2,1)S(1)}, bf16[16,6272]{1,0:T(8,128)(2,1)S(1)}, u32[]{:S(2)}, u32[]{:S(2)}) collective-permute-start(bf16[16,6272]{1,0:T(8,128)(2,1)S(1)} %get-tuple-element.76), channel_id=1, source_target_pairs={{0,3},{1,0},{2,1},{3,2},{4,7},{5,4},{6,5},{7,6},{8,11},{9,8},{10,9... | collective-permute-start | bytes 602120 | tf_op jit(solution)/shard_map/ppermute | solution.py:325
  60.1 9.5 %shard_map.186 = (bf16[64,6272]{1,0:T(8,128)(2,1)S(1)}, bf16[64,6272]{1,0:T(8,128)(2,1)S(1)}, bf16[16,6272]{1,0:T(8,128)(2,1)S(1)}, bf16[16,6272]{1,0:T(8,128)(2...) custom-call(bf16[16,6272]{1,0:T(8,128)(2,1)S(1)} %pad_maximum_fusion.1.up0, ...), custom_call_target="tpu_custom_call" | custom-call | flops 5000000000 | bytes 20000000 | tf_op jit(solution)/shard_map/pallas_call | solution.py:440
  69.6 0.1 convert_add_fusion.1
  69.7 0.1 collective-permute-start.23
  69.8 1.5 %collective-permute-start.24 = (bf16[16,6272]{1,0:T(8,128)(2,1)S(1)}, bf16[16,6272]{1,0:T(8,128)(2,1)S(1)}, u32[]{:S(2)}, u32[]{:S(2)}) collective-permute-start(bf16[16,6272]{1,0:T(8,128)(2,1)S(1)} %get-tuple-element.84), channel_id=1, source_target_pairs={{0,2},{1,3},{2,0},{3,1},{4,6},{5,7},{6,4},{7,5},{8,10},{9,11},{10,... | collective-permute-start | bytes 602120 | tf_op jit(solution)/shard_map/ppermute | solution.py:325
  71.3 1.7 %collective-permute-start.25 = (bf16[16,6272]{1,0:T(8,128)(2,1)S(1)}, bf16[16,6272]{1,0:T(8,128)(2,1)S(1)}, u32[]{:S(2)}, u32[]{:S(2)}) collective-permute-start(bf16[16,6272]{1,0:T(8,128)(2,1)S(1)} %get-tuple-element.85), channel_id=1, source_target_pairs={{0,3},{1,0},{2,1},{3,2},{4,7},{5,4},{6,5},{7,6},{8,11},{9,8},{10,9... | collective-permute-start | bytes 602120 | tf_op jit(solution)/shard_map/ppermute | solution.py:325
  73.1 6.8 %collective-permute-start.19 = (bf16[8,6272]{1,0:T(8,128)(2,1)S(1)}, bf16[8,6272]{1,0:T(8,128)(2,1)S(1)}, u32[]{:S(2)}, u32[]{:S(2)}) collective-permute-start(bf16[8,6272]{1,0:T(8,128)(2,1)S(1)} %slice.55), channel_id=1, source_target_pairs={{0,4},{1,5},{2,6},{3,7},{4,0},{5,1},{6,2},{7,3},{8,12},{9,13},{10,... | collective-permute-start | bytes 301064 | tf_op jit(solution)/shard_map/ppermute | solution.py:322
  79.9 1.1 %collective-permute-done.23 = bf16[16,6272]{1,0:T(8,128)(2,1)S(1)} collective-permute-done((bf16[16,6272]{1,0:T(8,128)(2,1)S(1)}, bf16[16,6272]{1,0:T(8,128)(2,1)S(1)}, u32[]{:S(2)}, u32[]{:S(2)}) %collective-permute-start.23) | collective-permute-done | bytes 200736 | tf_op jit(solution)/shard_map/ppermute | solution.py:325
  81.0 0.6 collective-permute-done.25
  81.7 0.1 add_convert_fusion.1
  81.8 0.2 collective-permute-start.26
  81.9 1.6 %collective-permute-done.19 = bf16[8,6272]{1,0:T(8,128)(2,1)S(1)} collective-permute-done((bf16[8,6272]{1,0:T(8,128)(2,1)S(1)}, bf16[8,6272]{1,0:T(8,128)(2,1)S(1)}, u32[]{:S(2)}, u32[]{:S(2)}) %collective-permute-start.19) | collective-permute-done | bytes 100384 | tf_op jit(solution)/shard_map/ppermute | solution.py:322
  83.5 0.2 add_convert_fusion
  83.7 0.0 copy-start.6
  83.7 0.0 copy-start.5
  83.8 0.9 collective-permute-start.20
  84.7 2.3 %collective-permute-start.21 = (bf16[16,6272]{1,0:T(8,128)(2,1)S(1)}, bf16[16,6272]{1,0:T(8,128)(2,1)S(1)}, u32[]{:S(2)}, u32[]{:S(2)}) collective-permute-start(bf16[16,6272]{1,0:T(8,128)(2,1)S(1)} %get-tuple-element.89), channel_id=1, source_target_pairs={{0,2},{1,3},{2,0},{3,1},{4,6},{5,7},{6,4},{7,5},{8,10},{9,11},{10,... | collective-permute-start | bytes 602120 | tf_op jit(solution)/shard_map/ppermute | solution.py:325
  87.0 2.4 %collective-permute-start.22 = (bf16[16,6272]{1,0:T(8,128)(2,1)S(1)}, bf16[16,6272]{1,0:T(8,128)(2,1)S(1)}, u32[]{:S(2)}, u32[]{:S(2)}) collective-permute-start(bf16[16,6272]{1,0:T(8,128)(2,1)S(1)} %get-tuple-element.88), channel_id=1, source_target_pairs={{0,3},{1,0},{2,1},{3,2},{4,7},{5,4},{6,5},{7,6},{8,11},{9,8},{10,9... | collective-permute-start | bytes 602120 | tf_op jit(solution)/shard_map/ppermute | solution.py:325
  89.4 0.6 collective-permute-done.26
  90.0 3.5 %collective-permute-done.20 = bf16[16,6272]{1,0:T(8,128)(2,1)S(1)} collective-permute-done((bf16[16,6272]{1,0:T(8,128)(2,1)S(1)}, bf16[16,6272]{1,0:T(8,128)(2,1)S(1)}, u32[]{:S(2)}, u32[]{:S(2)}) %collective-permute-start.20) | collective-permute-done | bytes 200736 | tf_op jit(solution)/shard_map/ppermute | solution.py:325
  93.4 2.9 %collective-permute-done.21 = bf16[16,6272]{1,0:T(8,128)(2,1)S(1)} collective-permute-done((bf16[16,6272]{1,0:T(8,128)(2,1)S(1)}, bf16[16,6272]{1,0:T(8,128)(2,1)S(1)}, u32[]{:S(2)}, u32[]{:S(2)}) %collective-permute-start.21) | collective-permute-done | bytes 200736 | tf_op jit(solution)/shard_map/ppermute | solution.py:325
  96.4 1.7 %collective-permute-done.22 = bf16[16,6272]{1,0:T(8,128)(2,1)S(1)} collective-permute-done((bf16[16,6272]{1,0:T(8,128)(2,1)S(1)}, bf16[16,6272]{1,0:T(8,128)(2,1)S(1)}, u32[]{:S(2)}, u32[]{:S(2)}) %collective-permute-start.22) | collective-permute-done | bytes 200736 | tf_op jit(solution)/shard_map/ppermute | solution.py:325
  98.1 0.1 convert_add_fusion
  98.2 6.5 %collective-permute-start.27 = (bf16[8,6272]{1,0:T(8,128)(2,1)S(1)}, bf16[8,6272]{1,0:T(8,128)(2,1)S(1)}, u32[]{:S(2)}, u32[]{:S(2)}) collective-permute-start(bf16[8,6272]{1,0:T(8,128)(2,1)S(1)} %slice.54), channel_id=1, source_target_pairs={{0,4},{1,5},{2,6},{3,7},{4,0},{5,1},{6,2},{7,3},{8,12},{9,13},{10,... | collective-permute-start | bytes 301064 | tf_op jit(solution)/shard_map/ppermute | solution.py:322
  104.7 0.7 fusion.4
  105.4 2.8 %collective-permute-done.27 = bf16[8,6272]{1,0:T(8,128)(2,1)S(1)} collective-permute-done((bf16[8,6272]{1,0:T(8,128)(2,1)S(1)}, bf16[8,6272]{1,0:T(8,128)(2,1)S(1)}, u32[]{:S(2)}, u32[]{:S(2)}) %collective-permute-start.27) | collective-permute-done | bytes 100384 | tf_op jit(solution)/shard_map/ppermute | solution.py:322
  108.2 0.7 convert_add_fusion.2
  (40 shorter events, 0.3 us)
Async XLA Ops:
  0.6 7.3 %copy-start = (f32[100,128]{1,0:T(8,128)S(1)}, f32[100,128]{1,0:T(8,128)}, u32[]{:S(2)}) copy-start(f32[100,128]{1,0:T(8,128)} %param.19) | copy-start | bytes 153604
  0.6 10.5 %collective-permute-start = (bf16[8,6272]{1,0:T(8,128)(2,1)}, bf16[8,6272]{1,0:T(8,128)(2,1)S(1)}, u32[]{:S(2)}, u32[]{:S(2)}) collective-permute-start(bf16[8,6272]{1,0:T(8,128)(2,1)} %bitcast.27), channel_id=1, source_target_pairs={{0,4},{1,5},{2,6},{3,7},{4,0},{5,1},{6,2},{7,3},{8,12},{9,13},{10,... | collective-permute-start | bytes 301064 | tf_op jit(solution)/shard_map/ppermute | solution.py:322
  9.7 28.1 %collective-permute-start.5 = (bf16[8,6272]{1,0:T(8,128)(2,1)S(1)}, bf16[8,6272]{1,0:T(8,128)(2,1)S(1)}, u32[]{:S(2)}, u32[]{:S(2)}) collective-permute-start(bf16[8,6272]{1,0:T(8,128)(2,1)S(1)} %fusion.5), channel_id=1, source_target_pairs={{0,4},{1,5},{2,6},{3,7},{4,0},{5,1},{6,2},{7,3},{8,12},{9,13},{10,... | collective-permute-start | bytes 301064 | tf_op jit(solution)/shard_map/ppermute | solution.py:322
  12.1 14.2 %collective-permute-start.1 = (bf16[16,6272]{1,0:T(8,128)(2,1)S(1)}, bf16[16,6272]{1,0:T(8,128)(2,1)S(1)}, u32[]{:S(2)}, u32[]{:S(2)}) collective-permute-start(bf16[16,6272]{1,0:T(8,128)(2,1)S(1)} %pad_maximum_fusion), channel_id=1, source_target_pairs={{0,248},{8,16},{16,8},{24,32},{32,24},{40,48},{48,40},{56,64},{64,... | collective-permute-start | bytes 602120 | tf_op jit(solution)/shard_map/ppermute | solution.py:331
  13.7 15.1 %collective-permute-start.11 = (bf16[16,6272]{1,0:T(8,128)(2,1)S(1)}, bf16[16,6272]{1,0:T(8,128)(2,1)S(1)}, u32[]{:S(2)}, u32[]{:S(2)}) collective-permute-start(bf16[16,6272]{1,0:T(8,128)(2,1)S(1)} %pad_maximum_fusion), channel_id=1, source_target_pairs={{0,3},{1,0},{2,1},{3,2},{4,7},{5,4},{6,5},{7,6},{8,11},{9,8},{10,9... | collective-permute-start | bytes 602120 | tf_op jit(solution)/shard_map/ppermute | solution.py:325
  16.4 13.8 %collective-permute-start.12 = (bf16[16,6272]{1,0:T(8,128)(2,1)S(1)}, bf16[16,6272]{1,0:T(8,128)(2,1)S(1)}, u32[]{:S(2)}, u32[]{:S(2)}) collective-permute-start(bf16[16,6272]{1,0:T(8,128)(2,1)S(1)} %pad_maximum_fusion), channel_id=1, source_target_pairs={{0,2},{1,3},{2,0},{3,1},{4,6},{5,7},{6,4},{7,5},{8,10},{9,11},{10,... | collective-permute-start | bytes 602120 | tf_op jit(solution)/shard_map/ppermute | solution.py:325
  17.2 14.6 %collective-permute-start.13 = (bf16[16,6272]{1,0:T(8,128)(2,1)S(1)}, bf16[16,6272]{1,0:T(8,128)(2,1)S(1)}, u32[]{:S(2)}, u32[]{:S(2)}) collective-permute-start(bf16[16,6272]{1,0:T(8,128)(2,1)S(1)} %pad_maximum_fusion), channel_id=1, source_target_pairs={{0,1},{1,2},{2,3},{3,0},{4,5},{5,6},{6,7},{7,4},{8,9},{9,10},{10,1... | collective-permute-start | bytes 602120 | tf_op jit(solution)/shard_map/ppermute | solution.py:325
  19.6 0.8 copy-start.1
  20.4 9.8 %copy-start.8 = (s32[1,32]{1,0:T(1,128)S(1)}, s32[1,32]{1,0:T(1,128)}, u32[]{:S(2)}) copy-start(s32[1,32]{1,0:T(1,128)} %param.23) | copy-start | bytes 388
  20.4 11.4 %copy-start.9 = (s32[1,32]{1,0:T(1,128)S(1)}, s32[1,32]{1,0:T(1,128)}, u32[]{:S(2)}) copy-start(s32[1,32]{1,0:T(1,128)} %param.24) | copy-start | bytes 388
  25.0 1.3 %copy-start.4 = (bf16[8,464,256]{2,1,0:T(8,128)(2,1)}, bf16[8,464,256]{2,1,0:T(8,128)(2,1)S(1)}, u32[]{:S(2)}) copy-start(bf16[8,464,256]{2,1,0:T(8,128)(2,1)S(1)} %get-tuple-element.54.turn) | copy-start | bytes 5701636
  26.3 5.9 %copy-start.7 = (s32[128]{0:T(128)S(1)}, s32[128]{0:T(128)}, u32[]{:S(2)}) copy-start(s32[128]{0:T(128)} %param.20) | copy-start | bytes 1540
  26.3 18.6 %copy-start.2 = (bf16[128,128]{1,0:T(8,128)(2,1)S(1)}, bf16[128,128]{1,0:T(8,128)(2,1)}, u32[]{:S(2)}) copy-start(bf16[128,128]{1,0:T(8,128)(2,1)} %basis.1) | copy-start | bytes 98308
  26.3 18.6 %copy-start.3 = (bf16[128,128]{1,0:T(8,128)(2,1)S(1)}, bf16[128,128]{1,0:T(8,128)(2,1)}, u32[]{:S(2)}) copy-start(bf16[128,128]{1,0:T(8,128)(2,1)} %w_rad.3) | copy-start | bytes 98308
  26.3 11.5 %collective-permute-start.2 = (bf16[16,6272]{1,0:T(8,128)(2,1)S(1)}, bf16[16,6272]{1,0:T(8,128)(2,1)S(1)}, u32[]{:S(2)}, u32[]{:S(2)}) collective-permute-start(bf16[16,6272]{1,0:T(8,128)(2,1)S(1)} %collective-permute-done.1.far0), channel_id=1, source_target_pairs={{0,3},{1,0},{2,1},{3,2},{4,7},{5,4},{6,5},{7,6},{8,11},{9,8},{10,9... | collective-permute-start | bytes 602120 | tf_op jit(solution)/shard_map/ppermute | solution.py:325
  28.7 9.1 %collective-permute-start.3 = (bf16[16,6272]{1,0:T(8,128)(2,1)S(1)}, bf16[16,6272]{1,0:T(8,128)(2,1)S(1)}, u32[]{:S(2)}, u32[]{:S(2)}) collective-permute-start(bf16[16,6272]{1,0:T(8,128)(2,1)S(1)} %collective-permute-done.1.far0), channel_id=1, source_target_pairs={{0,2},{1,3},{2,0},{3,1},{4,6},{5,7},{6,4},{7,5},{8,10},{9,11},{10,... | collective-permute-start | bytes 602120 | tf_op jit(solution)/shard_map/ppermute | solution.py:325
  30.2 2.9 %collective-permute-start.10 = (s32[1,32]{1,0:T(1,128)S(1)}, s32[1,32]{1,0:T(1,128)S(1)}, u32[]{:S(2)}, u32[]{:S(2)}) collective-permute-start(s32[1,32]{1,0:T(1,128)S(1)} %copy-done.8), channel_id=1, source_target_pairs={{0,248},{8,0},{16,8},{24,16},{32,24},{40,32},{48,40},{56,48},{64,5... | collective-permute-start | bytes 392 | tf_op jit(solution)/shard_map/ppermute | solution.py:334
  31.8 5.7 %collective-permute-start.9 = (s32[1,32]{1,0:T(1,128)S(1)}, s32[1,32]{1,0:T(1,128)S(1)}, u32[]{:S(2)}, u32[]{:S(2)}) collective-permute-start(s32[1,32]{1,0:T(1,128)S(1)} %copy-done.9), channel_id=1, source_target_pairs={{0,8},{8,16},{16,24},{24,32},{32,40},{40,48},{48,56},{56,64},{64,7... | collective-permute-start | bytes 392 | tf_op jit(solution)/shard_map/ppermute | solution.py:334
  33.1 9.0 %collective-permute-start.4 = (bf16[16,6272]{1,0:T(8,128)(2,1)S(1)}, bf16[16,6272]{1,0:T(8,128)(2,1)S(1)}, u32[]{:S(2)}, u32[]{:S(2)}) collective-permute-start(bf16[16,6272]{1,0:T(8,128)(2,1)S(1)} %collective-permute-done.1.far0), channel_id=1, source_target_pairs={{0,1},{1,2},{2,3},{3,0},{4,5},{5,6},{6,7},{7,4},{8,9},{9,10},{10,1... | collective-permute-start | bytes 602120 | tf_op jit(solution)/shard_map/ppermute | solution.py:325
  37.5 7.4 %collective-permute-start.14 = (bf16[64,6272]{1,0:T(8,128)(2,1)S(1)}, bf16[64,6272]{1,0:T(8,128)(2,1)S(1)}, u32[]{:S(2)}, u32[]{:S(2)}) collective-permute-start(bf16[64,6272]{1,0:T(8,128)(2,1)S(1)} %constant_dynamic-update-slice_fusion.own), channel_id=1, source_target_pairs={{0,8},{8,0},{16,24},{24,16},{32,40},{40,32},{48,56},{56,48},{64,72... | collective-permute-start | bytes 2408456 | tf_op jit(solution)/shard_map/ppermute | solution.py:328
  42.1 15.5 %collective-permute-start.6 = (bf16[16,6272]{1,0:T(8,128)(2,1)S(1)}, bf16[16,6272]{1,0:T(8,128)(2,1)S(1)}, u32[]{:S(2)}, u32[]{:S(2)}) collective-permute-start(bf16[16,6272]{1,0:T(8,128)(2,1)S(1)} %pad_maximum_fusion.1.up0), channel_id=1, source_target_pairs={{0,3},{1,0},{2,1},{3,2},{4,7},{5,4},{6,5},{7,6},{8,11},{9,8},{10,9... | collective-permute-start | bytes 602120 | tf_op jit(solution)/shard_map/ppermute | solution.py:325
  42.2 17.9 %collective-permute-start.7 = (bf16[16,6272]{1,0:T(8,128)(2,1)S(1)}, bf16[16,6272]{1,0:T(8,128)(2,1)S(1)}, u32[]{:S(2)}, u32[]{:S(2)}) collective-permute-start(bf16[16,6272]{1,0:T(8,128)(2,1)S(1)} %pad_maximum_fusion.1.up0), channel_id=1, source_target_pairs={{0,2},{1,3},{2,0},{3,1},{4,6},{5,7},{6,4},{7,5},{8,10},{9,11},{10,... | collective-permute-start | bytes 602120 | tf_op jit(solution)/shard_map/ppermute | solution.py:325
  43.8 16.3 %collective-permute-start.8 = (bf16[16,6272]{1,0:T(8,128)(2,1)S(1)}, bf16[16,6272]{1,0:T(8,128)(2,1)S(1)}, u32[]{:S(2)}, u32[]{:S(2)}) collective-permute-start(bf16[16,6272]{1,0:T(8,128)(2,1)S(1)} %pad_maximum_fusion.1.up0), channel_id=1, source_target_pairs={{0,1},{1,2},{2,3},{3,0},{4,5},{5,6},{6,7},{7,4},{8,9},{9,10},{10,1... | collective-permute-start | bytes 602120 | tf_op jit(solution)/shard_map/ppermute | solution.py:325
  53.9 15.7 %collective-permute-start.15 = (bf16[16,6272]{1,0:T(8,128)(2,1)S(1)}, bf16[16,6272]{1,0:T(8,128)(2,1)S(1)}, u32[]{:S(2)}, u32[]{:S(2)}) collective-permute-start(bf16[16,6272]{1,0:T(8,128)(2,1)S(1)} %get-tuple-element.74), channel_id=1, source_target_pairs={{0,1},{1,2},{2,3},{3,0},{4,5},{5,6},{6,7},{7,4},{8,9},{9,10},{10,1... | collective-permute-start | bytes 602120 | tf_op jit(solution)/shard_map/ppermute | solution.py:325
  55.1 14.5 %collective-permute-start.16 = (bf16[16,6272]{1,0:T(8,128)(2,1)S(1)}, bf16[16,6272]{1,0:T(8,128)(2,1)S(1)}, u32[]{:S(2)}, u32[]{:S(2)}) collective-permute-start(bf16[16,6272]{1,0:T(8,128)(2,1)S(1)} %get-tuple-element.75), channel_id=1, source_target_pairs={{0,2},{1,3},{2,0},{3,1},{4,6},{5,7},{6,4},{7,5},{8,10},{9,11},{10,... | collective-permute-start | bytes 602120 | tf_op jit(solution)/shard_map/ppermute | solution.py:325
  57.6 12.0 %collective-permute-start.17 = (bf16[16,6272]{1,0:T(8,128)(2,1)S(1)}, bf16[16,6272]{1,0:T(8,128)(2,1)S(1)}, u32[]{:S(2)}, u32[]{:S(2)}) collective-permute-start(bf16[16,6272]{1,0:T(8,128)(2,1)S(1)} %get-tuple-element.76), channel_id=1, source_target_pairs={{0,3},{1,0},{2,1},{3,2},{4,7},{5,4},{6,5},{7,6},{8,11},{9,8},{10,9... | collective-permute-start | bytes 602120 | tf_op jit(solution)/shard_map/ppermute | solution.py:325
  69.7 11.3 %collective-permute-start.23 = (bf16[16,6272]{1,0:T(8,128)(2,1)S(1)}, bf16[16,6272]{1,0:T(8,128)(2,1)S(1)}, u32[]{:S(2)}, u32[]{:S(2)}) collective-permute-start(bf16[16,6272]{1,0:T(8,128)(2,1)S(1)} %get-tuple-element.83), channel_id=1, source_target_pairs={{0,1},{1,2},{2,3},{3,0},{4,5},{5,6},{6,7},{7,4},{8,9},{9,10},{10,1... | collective-permute-start | bytes 602120 | tf_op jit(solution)/shard_map/ppermute | solution.py:325
  69.8 11.2 %collective-permute-start.24 = (bf16[16,6272]{1,0:T(8,128)(2,1)S(1)}, bf16[16,6272]{1,0:T(8,128)(2,1)S(1)}, u32[]{:S(2)}, u32[]{:S(2)}) collective-permute-start(bf16[16,6272]{1,0:T(8,128)(2,1)S(1)} %get-tuple-element.84), channel_id=1, source_target_pairs={{0,2},{1,3},{2,0},{3,1},{4,6},{5,7},{6,4},{7,5},{8,10},{9,11},{10,... | collective-permute-start | bytes 602120 | tf_op jit(solution)/shard_map/ppermute | solution.py:325
  71.3 10.4 %collective-permute-start.25 = (bf16[16,6272]{1,0:T(8,128)(2,1)S(1)}, bf16[16,6272]{1,0:T(8,128)(2,1)S(1)}, u32[]{:S(2)}, u32[]{:S(2)}) collective-permute-start(bf16[16,6272]{1,0:T(8,128)(2,1)S(1)} %get-tuple-element.85), channel_id=1, source_target_pairs={{0,3},{1,0},{2,1},{3,2},{4,7},{5,4},{6,5},{7,6},{8,11},{9,8},{10,9... | collective-permute-start | bytes 602120 | tf_op jit(solution)/shard_map/ppermute | solution.py:325
  73.0 10.5 %collective-permute-start.18 = (bf16[64,6272]{1,0:T(8,128)(2,1)S(1)}, bf16[64,6272]{1,0:T(8,128)(2,1)S(1)}, u32[]{:S(2)}, u32[]{:S(2)}) collective-permute-start(bf16[64,6272]{1,0:T(8,128)(2,1)S(1)} %get-tuple-element.78), channel_id=1, source_target_pairs={{0,8},{8,0},{16,24},{24,16},{32,40},{40,32},{48,56},{56,48},{64,72... | collective-permute-start | bytes 2408456 | tf_op jit(solution)/shard_map/ppermute | solution.py:328
  73.1 10.4 %collective-permute-start.19 = (bf16[8,6272]{1,0:T(8,128)(2,1)S(1)}, bf16[8,6272]{1,0:T(8,128)(2,1)S(1)}, u32[]{:S(2)}, u32[]{:S(2)}) collective-permute-start(bf16[8,6272]{1,0:T(8,128)(2,1)S(1)} %slice.55), channel_id=1, source_target_pairs={{0,4},{1,5},{2,6},{3,7},{4,0},{5,1},{6,2},{7,3},{8,12},{9,13},{10,... | collective-permute-start | bytes 301064 | tf_op jit(solution)/shard_map/ppermute | solution.py:322
  81.8 8.2 %collective-permute-start.26 = (bf16[16,6272]{1,0:T(8,128)(2,1)S(1)}, bf16[16,6272]{1,0:T(8,128)(2,1)S(1)}, u32[]{:S(2)}, u32[]{:S(2)}) collective-permute-start(bf16[16,6272]{1,0:T(8,128)(2,1)S(1)} %add_convert_fusion.1), channel_id=1, source_target_pairs={{0,248},{8,16},{16,8},{24,32},{32,24},{40,48},{48,40},{56,64},{64,... | collective-permute-start | bytes 602120 | tf_op jit(solution)/shard_map/ppermute | solution.py:331
  83.7 21.0 %copy-start.6 = (bf16[8,49,128]{2,0,1:T(8,128)(2,1)S(1)}, bf16[8,49,128]{2,0,1:T(8,128)(2,1)}, u32[]{:S(2)}) copy-start(bf16[8,49,128]{2,0,1:T(8,128)(2,1)} %param.17) | copy-start | bytes 301060
  83.7 24.5 %copy-start.5 = (bf16[8,49,128]{2,0,1:T(8,128)(2,1)S(1)}, bf16[8,49,128]{2,0,1:T(8,128)(2,1)}, u32[]{:S(2)}) copy-start(bf16[8,49,128]{2,0,1:T(8,128)(2,1)} %param.33) | copy-start | bytes 301060
  83.8 9.7 %collective-permute-start.20 = (bf16[16,6272]{1,0:T(8,128)(2,1)S(1)}, bf16[16,6272]{1,0:T(8,128)(2,1)S(1)}, u32[]{:S(2)}, u32[]{:S(2)}) collective-permute-start(bf16[16,6272]{1,0:T(8,128)(2,1)S(1)} %get-tuple-element.87), channel_id=1, source_target_pairs={{0,1},{1,2},{2,3},{3,0},{4,5},{5,6},{6,7},{7,4},{8,9},{9,10},{10,1... | collective-permute-start | bytes 602120 | tf_op jit(solution)/shard_map/ppermute | solution.py:325
  84.7 11.7 %collective-permute-start.21 = (bf16[16,6272]{1,0:T(8,128)(2,1)S(1)}, bf16[16,6272]{1,0:T(8,128)(2,1)S(1)}, u32[]{:S(2)}, u32[]{:S(2)}) collective-permute-start(bf16[16,6272]{1,0:T(8,128)(2,1)S(1)} %get-tuple-element.89), channel_id=1, source_target_pairs={{0,2},{1,3},{2,0},{3,1},{4,6},{5,7},{6,4},{7,5},{8,10},{9,11},{10,... | collective-permute-start | bytes 602120 | tf_op jit(solution)/shard_map/ppermute | solution.py:325
  87.0 11.1 %collective-permute-start.22 = (bf16[16,6272]{1,0:T(8,128)(2,1)S(1)}, bf16[16,6272]{1,0:T(8,128)(2,1)S(1)}, u32[]{:S(2)}, u32[]{:S(2)}) collective-permute-start(bf16[16,6272]{1,0:T(8,128)(2,1)S(1)} %get-tuple-element.88), channel_id=1, source_target_pairs={{0,3},{1,0},{2,1},{3,2},{4,7},{5,4},{6,5},{7,6},{8,11},{9,8},{10,9... | collective-permute-start | bytes 602120 | tf_op jit(solution)/shard_map/ppermute | solution.py:325
  98.2 10.0 %collective-permute-start.27 = (bf16[8,6272]{1,0:T(8,128)(2,1)S(1)}, bf16[8,6272]{1,0:T(8,128)(2,1)S(1)}, u32[]{:S(2)}, u32[]{:S(2)}) collective-permute-start(bf16[8,6272]{1,0:T(8,128)(2,1)S(1)} %slice.54), channel_id=1, source_target_pairs={{0,4},{1,5},{2,6},{3,7},{4,0},{5,1},{6,2},{7,3},{8,12},{9,13},{10,... | collective-permute-start | bytes 301064 | tf_op jit(solution)/shard_map/ppermute | solution.py:322

commit v5 on v4

--- a/solution.py
+++ b/solution.py
@@ -80,7 +80,7 @@
     ]
 
 
-def prep_kernel(rot, turn, back, rows_all):
+def prep_kernel(rot, first, turn, back, rows_all):
     pair_all, coef_all, pair_tile, coef_tile = selectors()
     rows_all[...] = jnp.zeros_like(rows_all)
     rows_all[pl.ds(0, ROT_ROWS), :] = rot[...]
@@ -168,16 +168,10 @@
 
 def forward_kernel(
     own, partner, far0, far1, far2, far3, src, tgt, turn, basis, w_rad,
-    w0_far, w1r_far, w1i_far, w2r_far, w2i_far, back_far,
-    agg0, agg1, agg2, agg3, pre, turned_far, outs_far,
-    wide, zero, one, two, w0, w1r, w1i, w2r, w2i, back, turned, outs, gated, rad, sems,
+    w0, w1r, w1i, w2r, w2i, back,
+    agg0, agg1, agg2, agg3, pre, turned, outs,
+    wide, zero, one, two, gated, rad,
 ):
-    loads = copies(
-        (w0_far, w1r_far, w1i_far, w2r_far, w2i_far, back_far), (w0, w1r, w1i, w2r, w2i, back), sems, 0
-    )
-    stores = copies((turned, outs), (turned_far, outs_far), sems, 6)
-    for c in loads:
-        c.start()
     value = dot(basis[...], w_rad[...])
     pre[...] = value
     rad[...] = value * jax.nn.sigmoid(value)
@@ -189,9 +183,6 @@
         put_order(zero, one, two, g, degree, order, (part * rad[rows, :]).astype(BF16))
 
     rotate(turn, wide, use)
-    stores[0].start()
-    for c in loads[:5]:
-        c.wait()
     for start, size in chunks(7 * LANES, 256):
         outs[:, pl.ds(start, size)] = dot(zero[...], w0[:, pl.ds(start, size)])
     for stacked, real, imag, up, down, count in (
@@ -203,16 +194,12 @@
             b = dot(stacked[...], imag[:, pl.ds(start, size)])
             outs[:, pl.ds(up * LANES + start, size)] = a[:LANES] - b[LANES:]
             outs[:, pl.ds(down * LANES + start, size)] = a[LANES:] + b[:LANES]
-    stores[1].start()
     gate = jax.nn.sigmoid(outs[:, pl.ds(0, LANES)])
     for q in range(ORDERS):
         lanes = pl.ds(q * LANES, LANES)
         gated[:, lanes] = (outs[:, lanes] * gate).astype(BF16)
-    loads[5].wait()
     rotate_back(back, gated, wide)
     add_rows(tgt, wide, (agg0, agg1, agg2, agg3))
-    for c in stores:
-        c.wait()
 
 
 def backward_kernel(
@@ -330,9 +317,6 @@
     def swap_far(v):
         return lax.ppermute(v, "space", [(b, (b + 2 * (b % 2) - 1) % blocks) for b in range(blocks)])
 
-    def roll(v, k):
-        return lax.ppermute(v, "space", [(b, (b + k) % blocks) for b in range(blocks)])
-
     def after(*values):
         return lax.optimization_barrier(values)
 
@@ -346,7 +330,10 @@
         return total
 
     flat = embeddings.reshape(atoms, WIDE)
-    pair = jnp.concatenate([flat, across(flat)], axis=0)
+    halo = send_left.shape[1]
+    lists = jnp.concatenate([send_left, send_right], axis=1).astype(BF16)
+    lists = jnp.pad(lists, ((0, 2 * atoms - 1), (0, LANES - 2 * halo)))
+    pair = jnp.concatenate([jnp.concatenate([flat, across(flat)], axis=0), lists], axis=1)
     gain = jnp.dot(
         (species[:, None] == lax.iota(jnp.int32, species_gain.shape[0])[None, :]).astype(F32),
         species_gain,
@@ -354,24 +341,22 @@
     )
     upstream = (cotangent.astype(F32) * gain[:, None, :] * scale).astype(BF16).reshape(atoms, WIDE)
     up_far = across(upstream)
-    pair, rotations, targets = after(pair, rotations, targets)
+    pair, targets = after(pair, targets)
     far_pair = swap_far(pair)
     own_pieces = spread(pair)
     groups = LANES // GROUP
     turn, back = kernel_call(
         prep_kernel,
         1,
-        0,
+        1,
         (shaped(groups, TURN_ROWS, 256), shaped(groups, BACK_ROWS, 256)),
         (),
         [pltpu.VMEM((ROT_PAD, LANES), BF16)],
         2 * 10**9,
         6 * 10**6,
-    )(rotations)
-
-    far_pair, back, send_left, send_right, sources = after(
-        far_pair, back, send_left, send_right, sources
-    )
+    )(rotations, pair)
+
+    far_pair, back, sources = after(far_pair, back, sources)
     *own_pieces, back = after(*own_pieces, back)
     far_pieces = spread(far_pair)
     own_table = jnp.concatenate(own_pieces, axis=0)
@@ -384,8 +369,15 @@
         owner, row = atom // atoms, atom % atoms
         return (owner % 4 - along) % 4 * (2 * atoms) + (owner // 4 - half) % 2 * atoms + row
 
-    lists = jnp.concatenate([roll(send_right, 1), roll(send_left, -1)], axis=1)[0]
-    halo = send_left.shape[1]
+    near_lists = partner_table[0, WIDE : WIDE + 2 * halo].astype(jnp.int32)
+    far_lists = far_pair[0, WIDE : WIDE + 2 * halo].astype(jnp.int32)
+    on_odd = odd == 1
+    lists = jnp.concatenate(
+        [
+            jnp.where(on_odd, near_lists, far_lists)[halo:],
+            jnp.where(on_odd, far_lists, near_lists)[:halo],
+        ]
+    )
     block_atoms = 8 * atoms
     halo_hot = (sources[:, None] - block_atoms) == lax.iota(jnp.int32, 2 * halo)[None, :]
     halo_atom = jnp.sum(jnp.where(halo_hot, lists[None, :], 0), axis=1)
@@ -407,10 +399,6 @@
             pltpu.VMEM((edges, 7 * LANES), BF16),
             pltpu.VMEM((2 * edges, 6 * LANES), BF16),
             pltpu.VMEM((2 * edges, 5 * LANES), BF16),
-            *[pltpu.VMEM(w.shape, BF16) for w in weights],
-            pltpu.VMEM(back.shape, BF16),
-            pltpu.VMEM((edges, ORDERS * LANES), F32),
-            pltpu.VMEM((edges, ORDERS * LANES), F32),
         ]
 
     piece = shaped(2 * atoms, WIDE)
@@ -419,16 +407,11 @@
     square = shaped(edges, LANES, kind=F32)
     *aggs, pre, turned, outs = kernel_call(
         forward_kernel,
-        11,
-        6,
-        (piece, piece, piece, piece, square),
-        (kept, kept),
-        work()
-        + [
-            pltpu.VMEM((edges, ORDERS * LANES), BF16),
-            pltpu.VMEM((edges, LANES), F32),
-            pltpu.SemaphoreType.DMA((8,)),
-        ],
+        17,
+        0,
+        (piece, piece, piece, piece, square, kept, kept),
+        (),
+        work() + [pltpu.VMEM((edges, ORDERS * LANES), BF16), pltpu.VMEM((edges, LANES), F32)],
         4 * 10**9,
         20 * 10**6,
     )(
@@ -445,6 +428,10 @@
         (),
         work()
         + [
+            *[pltpu.VMEM(w.shape, BF16) for w in weights],
+            pltpu.VMEM(back.shape, BF16),
+            pltpu.VMEM((edges, ORDERS * LANES), F32),
+            pltpu.VMEM((edges, ORDERS * LANES), F32),
             pltpu.VMEM((edges, ORDERS * LANES), F32),
             pltpu.VMEM((edges, ORDERS * LANES), BF16),
             pltpu.VMEM((edges, LANES), F32),
@@ -456,14 +443,14 @@
 
     *far_grads, near_grad, agg_pair = after(*far_grads, near_grad, agg_pair)
     near_home, agg_far = after(swap_near(near_grad), across(agg_pair[atoms:].astype(BF16)))
-    far_home = swap_far(collect(far_grads).astype(BF16)).astype(F32)
     aggregate = agg_pair[:atoms] + agg_far.astype(F32)
     updated = (
         embeddings.astype(F32) + gain[:, None, :] * scale * aggregate.reshape(embeddings.shape)
     ).astype(BF16)
     summed = own_grad.astype(F32) + near_home.astype(F32)
     parts = [summed[2 * atoms * d : 2 * atoms * (d + 1)].astype(BF16) for d in range(4)]
-    grad_pair = collect(parts) + far_home
+    *parts, far_sum = after(*parts, collect(far_grads).astype(BF16))
+    grad_pair = collect(parts) + swap_far(far_sum).astype(F32)
     grad_rows = grad_pair[:atoms] + across(grad_pair[atoms:].astype(BF16)).astype(F32)
     grad_embeddings = cotangent.astype(F32) + grad_rows.reshape(cotangent.shape)
     return (updated, grad_embeddings, grad_basis)

time: 110 us -> 110 us (level)
  waiting for transfers between devices: 23.8 us -> 29.1 us
  starting transfers between devices: 51.8 us -> 46.7 us
  other arithmetic: 5.37 us -> 7.66 us
  local copies, waits for them, and re-layouts: 2.52 us -> 1.31 us
    ppermute x18, waiting for transfers between devices: 14.1 us -> 21.6 us  [shift(): lax.ppermute(v, 'edge', [(s, s // 4 * 4 + (s + k) % 4) for s in range(8)])]
    ppermute x2 -> x0, waiting for transfers between devices: 4.67 us -> none  [roll(): lax.ppermute(v, 'space', [(b, (b + k) % blocks) for b in range(blocks)])]
    ppermute x4, starting transfers between devices: 21.4 us -> 18.4 us  [across(): return lax.ppermute(v, 'edge', [(s, (s + 4) % 8) for s in range(8)])]
    ppermute x4, waiting for transfers between devices: 4.37 us -> 6.69 us  [across(): return lax.ppermute(v, 'edge', [(s, (s + 4) % 8) for s in range(8)])]
    ppermute x2 -> x0, starting transfers between devices: 1.89 us -> none  [roll(): lax.ppermute(v, 'space', [(b, (b + k) % blocks) for b in range(blocks)])]
    another operation x1 -> x3, other arithmetic: 0.18 us -> 1.5 us
    unnamed x23 -> x19, local copies, waits for them, and re-layouts: 2.21 us -> 0.91 us
  transfers between devices with their start and end apart: 28 -> 26, of which waited for: 11 -> 11; matrix products, arithmetic and copies ran while one was open for 5% -> 7% of each run, Pallas kernels for 21% -> 20%
where the time goes in v5:
time: 110 us; the launch traced here: 109 us
  starting transfers between devices  46.7 us (42%)
  waiting for transfers between devices  29.1 us (26%)
  Pallas kernels  22.3 us (20%)
  other arithmetic  7.66 us (7%)
  between operations  1.52 us (1%)
  local copies, waits for them, and re-layouts  1.31 us (1%)
    ppermute x18, starting transfers between devices, shift(): lax.ppermute(v, 'edge', [(s, s // 4 * 4 + (s + k) % 4) for s in range(8)])  26.2 us
    ppermute x18, waiting for transfers between devices, shift(): lax.ppermute(v, 'edge', [(s, s // 4 * 4 + (s + k) % 4) for s in range(8)])  21.6 us
    ppermute x4, starting transfers between devices, across(): return lax.ppermute(v, 'edge', [(s, (s + 4) % 8) for s in range(8)])  18.4 us
    pallas_call x1, Pallas kernels, on_device(): kernel_call(backward_kernel, 9, 8, (whole, whole, piece, piece, piece, pi...  9.49 us
    pallas_call x1, Pallas kernels, on_device(): kernel_call(forward_kernel, 17, 0, (piece, piece, piece, piece, square, k...  8.25 us
    ppermute x4, waiting for transfers between devices, across(): return lax.ppermute(v, 'edge', [(s, (s + 4) % 8) for s in range(8)])  6.69 us
    pallas_call x1, Pallas kernels, on_device(): kernel_call(prep_kernel, 1, 1, (shaped(groups, TURN_ROWS, 256), shaped(gr...  4.58 us
  transfers between devices with their start and end apart: 26, of which 11 were waited for; matrix products, arithmetic and copies ran while one was open for 7% of the time, Pallas kernels for 20%

profile of v5, /device:TPU:8, one launch (start us, length us, event | category | flops | bytes accessed | tf_op | source)
XLA Modules:
  0.0 109.4 jit_solution(17868739220873234117)
XLA Ops:
  0.6 0.0 copy-start
  0.6 7.3 %collective-permute-start = (bf16[8,6272]{1,0:T(8,128)(2,1)}, bf16[8,6272]{1,0:T(8,128)(2,1)S(1)}, u32[]{:S(2)}, u32[]{:S(2)}) collective-permute-start(bf16[8,6272]{1,0:T(8,128)(2,1)} %bitcast.29), channel_id=1, source_target_pairs={{0,4},{1,5},{2,6},{3,7},{4,0},{5,1},{6,2},{7,3},{8,12},{9,13},{10,... | collective-permute-start | bytes 301064 | tf_op jit(solution)/shard_map/ppermute | solution.py:309
  7.9 0.8 broadcast_multiply_fusion
  8.8 0.9 fusion.5
  9.7 0.8 collective-permute-start.5
  10.5 0.7 convert.18
  11.2 0.7 convert.19
  12.5 0.1 fusion.11
  12.6 0.0 collective-permute-done
  12.6 0.9 pad_maximum_fusion.first
  13.5 1.5 %collective-permute-start.1 = (bf16[16,6400]{1,0:T(8,128)(2,1)S(1)}, bf16[16,6400]{1,0:T(8,128)(2,1)S(1)}, u32[]{:S(2)}, u32[]{:S(2)}) collective-permute-start(bf16[16,6400]{1,0:T(8,128)(2,1)S(1)} %pad_maximum_fusion.first), channel_id=1, source_target_pairs={{0,248},{8,16},{16,8},{24,32},{32,24},{40,48},{48,40},{56,64},{64,... | collective-permute-start | bytes 614408 | tf_op jit(solution)/shard_map/ppermute | solution.py:318
  15.0 3.0 %collective-permute-start.10 = (bf16[16,6400]{1,0:T(8,128)(2,1)S(1)}, bf16[16,6400]{1,0:T(8,128)(2,1)S(1)}, u32[]{:S(2)}, u32[]{:S(2)}) collective-permute-start(bf16[16,6400]{1,0:T(8,128)(2,1)S(1)} %pad_maximum_fusion.first), channel_id=1, source_target_pairs={{0,2},{1,3},{2,0},{3,1},{4,6},{5,7},{6,4},{7,5},{8,10},{9,11},{10,... | collective-permute-start | bytes 614408 | tf_op jit(solution)/shard_map/ppermute | solution.py:312
  18.0 0.6 collective-permute-start.11
  18.6 2.6 %collective-permute-start.9 = (bf16[16,6400]{1,0:T(8,128)(2,1)S(1)}, bf16[16,6400]{1,0:T(8,128)(2,1)S(1)}, u32[]{:S(2)}, u32[]{:S(2)}) collective-permute-start(bf16[16,6400]{1,0:T(8,128)(2,1)S(1)} %pad_maximum_fusion.first), channel_id=1, source_target_pairs={{0,3},{1,0},{2,1},{3,2},{4,7},{5,4},{6,5},{7,6},{8,11},{9,8},{10,9... | collective-permute-start | bytes 614408 | tf_op jit(solution)/shard_map/ppermute | solution.py:312
  21.2 0.7 fusion.38.tgt
  21.9 0.7 fusion.39
  22.6 0.1 copy.23.tgt
  22.7 0.8 copy-done.1
  23.6 4.6 %shard_map.184 = (bf16[8,464,256]{2,1,0:T(8,128)(2,1)S(1)}, bf16[8,784,256]{2,1,0:T(8,128)(2,1)}) custom-call(bf16[235,128]{1,0:T(8,128)(2,1)S(1)} %copy-done.1, bf16[16,6400]{1,0:T(8,128)(2,1)S(1)} %pad_maximum_fusion.first), custom_call_target="tpu_custom_call" | custom-call | flops 2000000000 | bytes 6000000 | tf_op jit(solution)/shard_map/pallas_call | solution.py:348
  28.2 0.1 collective-permute-start.2
  28.3 1.4 %collective-permute-start.3 = (bf16[16,6400]{1,0:T(8,128)(2,1)S(1)}, bf16[16,6400]{1,0:T(8,128)(2,1)S(1)}, u32[]{:S(2)}, u32[]{:S(2)}) collective-permute-start(bf16[16,6400]{1,0:T(8,128)(2,1)S(1)} %collective-permute-done.1.far0), channel_id=1, source_target_pairs={{0,2},{1,3},{2,0},{3,1},{4,6},{5,7},{6,4},{7,5},{8,10},{9,11},{10,... | collective-permute-start | bytes 614408 | tf_op jit(solution)/shard_map/ppermute | solution.py:312
  29.7 0.7 collective-permute-start.4
  30.4 0.6 collective-permute-start.12
  31.0 5.1 %collective-permute-done.2.far1 = bf16[16,6400]{1,0:T(8,128)(2,1)S(1)} collective-permute-done((bf16[16,6400]{1,0:T(8,128)(2,1)S(1)}, bf16[16,6400]{1,0:T(8,128)(2,1)S(1)}, u32[]{:S(2)}, u32[]{:S(2)}) %collective-permute-start.2) | collective-permute-done | bytes 204832 | tf_op jit(solution)/shard_map/ppermute | solution.py:312
  36.1 1.7 %collective-permute-done.3.far2 = bf16[16,6400]{1,0:T(8,128)(2,1)S(1)} collective-permute-done((bf16[16,6400]{1,0:T(8,128)(2,1)S(1)}, bf16[16,6400]{1,0:T(8,128)(2,1)S(1)}, u32[]{:S(2)}, u32[]{:S(2)}) %collective-permute-start.3) | collective-permute-done | bytes 204832 | tf_op jit(solution)/shard_map/ppermute | solution.py:312
  37.8 4.3 %collective-permute-done.4.far3 = bf16[16,6400]{1,0:T(8,128)(2,1)S(1)} collective-permute-done((bf16[16,6400]{1,0:T(8,128)(2,1)S(1)}, bf16[16,6400]{1,0:T(8,128)(2,1)S(1)}, u32[]{:S(2)}, u32[]{:S(2)}) %collective-permute-start.4) | collective-permute-done | bytes 204832 | tf_op jit(solution)/shard_map/ppermute | solution.py:312
  42.2 0.9 pad_maximum_fusion.1.up0
  43.1 1.1 collective-permute-start.6
  44.2 0.7 collective-permute-start.7
  44.9 0.8 collective-permute-start.8
  45.7 0.1 slice_bitcast_fusion
  45.8 0.1 pad_add_fusion
  45.9 0.1 select_reduce_fusion
  46.0 0.1 copy.22.src
  46.2 8.3 %shard_map.185 = (bf16[16,6272]{1,0:T(8,128)(2,1)S(1)}, bf16[16,6272]{1,0:T(8,128)(2,1)S(1)}, bf16[16,6272]{1,0:T(8,128)(2,1)S(1)}, bf16[16,6272]{1,0:T(8,128)(2...) custom-call(bf16[64,6400]{1,0:T(8,128)(2,1)S(1)} %constant_dynamic-update-slice_fusion.own, ...), custom_call_target="tpu_custom_call" | custom-call | flops 4000000000 | bytes 20000000 | tf_op jit(solution)/shard_map/pallas_call | solution.py:408
  54.4 1.9 %collective-permute-start.13 = (bf16[16,6272]{1,0:T(8,128)(2,1)S(1)}, bf16[16,6272]{1,0:T(8,128)(2,1)S(1)}, u32[]{:S(2)}, u32[]{:S(2)}) collective-permute-start(bf16[16,6272]{1,0:T(8,128)(2,1)S(1)} %get-tuple-element.73), channel_id=1, source_target_pairs={{0,1},{1,2},{2,3},{3,0},{4,5},{5,6},{6,7},{7,4},{8,9},{9,10},{10,1... | collective-permute-start | bytes 602120 | tf_op jit(solution)/shard_map/ppermute | solution.py:312
  56.4 1.9 %collective-permute-start.14 = (bf16[16,6272]{1,0:T(8,128)(2,1)S(1)}, bf16[16,6272]{1,0:T(8,128)(2,1)S(1)}, u32[]{:S(2)}, u32[]{:S(2)}) collective-permute-start(bf16[16,6272]{1,0:T(8,128)(2,1)S(1)} %get-tuple-element.74), channel_id=1, source_target_pairs={{0,2},{1,3},{2,0},{3,1},{4,6},{5,7},{6,4},{7,5},{8,10},{9,11},{10,... | collective-permute-start | bytes 602120 | tf_op jit(solution)/shard_map/ppermute | solution.py:312
  58.3 2.4 %collective-permute-start.15 = (bf16[16,6272]{1,0:T(8,128)(2,1)S(1)}, bf16[16,6272]{1,0:T(8,128)(2,1)S(1)}, u32[]{:S(2)}, u32[]{:S(2)}) collective-permute-start(bf16[16,6272]{1,0:T(8,128)(2,1)S(1)} %get-tuple-element.75), channel_id=1, source_target_pairs={{0,3},{1,0},{2,1},{3,2},{4,7},{5,4},{6,5},{7,6},{8,11},{9,8},{10,9... | collective-permute-start | bytes 602120 | tf_op jit(solution)/shard_map/ppermute | solution.py:312
  60.7 9.5 %shard_map.186 = (bf16[64,6272]{1,0:T(8,128)(2,1)S(1)}, bf16[64,6272]{1,0:T(8,128)(2,1)S(1)}, bf16[16,6272]{1,0:T(8,128)(2,1)S(1)}, bf16[16,6272]{1,0:T(8,128)(2...) custom-call(bf16[16,6272]{1,0:T(8,128)(2,1)S(1)} %pad_maximum_fusion.1.up0, ...), custom_call_target="tpu_custom_call" | custom-call | flops 5000000000 | bytes 20000000 | tf_op jit(solution)/shard_map/pallas_call | solution.py:423
  70.2 0.1 convert_add_fusion.1
  70.3 0.1 collective-permute-start.18
  70.4 1.5 %collective-permute-start.19 = (bf16[16,6272]{1,0:T(8,128)(2,1)S(1)}, bf16[16,6272]{1,0:T(8,128)(2,1)S(1)}, u32[]{:S(2)}, u32[]{:S(2)}) collective-permute-start(bf16[16,6272]{1,0:T(8,128)(2,1)S(1)} %get-tuple-element.83), channel_id=1, source_target_pairs={{0,2},{1,3},{2,0},{3,1},{4,6},{5,7},{6,4},{7,5},{8,10},{9,11},{10,... | collective-permute-start | bytes 602120 | tf_op jit(solution)/shard_map/ppermute | solution.py:312
  71.9 1.7 %collective-permute-start.20 = (bf16[16,6272]{1,0:T(8,128)(2,1)S(1)}, bf16[16,6272]{1,0:T(8,128)(2,1)S(1)}, u32[]{:S(2)}, u32[]{:S(2)}) collective-permute-start(bf16[16,6272]{1,0:T(8,128)(2,1)S(1)} %get-tuple-element.84), channel_id=1, source_target_pairs={{0,3},{1,0},{2,1},{3,2},{4,7},{5,4},{6,5},{7,6},{8,11},{9,8},{10,9... | collective-permute-start | bytes 602120 | tf_op jit(solution)/shard_map/ppermute | solution.py:312
  73.6 5.0 %collective-permute-start.17 = (bf16[8,6272]{1,0:T(8,128)(2,1)S(1)}, bf16[8,6272]{1,0:T(8,128)(2,1)S(1)}, u32[]{:S(2)}, u32[]{:S(2)}) collective-permute-start(bf16[8,6272]{1,0:T(8,128)(2,1)S(1)} %slice.88), channel_id=1, source_target_pairs={{0,4},{1,5},{2,6},{3,7},{4,0},{5,1},{6,2},{7,3},{8,12},{9,13},{10,... | collective-permute-start | bytes 301064 | tf_op jit(solution)/shard_map/ppermute | solution.py:309
  78.6 2.6 %collective-permute-done.18 = bf16[16,6272]{1,0:T(8,128)(2,1)S(1)} collective-permute-done((bf16[16,6272]{1,0:T(8,128)(2,1)S(1)}, bf16[16,6272]{1,0:T(8,128)(2,1)S(1)}, u32[]{:S(2)}, u32[]{:S(2)}) %collective-permute-start.18) | collective-permute-done | bytes 200736 | tf_op jit(solution)/shard_map/ppermute | solution.py:312
  81.2 0.6 collective-permute-done.20
  81.8 0.1 add_convert_fusion.1
  81.9 0.9 collective-permute-done.17
  82.9 0.2 add_convert_fusion
  83.1 0.0 copy-start.6
  83.1 0.0 copy-start.5
  83.1 0.1 fusion.36
  83.2 0.9 collective-permute-start.21
  84.1 2.2 %collective-permute-start.22 = (bf16[16,6272]{1,0:T(8,128)(2,1)S(1)}, bf16[16,6272]{1,0:T(8,128)(2,1)S(1)}, u32[]{:S(2)}, u32[]{:S(2)}) collective-permute-start(bf16[16,6272]{1,0:T(8,128)(2,1)S(1)} %get-tuple-element.87), channel_id=1, source_target_pairs={{0,2},{1,3},{2,0},{3,1},{4,6},{5,7},{6,4},{7,5},{8,10},{9,11},{10,... | collective-permute-start | bytes 602120 | tf_op jit(solution)/shard_map/ppermute | solution.py:312
  86.3 2.5 %collective-permute-start.23 = (bf16[16,6272]{1,0:T(8,128)(2,1)S(1)}, bf16[16,6272]{1,0:T(8,128)(2,1)S(1)}, u32[]{:S(2)}, u32[]{:S(2)}) collective-permute-start(bf16[16,6272]{1,0:T(8,128)(2,1)S(1)} %get-tuple-element.88), channel_id=1, source_target_pairs={{0,3},{1,0},{2,1},{3,2},{4,7},{5,4},{6,5},{7,6},{8,11},{9,8},{10,9... | collective-permute-start | bytes 602120 | tf_op jit(solution)/shard_map/ppermute | solution.py:312
  88.8 3.2 %collective-permute-done.21 = bf16[16,6272]{1,0:T(8,128)(2,1)S(1)} collective-permute-done((bf16[16,6272]{1,0:T(8,128)(2,1)S(1)}, bf16[16,6272]{1,0:T(8,128)(2,1)S(1)}, u32[]{:S(2)}, u32[]{:S(2)}) %collective-permute-start.21) | collective-permute-done | bytes 200736 | tf_op jit(solution)/shard_map/ppermute | solution.py:312
  92.0 3.3 %collective-permute-done.22 = bf16[16,6272]{1,0:T(8,128)(2,1)S(1)} collective-permute-done((bf16[16,6272]{1,0:T(8,128)(2,1)S(1)}, bf16[16,6272]{1,0:T(8,128)(2,1)S(1)}, u32[]{:S(2)}, u32[]{:S(2)}) %collective-permute-start.22) | collective-permute-done | bytes 200736 | tf_op jit(solution)/shard_map/ppermute | solution.py:312
  95.4 0.6 collective-permute-done.23
  95.9 0.8 collective-permute-done.24
  96.8 0.1 convert_add_fusion
  96.9 5.4 %collective-permute-start.25 = (bf16[8,6272]{1,0:T(8,128)(2,1)S(1)}, bf16[8,6272]{1,0:T(8,128)(2,1)S(1)}, u32[]{:S(2)}, u32[]{:S(2)}) collective-permute-start(bf16[8,6272]{1,0:T(8,128)(2,1)S(1)} %slice.87), channel_id=1, source_target_pairs={{0,4},{1,5},{2,6},{3,7},{4,0},{5,1},{6,2},{7,3},{8,12},{9,13},{10,... | collective-permute-start | bytes 301064 | tf_op jit(solution)/shard_map/ppermute | solution.py:309
  102.3 0.7 fusion.4
  103.0 5.7 %collective-permute-done.25 = bf16[8,6272]{1,0:T(8,128)(2,1)S(1)} collective-permute-done((bf16[8,6272]{1,0:T(8,128)(2,1)S(1)}, bf16[8,6272]{1,0:T(8,128)(2,1)S(1)}, u32[]{:S(2)}, u32[]{:S(2)}) %collective-permute-start.25) | collective-permute-done | bytes 100384 | tf_op jit(solution)/shard_map/ppermute | solution.py:309
  108.7 0.7 convert_add_fusion.2
  (37 shorter events, 0.2 us)
Async XLA Ops:
  0.6 7.3 %copy-start = (f32[100,128]{1,0:T(8,128)S(1)}, f32[100,128]{1,0:T(8,128)}, u32[]{:S(2)}) copy-start(f32[100,128]{1,0:T(8,128)} %param.19) | copy-start | bytes 153604
  0.6 11.9 %collective-permute-start = (bf16[8,6272]{1,0:T(8,128)(2,1)}, bf16[8,6272]{1,0:T(8,128)(2,1)S(1)}, u32[]{:S(2)}, u32[]{:S(2)}) collective-permute-start(bf16[8,6272]{1,0:T(8,128)(2,1)} %bitcast.29), channel_id=1, source_target_pairs={{0,4},{1,5},{2,6},{3,7},{4,0},{5,1},{6,2},{7,3},{8,12},{9,13},{10,... | collective-permute-start | bytes 301064 | tf_op jit(solution)/shard_map/ppermute | solution.py:309
  9.7 21.3 %collective-permute-start.5 = (bf16[8,6272]{1,0:T(8,128)(2,1)S(1)}, bf16[8,6272]{1,0:T(8,128)(2,1)}, u32[]{:S(2)}, u32[]{:S(2)}) collective-permute-start(bf16[8,6272]{1,0:T(8,128)(2,1)S(1)} %fusion.5), channel_id=1, source_target_pairs={{0,4},{1,5},{2,6},{3,7},{4,0},{5,1},{6,2},{7,3},{8,12},{9,13},{10,... | collective-permute-start | bytes 301064 | tf_op jit(solution)/shard_map/ppermute | solution.py:309
  13.5 14.7 %collective-permute-start.1 = (bf16[16,6400]{1,0:T(8,128)(2,1)S(1)}, bf16[16,6400]{1,0:T(8,128)(2,1)S(1)}, u32[]{:S(2)}, u32[]{:S(2)}) collective-permute-start(bf16[16,6400]{1,0:T(8,128)(2,1)S(1)} %pad_maximum_fusion.first), channel_id=1, source_target_pairs={{0,248},{8,16},{16,8},{24,32},{32,24},{40,48},{48,40},{56,64},{64,... | collective-permute-start | bytes 614408 | tf_op jit(solution)/shard_map/ppermute | solution.py:318
  15.0 13.3 %collective-permute-start.10 = (bf16[16,6400]{1,0:T(8,128)(2,1)S(1)}, bf16[16,6400]{1,0:T(8,128)(2,1)S(1)}, u32[]{:S(2)}, u32[]{:S(2)}) collective-permute-start(bf16[16,6400]{1,0:T(8,128)(2,1)S(1)} %pad_maximum_fusion.first), channel_id=1, source_target_pairs={{0,2},{1,3},{2,0},{3,1},{4,6},{5,7},{6,4},{7,5},{8,10},{9,11},{10,... | collective-permute-start | bytes 614408 | tf_op jit(solution)/shard_map/ppermute | solution.py:312
  18.0 11.7 %collective-permute-start.11 = (bf16[16,6400]{1,0:T(8,128)(2,1)S(1)}, bf16[16,6400]{1,0:T(8,128)(2,1)S(1)}, u32[]{:S(2)}, u32[]{:S(2)}) collective-permute-start(bf16[16,6400]{1,0:T(8,128)(2,1)S(1)} %pad_maximum_fusion.first), channel_id=1, source_target_pairs={{0,1},{1,2},{2,3},{3,0},{4,5},{5,6},{6,7},{7,4},{8,9},{9,10},{10,1... | collective-permute-start | bytes 614408 | tf_op jit(solution)/shard_map/ppermute | solution.py:312
  18.6 11.8 %collective-permute-start.9 = (bf16[16,6400]{1,0:T(8,128)(2,1)S(1)}, bf16[16,6400]{1,0:T(8,128)(2,1)S(1)}, u32[]{:S(2)}, u32[]{:S(2)}) collective-permute-start(bf16[16,6400]{1,0:T(8,128)(2,1)S(1)} %pad_maximum_fusion.first), channel_id=1, source_target_pairs={{0,3},{1,0},{2,1},{3,2},{4,7},{5,4},{6,5},{7,6},{8,11},{9,8},{10,9... | collective-permute-start | bytes 614408 | tf_op jit(solution)/shard_map/ppermute | solution.py:312
  22.7 0.8 copy-start.1
  28.1 17.9 %copy-start.4 = (bf16[8,464,256]{2,1,0:T(8,128)(2,1)}, bf16[8,464,256]{2,1,0:T(8,128)(2,1)S(1)}, u32[]{:S(2)}) copy-start(bf16[8,464,256]{2,1,0:T(8,128)(2,1)S(1)} %get-tuple-element.58.turn) | copy-start | bytes 5701636
  28.1 2.9 %copy-start.7 = (s32[128]{0:T(128)S(1)}, s32[128]{0:T(128)}, u32[]{:S(2)}) copy-start(s32[128]{0:T(128)} %param.20) | copy-start | bytes 1540
  28.1 18.0 %copy-start.2 = (bf16[128,128]{1,0:T(8,128)(2,1)S(1)}, bf16[128,128]{1,0:T(8,128)(2,1)}, u32[]{:S(2)}) copy-start(bf16[128,128]{1,0:T(8,128)(2,1)} %basis.1) | copy-start | bytes 98308
  28.1 18.0 %copy-start.3 = (bf16[128,128]{1,0:T(8,128)(2,1)S(1)}, bf16[128,128]{1,0:T(8,128)(2,1)}, u32[]{:S(2)}) copy-start(bf16[128,128]{1,0:T(8,128)(2,1)} %w_rad.3) | copy-start | bytes 98308
  28.2 8.0 %collective-permute-start.2 = (bf16[16,6400]{1,0:T(8,128)(2,1)S(1)}, bf16[16,6400]{1,0:T(8,128)(2,1)S(1)}, u32[]{:S(2)}, u32[]{:S(2)}) collective-permute-start(bf16[16,6400]{1,0:T(8,128)(2,1)S(1)} %collective-permute-done.1.far0), channel_id=1, source_target_pairs={{0,3},{1,0},{2,1},{3,2},{4,7},{5,4},{6,5},{7,6},{8,11},{9,8},{10,9... | collective-permute-start | bytes 614408 | tf_op jit(solution)/shard_map/ppermute | solution.py:312
  28.3 9.6 %collective-permute-start.3 = (bf16[16,6400]{1,0:T(8,128)(2,1)S(1)}, bf16[16,6400]{1,0:T(8,128)(2,1)S(1)}, u32[]{:S(2)}, u32[]{:S(2)}) collective-permute-start(bf16[16,6400]{1,0:T(8,128)(2,1)S(1)} %collective-permute-done.1.far0), channel_id=1, source_target_pairs={{0,2},{1,3},{2,0},{3,1},{4,6},{5,7},{6,4},{7,5},{8,10},{9,11},{10,... | collective-permute-start | bytes 614408 | tf_op jit(solution)/shard_map/ppermute | solution.py:312
  29.7 12.5 %collective-permute-start.4 = (bf16[16,6400]{1,0:T(8,128)(2,1)S(1)}, bf16[16,6400]{1,0:T(8,128)(2,1)S(1)}, u32[]{:S(2)}, u32[]{:S(2)}) collective-permute-start(bf16[16,6400]{1,0:T(8,128)(2,1)S(1)} %collective-permute-done.1.far0), channel_id=1, source_target_pairs={{0,1},{1,2},{2,3},{3,0},{4,5},{5,6},{6,7},{7,4},{8,9},{9,10},{10,1... | collective-permute-start | bytes 614408 | tf_op jit(solution)/shard_map/ppermute | solution.py:312
  30.4 15.3 %collective-permute-start.12 = (bf16[64,6400]{1,0:T(8,128)(2,1)S(1)}, bf16[64,6400]{1,0:T(8,128)(2,1)S(1)}, u32[]{:S(2)}, u32[]{:S(2)}) collective-permute-start(bf16[64,6400]{1,0:T(8,128)(2,1)S(1)} %constant_dynamic-update-slice_fusion.own), channel_id=1, source_target_pairs={{0,8},{8,0},{16,24},{24,16},{32,40},{40,32},{48,56},{56,48},{64,72... | collective-permute-start | bytes 2457608 | tf_op jit(solution)/shard_map/ppermute | solution.py:315
  43.1 15.2 %collective-permute-start.6 = (bf16[16,6272]{1,0:T(8,128)(2,1)S(1)}, bf16[16,6272]{1,0:T(8,128)(2,1)S(1)}, u32[]{:S(2)}, u32[]{:S(2)}) collective-permute-start(bf16[16,6272]{1,0:T(8,128)(2,1)S(1)} %pad_maximum_fusion.1.up0), channel_id=1, source_target_pairs={{0,3},{1,0},{2,1},{3,2},{4,7},{5,4},{6,5},{7,6},{8,11},{9,8},{10,9... | collective-permute-start | bytes 602120 | tf_op jit(solution)/shard_map/ppermute | solution.py:312
  44.2 16.5 %collective-permute-start.7 = (bf16[16,6272]{1,0:T(8,128)(2,1)S(1)}, bf16[16,6272]{1,0:T(8,128)(2,1)S(1)}, u32[]{:S(2)}, u32[]{:S(2)}) collective-permute-start(bf16[16,6272]{1,0:T(8,128)(2,1)S(1)} %pad_maximum_fusion.1.up0), channel_id=1, source_target_pairs={{0,2},{1,3},{2,0},{3,1},{4,6},{5,7},{6,4},{7,5},{8,10},{9,11},{10,... | collective-permute-start | bytes 602120 | tf_op jit(solution)/shard_map/ppermute | solution.py:312
  44.9 15.8 %collective-permute-start.8 = (bf16[16,6272]{1,0:T(8,128)(2,1)S(1)}, bf16[16,6272]{1,0:T(8,128)(2,1)S(1)}, u32[]{:S(2)}, u32[]{:S(2)}) collective-permute-start(bf16[16,6272]{1,0:T(8,128)(2,1)S(1)} %pad_maximum_fusion.1.up0), channel_id=1, source_target_pairs={{0,1},{1,2},{2,3},{3,0},{4,5},{5,6},{6,7},{7,4},{8,9},{9,10},{10,1... | collective-permute-start | bytes 602120 | tf_op jit(solution)/shard_map/ppermute | solution.py:312
  54.4 15.8 %collective-permute-start.13 = (bf16[16,6272]{1,0:T(8,128)(2,1)S(1)}, bf16[16,6272]{1,0:T(8,128)(2,1)S(1)}, u32[]{:S(2)}, u32[]{:S(2)}) collective-permute-start(bf16[16,6272]{1,0:T(8,128)(2,1)S(1)} %get-tuple-element.73), channel_id=1, source_target_pairs={{0,1},{1,2},{2,3},{3,0},{4,5},{5,6},{6,7},{7,4},{8,9},{9,10},{10,1... | collective-permute-start | bytes 602120 | tf_op jit(solution)/shard_map/ppermute | solution.py:312
  56.4 13.8 %collective-permute-start.14 = (bf16[16,6272]{1,0:T(8,128)(2,1)S(1)}, bf16[16,6272]{1,0:T(8,128)(2,1)S(1)}, u32[]{:S(2)}, u32[]{:S(2)}) collective-permute-start(bf16[16,6272]{1,0:T(8,128)(2,1)S(1)} %get-tuple-element.74), channel_id=1, source_target_pairs={{0,2},{1,3},{2,0},{3,1},{4,6},{5,7},{6,4},{7,5},{8,10},{9,11},{10,... | collective-permute-start | bytes 602120 | tf_op jit(solution)/shard_map/ppermute | solution.py:312
  58.3 11.9 %collective-permute-start.15 = (bf16[16,6272]{1,0:T(8,128)(2,1)S(1)}, bf16[16,6272]{1,0:T(8,128)(2,1)S(1)}, u32[]{:S(2)}, u32[]{:S(2)}) collective-permute-start(bf16[16,6272]{1,0:T(8,128)(2,1)S(1)} %get-tuple-element.75), channel_id=1, source_target_pairs={{0,3},{1,0},{2,1},{3,2},{4,7},{5,4},{6,5},{7,6},{8,11},{9,8},{10,9... | collective-permute-start | bytes 602120 | tf_op jit(solution)/shard_map/ppermute | solution.py:312
  70.3 10.9 %collective-permute-start.18 = (bf16[16,6272]{1,0:T(8,128)(2,1)S(1)}, bf16[16,6272]{1,0:T(8,128)(2,1)S(1)}, u32[]{:S(2)}, u32[]{:S(2)}) collective-permute-start(bf16[16,6272]{1,0:T(8,128)(2,1)S(1)} %get-tuple-element.82), channel_id=1, source_target_pairs={{0,1},{1,2},{2,3},{3,0},{4,5},{5,6},{6,7},{7,4},{8,9},{9,10},{10,1... | collective-permute-start | bytes 602120 | tf_op jit(solution)/shard_map/ppermute | solution.py:312
  70.4 10.8 %collective-permute-start.19 = (bf16[16,6272]{1,0:T(8,128)(2,1)S(1)}, bf16[16,6272]{1,0:T(8,128)(2,1)S(1)}, u32[]{:S(2)}, u32[]{:S(2)}) collective-permute-start(bf16[16,6272]{1,0:T(8,128)(2,1)S(1)} %get-tuple-element.83), channel_id=1, source_target_pairs={{0,2},{1,3},{2,0},{3,1},{4,6},{5,7},{6,4},{7,5},{8,10},{9,11},{10,... | collective-permute-start | bytes 602120 | tf_op jit(solution)/shard_map/ppermute | solution.py:312
  71.9 9.9 %collective-permute-start.20 = (bf16[16,6272]{1,0:T(8,128)(2,1)S(1)}, bf16[16,6272]{1,0:T(8,128)(2,1)S(1)}, u32[]{:S(2)}, u32[]{:S(2)}) collective-permute-start(bf16[16,6272]{1,0:T(8,128)(2,1)S(1)} %get-tuple-element.84), channel_id=1, source_target_pairs={{0,3},{1,0},{2,1},{3,2},{4,7},{5,4},{6,5},{7,6},{8,11},{9,8},{10,9... | collective-permute-start | bytes 602120 | tf_op jit(solution)/shard_map/ppermute | solution.py:312
  73.6 9.3 %collective-permute-start.16 = (bf16[64,6272]{1,0:T(8,128)(2,1)S(1)}, bf16[64,6272]{1,0:T(8,128)(2,1)S(1)}, u32[]{:S(2)}, u32[]{:S(2)}) collective-permute-start(bf16[64,6272]{1,0:T(8,128)(2,1)S(1)} %get-tuple-element.77), channel_id=1, source_target_pairs={{0,8},{8,0},{16,24},{24,16},{32,40},{40,32},{48,56},{56,48},{64,72... | collective-permute-start | bytes 2408456 | tf_op jit(solution)/shard_map/ppermute | solution.py:315
  73.6 9.2 %collective-permute-start.17 = (bf16[8,6272]{1,0:T(8,128)(2,1)S(1)}, bf16[8,6272]{1,0:T(8,128)(2,1)S(1)}, u32[]{:S(2)}, u32[]{:S(2)}) collective-permute-start(bf16[8,6272]{1,0:T(8,128)(2,1)S(1)} %slice.88), channel_id=1, source_target_pairs={{0,4},{1,5},{2,6},{3,7},{4,0},{5,1},{6,2},{7,3},{8,12},{9,13},{10,... | collective-permute-start | bytes 301064 | tf_op jit(solution)/shard_map/ppermute | solution.py:309
  83.1 19.2 %copy-start.6 = (bf16[8,49,128]{2,0,1:T(8,128)(2,1)S(1)}, bf16[8,49,128]{2,0,1:T(8,128)(2,1)}, u32[]{:S(2)}) copy-start(bf16[8,49,128]{2,0,1:T(8,128)(2,1)} %param.17) | copy-start | bytes 301060
  83.1 25.6 %copy-start.5 = (bf16[8,49,128]{2,0,1:T(8,128)(2,1)S(1)}, bf16[8,49,128]{2,0,1:T(8,128)(2,1)}, u32[]{:S(2)}) copy-start(bf16[8,49,128]{2,0,1:T(8,128)(2,1)} %param.33) | copy-start | bytes 301060
  83.2 8.9 %collective-permute-start.21 = (bf16[16,6272]{1,0:T(8,128)(2,1)S(1)}, bf16[16,6272]{1,0:T(8,128)(2,1)S(1)}, u32[]{:S(2)}, u32[]{:S(2)}) collective-permute-start(bf16[16,6272]{1,0:T(8,128)(2,1)S(1)} %get-tuple-element.86), channel_id=1, source_target_pairs={{0,1},{1,2},{2,3},{3,0},{4,5},{5,6},{6,7},{7,4},{8,9},{9,10},{10,1... | collective-permute-start | bytes 602120 | tf_op jit(solution)/shard_map/ppermute | solution.py:312
  84.1 11.3 %collective-permute-start.22 = (bf16[16,6272]{1,0:T(8,128)(2,1)S(1)}, bf16[16,6272]{1,0:T(8,128)(2,1)S(1)}, u32[]{:S(2)}, u32[]{:S(2)}) collective-permute-start(bf16[16,6272]{1,0:T(8,128)(2,1)S(1)} %get-tuple-element.87), channel_id=1, source_target_pairs={{0,2},{1,3},{2,0},{3,1},{4,6},{5,7},{6,4},{7,5},{8,10},{9,11},{10,... | collective-permute-start | bytes 602120 | tf_op jit(solution)/shard_map/ppermute | solution.py:312
  86.3 9.7 %collective-permute-start.23 = (bf16[16,6272]{1,0:T(8,128)(2,1)S(1)}, bf16[16,6272]{1,0:T(8,128)(2,1)S(1)}, u32[]{:S(2)}, u32[]{:S(2)}) collective-permute-start(bf16[16,6272]{1,0:T(8,128)(2,1)S(1)} %get-tuple-element.88), channel_id=1, source_target_pairs={{0,3},{1,0},{2,1},{3,2},{4,7},{5,4},{6,5},{7,6},{8,11},{9,8},{10,9... | collective-permute-start | bytes 602120 | tf_op jit(solution)/shard_map/ppermute | solution.py:312
  88.8 8.0 %collective-permute-start.24 = (bf16[16,6272]{1,0:T(8,128)(2,1)S(1)}, bf16[16,6272]{1,0:T(8,128)(2,1)S(1)}, u32[]{:S(2)}, u32[]{:S(2)}) collective-permute-start(bf16[16,6272]{1,0:T(8,128)(2,1)S(1)} %add_convert_fusion.1), channel_id=1, source_target_pairs={{0,248},{8,16},{16,8},{24,32},{32,24},{40,48},{48,40},{56,64},{64,... | collective-permute-start | bytes 602120 | tf_op jit(solution)/shard_map/ppermute | solution.py:318
  96.9 11.8 %collective-permute-start.25 = (bf16[8,6272]{1,0:T(8,128)(2,1)S(1)}, bf16[8,6272]{1,0:T(8,128)(2,1)S(1)}, u32[]{:S(2)}, u32[]{:S(2)}) collective-permute-start(bf16[8,6272]{1,0:T(8,128)(2,1)S(1)} %slice.87), channel_id=1, source_target_pairs={{0,4},{1,5},{2,6},{3,7},{4,0},{5,1},{6,2},{7,3},{8,12},{9,13},{10,... | collective-permute-start | bytes 301064 | tf_op jit(solution)/shard_map/ppermute | solution.py:309

commit v6 on v5

--- a/solution.py
+++ b/solution.py
@@ -331,8 +331,8 @@
 
     flat = embeddings.reshape(atoms, WIDE)
     halo = send_left.shape[1]
-    lists = jnp.concatenate([send_left, send_right], axis=1).astype(BF16)
-    lists = jnp.pad(lists, ((0, 2 * atoms - 1), (0, LANES - 2 * halo)))
+    lists = jnp.concatenate([send_left, send_right], axis=1)
+    lists = jnp.pad(lists, ((0, 2 * atoms - 1), (0, LANES - 2 * halo))).astype(BF16)
     pair = jnp.concatenate([jnp.concatenate([flat, across(flat)], axis=0), lists], axis=1)
     gain = jnp.dot(
         (species[:, None] == lax.iota(jnp.int32, species_gain.shape[0])[None, :]).astype(F32),
@@ -442,7 +442,7 @@
     )(*up_pieces, tgt_col, src_row, turn, pre, weight_radial, outs, *weights, turned, back)
 
     *far_grads, near_grad, agg_pair = after(*far_grads, near_grad, agg_pair)
-    near_home, agg_far = after(swap_near(near_grad), across(agg_pair[atoms:].astype(BF16)))
+    near_home, agg_far = swap_near(near_grad), across(agg_pair[atoms:].astype(BF16))
     aggregate = agg_pair[:atoms] + agg_far.astype(F32)
     updated = (
         embeddings.astype(F32) + gain[:, None, :] * scale * aggregate.reshape(embeddings.shape)

time: 110 us -> 108 us (0.982)
  starting transfers between devices: 46.7 us -> 43.8 us
    ppermute x18, starting transfers between devices: 26.2 us -> 24.5 us  [shift(): lax.ppermute(v, 'edge', [(s, s // 4 * 4 + (s + k) % 4) for s in range(8)])]
    ppermute x18, waiting for transfers between devices: 21.6 us -> 22.9 us  [shift(): lax.ppermute(v, 'edge', [(s, s // 4 * 4 + (s + k) % 4) for s in range(8)])]
    ppermute x4, starting transfers between devices: 18.4 us -> 17.2 us  [across(): return lax.ppermute(v, 'edge', [(s, (s + 4) % 8) for s in range(8)])]
  transfers between devices with their start and end apart: 26 -> 26, of which waited for: 11 -> 8; matrix products, arithmetic and copies ran while one was open for 7% -> 7% of each run, Pallas kernels for 20% -> 21%
where the time goes in v6:
time: 108 us; the launch traced here: 107 us
  starting transfers between devices  43.8 us (41%)
  waiting for transfers between devices  29.6 us (27%)
  Pallas kernels  22.3 us (21%)
  other arithmetic  7.66 us (7%)
  between operations  1.53 us (1%)
  local copies, waits for them, and re-layouts  1.31 us (1%)
    ppermute x18, starting transfers between devices, shift(): lax.ppermute(v, 'edge', [(s, s // 4 * 4 + (s + k) % 4) for s in range(8)])  24.5 us
    ppermute x18, waiting for transfers between devices, shift(): lax.ppermute(v, 'edge', [(s, s // 4 * 4 + (s + k) % 4) for s in range(8)])  22.9 us
    ppermute x4, starting transfers between devices, across(): return lax.ppermute(v, 'edge', [(s, (s + 4) % 8) for s in range(8)])  17.2 us
    pallas_call x1, Pallas kernels, on_device(): kernel_call(backward_kernel, 9, 8, (whole, whole, piece, piece, piece, pi...  9.49 us
    pallas_call x1, Pallas kernels, on_device(): kernel_call(forward_kernel, 17, 0, (piece, piece, piece, piece, square, k...  8.25 us
    ppermute x4, waiting for transfers between devices, across(): return lax.ppermute(v, 'edge', [(s, (s + 4) % 8) for s in range(8)])  5.83 us
    pallas_call x1, Pallas kernels, on_device(): kernel_call(prep_kernel, 1, 1, (shaped(groups, TURN_ROWS, 256), shaped(gr...  4.58 us
  transfers between devices with their start and end apart: 26, of which 8 were waited for; matrix products, arithmetic and copies ran while one was open for 7% of the time, Pallas kernels for 21%

profile of v6, /device:TPU:8, one launch (start us, length us, event | category | flops | bytes accessed | tf_op | source)
XLA Modules:
  0.0 107.0 jit_solution(3223387799628899652)
XLA Ops:
  0.6 0.0 copy-start
  0.6 7.3 %collective-permute-start = (bf16[8,6272]{1,0:T(8,128)(2,1)}, bf16[8,6272]{1,0:T(8,128)(2,1)S(1)}, u32[]{:S(2)}, u32[]{:S(2)}) collective-permute-start(bf16[8,6272]{1,0:T(8,128)(2,1)} %bitcast.29), channel_id=1, source_target_pairs={{0,4},{1,5},{2,6},{3,7},{4,0},{5,1},{6,2},{7,3},{8,12},{9,13},{10,... | collective-permute-start | bytes 301064 | tf_op jit(solution)/shard_map/ppermute | solution.py:309
  7.9 0.8 broadcast_multiply_fusion
  8.8 0.9 fusion.5
  9.7 0.8 collective-permute-start.5
  10.5 0.7 convert.20
  11.2 0.7 convert.21
  12.5 0.1 fusion.11
  12.6 0.0 collective-permute-done
  12.6 0.9 pad_maximum_fusion.first
  13.5 1.5 %collective-permute-start.1 = (bf16[16,6400]{1,0:T(8,128)(2,1)S(1)}, bf16[16,6400]{1,0:T(8,128)(2,1)S(1)}, u32[]{:S(2)}, u32[]{:S(2)}) collective-permute-start(bf16[16,6400]{1,0:T(8,128)(2,1)S(1)} %pad_maximum_fusion.first), channel_id=1, source_target_pairs={{0,248},{8,16},{16,8},{24,32},{32,24},{40,48},{48,40},{56,64},{64,... | collective-permute-start | bytes 614408 | tf_op jit(solution)/shard_map/ppermute | solution.py:318
  15.0 3.0 %collective-permute-start.10 = (bf16[16,6400]{1,0:T(8,128)(2,1)S(1)}, bf16[16,6400]{1,0:T(8,128)(2,1)S(1)}, u32[]{:S(2)}, u32[]{:S(2)}) collective-permute-start(bf16[16,6400]{1,0:T(8,128)(2,1)S(1)} %pad_maximum_fusion.first), channel_id=1, source_target_pairs={{0,2},{1,3},{2,0},{3,1},{4,6},{5,7},{6,4},{7,5},{8,10},{9,11},{10,... | collective-permute-start | bytes 614408 | tf_op jit(solution)/shard_map/ppermute | solution.py:312
  18.0 0.6 collective-permute-start.11
  18.6 2.6 %collective-permute-start.9 = (bf16[16,6400]{1,0:T(8,128)(2,1)S(1)}, bf16[16,6400]{1,0:T(8,128)(2,1)S(1)}, u32[]{:S(2)}, u32[]{:S(2)}) collective-permute-start(bf16[16,6400]{1,0:T(8,128)(2,1)S(1)} %pad_maximum_fusion.first), channel_id=1, source_target_pairs={{0,3},{1,0},{2,1},{3,2},{4,7},{5,4},{6,5},{7,6},{8,11},{9,8},{10,9... | collective-permute-start | bytes 614408 | tf_op jit(solution)/shard_map/ppermute | solution.py:312
  21.2 0.7 fusion.38.tgt
  21.9 0.7 fusion.39
  22.6 0.1 copy.23.tgt
  22.7 0.8 copy-done.1
  23.6 4.6 %shard_map.184 = (bf16[8,464,256]{2,1,0:T(8,128)(2,1)S(1)}, bf16[8,784,256]{2,1,0:T(8,128)(2,1)}) custom-call(bf16[235,128]{1,0:T(8,128)(2,1)S(1)} %copy-done.1, bf16[16,6400]{1,0:T(8,128)(2,1)S(1)} %pad_maximum_fusion.first), custom_call_target="tpu_custom_call" | custom-call | flops 2000000000 | bytes 6000000 | tf_op jit(solution)/shard_map/pallas_call | solution.py:348
  28.1 0.0 collective-permute-done.1.far0
  28.2 0.1 collective-permute-start.2
  28.2 0.0 collective-permute-done.10
  28.3 1.4 %collective-permute-start.3 = (bf16[16,6400]{1,0:T(8,128)(2,1)S(1)}, bf16[16,6400]{1,0:T(8,128)(2,1)S(1)}, u32[]{:S(2)}, u32[]{:S(2)}) collective-permute-start(bf16[16,6400]{1,0:T(8,128)(2,1)S(1)} %collective-permute-done.1.far0), channel_id=1, source_target_pairs={{0,2},{1,3},{2,0},{3,1},{4,6},{5,7},{6,4},{7,5},{8,10},{9,11},{10,... | collective-permute-start | bytes 614408 | tf_op jit(solution)/shard_map/ppermute | solution.py:312
  29.7 0.7 collective-permute-start.4
  30.4 0.6 collective-permute-start.12
  31.0 0.0 collective-permute-done.5
  31.0 5.1 %collective-permute-done.2.far1 = bf16[16,6400]{1,0:T(8,128)(2,1)S(1)} collective-permute-done((bf16[16,6400]{1,0:T(8,128)(2,1)S(1)}, bf16[16,6400]{1,0:T(8,128)(2,1)S(1)}, u32[]{:S(2)}, u32[]{:S(2)}) %collective-permute-start.2) | collective-permute-done | bytes 204832 | tf_op jit(solution)/shard_map/ppermute | solution.py:312
  36.1 1.7 %collective-permute-done.3.far2 = bf16[16,6400]{1,0:T(8,128)(2,1)S(1)} collective-permute-done((bf16[16,6400]{1,0:T(8,128)(2,1)S(1)}, bf16[16,6400]{1,0:T(8,128)(2,1)S(1)}, u32[]{:S(2)}, u32[]{:S(2)}) %collective-permute-start.3) | collective-permute-done | bytes 204832 | tf_op jit(solution)/shard_map/ppermute | solution.py:312
  37.8 4.3 %collective-permute-done.4.far3 = bf16[16,6400]{1,0:T(8,128)(2,1)S(1)} collective-permute-done((bf16[16,6400]{1,0:T(8,128)(2,1)S(1)}, bf16[16,6400]{1,0:T(8,128)(2,1)S(1)}, u32[]{:S(2)}, u32[]{:S(2)}) %collective-permute-start.4) | collective-permute-done | bytes 204832 | tf_op jit(solution)/shard_map/ppermute | solution.py:312
  42.2 0.9 pad_maximum_fusion.1.up0
  43.1 1.1 %collective-permute-start.6 = (bf16[16,6272]{1,0:T(8,128)(2,1)S(1)}, bf16[16,6272]{1,0:T(8,128)(2,1)S(1)}, u32[]{:S(2)}, u32[]{:S(2)}) collective-permute-start(bf16[16,6272]{1,0:T(8,128)(2,1)S(1)} %pad_maximum_fusion.1.up0), channel_id=1, source_target_pairs={{0,3},{1,0},{2,1},{3,2},{4,7},{5,4},{6,5},{7,6},{8,11},{9,8},{10,9... | collective-permute-start | bytes 602120 | tf_op jit(solution)/shard_map/ppermute | solution.py:312
  44.2 0.7 collective-permute-start.7
  44.9 0.8 collective-permute-start.8
  45.7 0.0 collective-permute-done.12.partner
  45.7 0.1 slice_bitcast_fusion
  45.8 0.1 pad_add_fusion
  45.9 0.1 select_reduce_fusion
  46.0 0.1 copy.22.src
  46.2 8.3 %shard_map.185 = (bf16[16,6272]{1,0:T(8,128)(2,1)S(1)}, bf16[16,6272]{1,0:T(8,128)(2,1)S(1)}, bf16[16,6272]{1,0:T(8,128)(2,1)S(1)}, bf16[16,6272]{1,0:T(8,128)(2...) custom-call(bf16[64,6400]{1,0:T(8,128)(2,1)S(1)} %constant_dynamic-update-slice_fusion.own, ...), custom_call_target="tpu_custom_call" | custom-call | flops 4000000000 | bytes 20000000 | tf_op jit(solution)/shard_map/pallas_call | solution.py:408
  54.4 1.9 %collective-permute-start.13 = (bf16[16,6272]{1,0:T(8,128)(2,1)S(1)}, bf16[16,6272]{1,0:T(8,128)(2,1)S(1)}, u32[]{:S(2)}, u32[]{:S(2)}) collective-permute-start(bf16[16,6272]{1,0:T(8,128)(2,1)S(1)} %get-tuple-element.71), channel_id=1, source_target_pairs={{0,1},{1,2},{2,3},{3,0},{4,5},{5,6},{6,7},{7,4},{8,9},{9,10},{10,1... | collective-permute-start | bytes 602120 | tf_op jit(solution)/shard_map/ppermute | solution.py:312
  56.4 1.9 %collective-permute-start.14 = (bf16[16,6272]{1,0:T(8,128)(2,1)S(1)}, bf16[16,6272]{1,0:T(8,128)(2,1)S(1)}, u32[]{:S(2)}, u32[]{:S(2)}) collective-permute-start(bf16[16,6272]{1,0:T(8,128)(2,1)S(1)} %get-tuple-element.72), channel_id=1, source_target_pairs={{0,2},{1,3},{2,0},{3,1},{4,6},{5,7},{6,4},{7,5},{8,10},{9,11},{10,... | collective-permute-start | bytes 602120 | tf_op jit(solution)/shard_map/ppermute | solution.py:312
  58.3 2.4 %collective-permute-start.15 = (bf16[16,6272]{1,0:T(8,128)(2,1)S(1)}, bf16[16,6272]{1,0:T(8,128)(2,1)S(1)}, u32[]{:S(2)}, u32[]{:S(2)}) collective-permute-start(bf16[16,6272]{1,0:T(8,128)(2,1)S(1)} %get-tuple-element.73), channel_id=1, source_target_pairs={{0,3},{1,0},{2,1},{3,2},{4,7},{5,4},{6,5},{7,6},{8,11},{9,8},{10,9... | collective-permute-start | bytes 602120 | tf_op jit(solution)/shard_map/ppermute | solution.py:312
  60.7 9.5 %shard_map.186 = (bf16[64,6272]{1,0:T(8,128)(2,1)S(1)}, bf16[64,6272]{1,0:T(8,128)(2,1)S(1)}, bf16[16,6272]{1,0:T(8,128)(2,1)S(1)}, bf16[16,6272]{1,0:T(8,128)(2...) custom-call(bf16[16,6272]{1,0:T(8,128)(2,1)S(1)} %pad_maximum_fusion.1.up0, ...), custom_call_target="tpu_custom_call" | custom-call | flops 5000000000 | bytes 20000000 | tf_op jit(solution)/shard_map/pallas_call | solution.py:423
  70.2 0.1 convert_add_fusion.1
  70.3 0.1 collective-permute-start.18
  70.4 1.5 %collective-permute-start.19 = (bf16[16,6272]{1,0:T(8,128)(2,1)S(1)}, bf16[16,6272]{1,0:T(8,128)(2,1)S(1)}, u32[]{:S(2)}, u32[]{:S(2)}) collective-permute-start(bf16[16,6272]{1,0:T(8,128)(2,1)S(1)} %get-tuple-element.79), channel_id=1, source_target_pairs={{0,2},{1,3},{2,0},{3,1},{4,6},{5,7},{6,4},{7,5},{8,10},{9,11},{10,... | collective-permute-start | bytes 602120 | tf_op jit(solution)/shard_map/ppermute | solution.py:312
  71.9 1.7 %collective-permute-start.20 = (bf16[16,6272]{1,0:T(8,128)(2,1)S(1)}, bf16[16,6272]{1,0:T(8,128)(2,1)S(1)}, u32[]{:S(2)}, u32[]{:S(2)}) collective-permute-start(bf16[16,6272]{1,0:T(8,128)(2,1)S(1)} %get-tuple-element.80), channel_id=1, source_target_pairs={{0,3},{1,0},{2,1},{3,2},{4,7},{5,4},{6,5},{7,6},{8,11},{9,8},{10,9... | collective-permute-start | bytes 602120 | tf_op jit(solution)/shard_map/ppermute | solution.py:312
  73.6 7.6 %collective-permute-done.18 = bf16[16,6272]{1,0:T(8,128)(2,1)S(1)} collective-permute-done((bf16[16,6272]{1,0:T(8,128)(2,1)S(1)}, bf16[16,6272]{1,0:T(8,128)(2,1)S(1)}, u32[]{:S(2)}, u32[]{:S(2)}) %collective-permute-start.18) | collective-permute-done | bytes 200736 | tf_op jit(solution)/shard_map/ppermute | solution.py:312
  81.2 0.6 collective-permute-done.20
  81.8 0.1 add_convert_fusion.1
  81.9 0.2 add_convert_fusion
  82.1 0.0 copy-start.6
  82.1 0.0 copy-start.5
  82.2 0.1 fusion.36
  82.2 0.3 collective-permute-start.21
  82.5 3.6 %collective-permute-start.22 = (bf16[16,6272]{1,0:T(8,128)(2,1)S(1)}, bf16[16,6272]{1,0:T(8,128)(2,1)S(1)}, u32[]{:S(2)}, u32[]{:S(2)}) collective-permute-start(bf16[16,6272]{1,0:T(8,128)(2,1)S(1)} %get-tuple-element.83), channel_id=1, source_target_pairs={{0,2},{1,3},{2,0},{3,1},{4,6},{5,7},{6,4},{7,5},{8,10},{9,11},{10,... | collective-permute-start | bytes 602120 | tf_op jit(solution)/shard_map/ppermute | solution.py:312
  86.1 5.0 %collective-permute-start.16 = (bf16[8,6272]{1,0:T(8,128)(2,1)S(1)}, bf16[8,6272]{1,0:T(8,128)(2,1)S(1)}, u32[]{:S(2)}, u32[]{:S(2)}) collective-permute-start(bf16[8,6272]{1,0:T(8,128)(2,1)S(1)} %slice.88), channel_id=1, source_target_pairs={{0,4},{1,5},{2,6},{3,7},{4,0},{5,1},{6,2},{7,3},{8,12},{9,13},{10,... | collective-permute-start | bytes 301064 | tf_op jit(solution)/shard_map/ppermute | solution.py:309
  91.1 3.5 %collective-permute-done.22 = bf16[16,6272]{1,0:T(8,128)(2,1)S(1)} collective-permute-done((bf16[16,6272]{1,0:T(8,128)(2,1)S(1)}, bf16[16,6272]{1,0:T(8,128)(2,1)S(1)}, u32[]{:S(2)}, u32[]{:S(2)}) %collective-permute-start.22) | collective-permute-done | bytes 200736 | tf_op jit(solution)/shard_map/ppermute | solution.py:312
  94.6 0.8 collective-permute-done.24
  95.4 0.1 convert_add_fusion
  95.6 4.2 %collective-permute-start.25 = (bf16[8,6272]{1,0:T(8,128)(2,1)S(1)}, bf16[8,6272]{1,0:T(8,128)(2,1)S(1)}, u32[]{:S(2)}, u32[]{:S(2)}) collective-permute-start(bf16[8,6272]{1,0:T(8,128)(2,1)S(1)} %slice.87), channel_id=1, source_target_pairs={{0,4},{1,5},{2,6},{3,7},{4,0},{5,1},{6,2},{7,3},{8,12},{9,13},{10,... | collective-permute-start | bytes 301064 | tf_op jit(solution)/shard_map/ppermute | solution.py:309
  99.8 0.7 fusion.4
  100.5 5.8 %collective-permute-done.25 = bf16[8,6272]{1,0:T(8,128)(2,1)S(1)} collective-permute-done((bf16[8,6272]{1,0:T(8,128)(2,1)S(1)}, bf16[8,6272]{1,0:T(8,128)(2,1)S(1)}, u32[]{:S(2)}, u32[]{:S(2)}) %collective-permute-start.25) | collective-permute-done | bytes 100384 | tf_op jit(solution)/shard_map/ppermute | solution.py:309
  106.3 0.7 convert_add_fusion.2
  (37 shorter events, 0.2 us)
Async XLA Ops:
  0.6 7.3 %copy-start = (f32[100,128]{1,0:T(8,128)S(1)}, f32[100,128]{1,0:T(8,128)}, u32[]{:S(2)}) copy-start(f32[100,128]{1,0:T(8,128)} %param.19) | copy-start | bytes 153604
  0.6 11.9 %collective-permute-start = (bf16[8,6272]{1,0:T(8,128)(2,1)}, bf16[8,6272]{1,0:T(8,128)(2,1)S(1)}, u32[]{:S(2)}, u32[]{:S(2)}) collective-permute-start(bf16[8,6272]{1,0:T(8,128)(2,1)} %bitcast.29), channel_id=1, source_target_pairs={{0,4},{1,5},{2,6},{3,7},{4,0},{5,1},{6,2},{7,3},{8,12},{9,13},{10,... | collective-permute-start | bytes 301064 | tf_op jit(solution)/shard_map/ppermute | solution.py:309
  9.7 21.3 %collective-permute-start.5 = (bf16[8,6272]{1,0:T(8,128)(2,1)S(1)}, bf16[8,6272]{1,0:T(8,128)(2,1)}, u32[]{:S(2)}, u32[]{:S(2)}) collective-permute-start(bf16[8,6272]{1,0:T(8,128)(2,1)S(1)} %fusion.5), channel_id=1, source_target_pairs={{0,4},{1,5},{2,6},{3,7},{4,0},{5,1},{6,2},{7,3},{8,12},{9,13},{10,... | collective-permute-start | bytes 301064 | tf_op jit(solution)/shard_map/ppermute | solution.py:309
  13.5 14.7 %collective-permute-start.1 = (bf16[16,6400]{1,0:T(8,128)(2,1)S(1)}, bf16[16,6400]{1,0:T(8,128)(2,1)S(1)}, u32[]{:S(2)}, u32[]{:S(2)}) collective-permute-start(bf16[16,6400]{1,0:T(8,128)(2,1)S(1)} %pad_maximum_fusion.first), channel_id=1, source_target_pairs={{0,248},{8,16},{16,8},{24,32},{32,24},{40,48},{48,40},{56,64},{64,... | collective-permute-start | bytes 614408 | tf_op jit(solution)/shard_map/ppermute | solution.py:318
  15.0 13.3 %collective-permute-start.10 = (bf16[16,6400]{1,0:T(8,128)(2,1)S(1)}, bf16[16,6400]{1,0:T(8,128)(2,1)S(1)}, u32[]{:S(2)}, u32[]{:S(2)}) collective-permute-start(bf16[16,6400]{1,0:T(8,128)(2,1)S(1)} %pad_maximum_fusion.first), channel_id=1, source_target_pairs={{0,2},{1,3},{2,0},{3,1},{4,6},{5,7},{6,4},{7,5},{8,10},{9,11},{10,... | collective-permute-start | bytes 614408 | tf_op jit(solution)/shard_map/ppermute | solution.py:312
  18.0 11.7 %collective-permute-start.11 = (bf16[16,6400]{1,0:T(8,128)(2,1)S(1)}, bf16[16,6400]{1,0:T(8,128)(2,1)S(1)}, u32[]{:S(2)}, u32[]{:S(2)}) collective-permute-start(bf16[16,6400]{1,0:T(8,128)(2,1)S(1)} %pad_maximum_fusion.first), channel_id=1, source_target_pairs={{0,1},{1,2},{2,3},{3,0},{4,5},{5,6},{6,7},{7,4},{8,9},{9,10},{10,1... | collective-permute-start | bytes 614408 | tf_op jit(solution)/shard_map/ppermute | solution.py:312
  18.6 11.8 %collective-permute-start.9 = (bf16[16,6400]{1,0:T(8,128)(2,1)S(1)}, bf16[16,6400]{1,0:T(8,128)(2,1)S(1)}, u32[]{:S(2)}, u32[]{:S(2)}) collective-permute-start(bf16[16,6400]{1,0:T(8,128)(2,1)S(1)} %pad_maximum_fusion.first), channel_id=1, source_target_pairs={{0,3},{1,0},{2,1},{3,2},{4,7},{5,4},{6,5},{7,6},{8,11},{9,8},{10,9... | collective-permute-start | bytes 614408 | tf_op jit(solution)/shard_map/ppermute | solution.py:312
  22.7 0.8 copy-start.1
  28.1 17.9 %copy-start.4 = (bf16[8,464,256]{2,1,0:T(8,128)(2,1)}, bf16[8,464,256]{2,1,0:T(8,128)(2,1)S(1)}, u32[]{:S(2)}) copy-start(bf16[8,464,256]{2,1,0:T(8,128)(2,1)S(1)} %get-tuple-element.56.turn) | copy-start | bytes 5701636
  28.1 2.9 %copy-start.7 = (s32[128]{0:T(128)S(1)}, s32[128]{0:T(128)}, u32[]{:S(2)}) copy-start(s32[128]{0:T(128)} %param.20) | copy-start | bytes 1540
  28.1 18.0 %copy-start.2 = (bf16[128,128]{1,0:T(8,128)(2,1)S(1)}, bf16[128,128]{1,0:T(8,128)(2,1)}, u32[]{:S(2)}) copy-start(bf16[128,128]{1,0:T(8,128)(2,1)} %basis.1) | copy-start | bytes 98308
  28.1 18.0 %copy-start.3 = (bf16[128,128]{1,0:T(8,128)(2,1)S(1)}, bf16[128,128]{1,0:T(8,128)(2,1)}, u32[]{:S(2)}) copy-start(bf16[128,128]{1,0:T(8,128)(2,1)} %w_rad.3) | copy-start | bytes 98308
  28.2 8.0 %collective-permute-start.2 = (bf16[16,6400]{1,0:T(8,128)(2,1)S(1)}, bf16[16,6400]{1,0:T(8,128)(2,1)S(1)}, u32[]{:S(2)}, u32[]{:S(2)}) collective-permute-start(bf16[16,6400]{1,0:T(8,128)(2,1)S(1)} %collective-permute-done.1.far0), channel_id=1, source_target_pairs={{0,3},{1,0},{2,1},{3,2},{4,7},{5,4},{6,5},{7,6},{8,11},{9,8},{10,9... | collective-permute-start | bytes 614408 | tf_op jit(solution)/shard_map/ppermute | solution.py:312
  28.3 9.6 %collective-permute-start.3 = (bf16[16,6400]{1,0:T(8,128)(2,1)S(1)}, bf16[16,6400]{1,0:T(8,128)(2,1)S(1)}, u32[]{:S(2)}, u32[]{:S(2)}) collective-permute-start(bf16[16,6400]{1,0:T(8,128)(2,1)S(1)} %collective-permute-done.1.far0), channel_id=1, source_target_pairs={{0,2},{1,3},{2,0},{3,1},{4,6},{5,7},{6,4},{7,5},{8,10},{9,11},{10,... | collective-permute-start | bytes 614408 | tf_op jit(solution)/shard_map/ppermute | solution.py:312
  29.7 12.5 %collective-permute-start.4 = (bf16[16,6400]{1,0:T(8,128)(2,1)S(1)}, bf16[16,6400]{1,0:T(8,128)(2,1)S(1)}, u32[]{:S(2)}, u32[]{:S(2)}) collective-permute-start(bf16[16,6400]{1,0:T(8,128)(2,1)S(1)} %collective-permute-done.1.far0), channel_id=1, source_target_pairs={{0,1},{1,2},{2,3},{3,0},{4,5},{5,6},{6,7},{7,4},{8,9},{9,10},{10,1... | collective-permute-start | bytes 614408 | tf_op jit(solution)/shard_map/ppermute | solution.py:312
  30.4 15.3 %collective-permute-start.12 = (bf16[64,6400]{1,0:T(8,128)(2,1)S(1)}, bf16[64,6400]{1,0:T(8,128)(2,1)S(1)}, u32[]{:S(2)}, u32[]{:S(2)}) collective-permute-start(bf16[64,6400]{1,0:T(8,128)(2,1)S(1)} %constant_dynamic-update-slice_fusion.own), channel_id=1, source_target_pairs={{0,8},{8,0},{16,24},{24,16},{32,40},{40,32},{48,56},{56,48},{64,72... | collective-permute-start | bytes 2457608 | tf_op jit(solution)/shard_map/ppermute | solution.py:315
  43.1 15.2 %collective-permute-start.6 = (bf16[16,6272]{1,0:T(8,128)(2,1)S(1)}, bf16[16,6272]{1,0:T(8,128)(2,1)S(1)}, u32[]{:S(2)}, u32[]{:S(2)}) collective-permute-start(bf16[16,6272]{1,0:T(8,128)(2,1)S(1)} %pad_maximum_fusion.1.up0), channel_id=1, source_target_pairs={{0,3},{1,0},{2,1},{3,2},{4,7},{5,4},{6,5},{7,6},{8,11},{9,8},{10,9... | collective-permute-start | bytes 602120 | tf_op jit(solution)/shard_map/ppermute | solution.py:312
  44.2 16.5 %collective-permute-start.7 = (bf16[16,6272]{1,0:T(8,128)(2,1)S(1)}, bf16[16,6272]{1,0:T(8,128)(2,1)S(1)}, u32[]{:S(2)}, u32[]{:S(2)}) collective-permute-start(bf16[16,6272]{1,0:T(8,128)(2,1)S(1)} %pad_maximum_fusion.1.up0), channel_id=1, source_target_pairs={{0,2},{1,3},{2,0},{3,1},{4,6},{5,7},{6,4},{7,5},{8,10},{9,11},{10,... | collective-permute-start | bytes 602120 | tf_op jit(solution)/shard_map/ppermute | solution.py:312
  44.9 15.8 %collective-permute-start.8 = (bf16[16,6272]{1,0:T(8,128)(2,1)S(1)}, bf16[16,6272]{1,0:T(8,128)(2,1)S(1)}, u32[]{:S(2)}, u32[]{:S(2)}) collective-permute-start(bf16[16,6272]{1,0:T(8,128)(2,1)S(1)} %pad_maximum_fusion.1.up0), channel_id=1, source_target_pairs={{0,1},{1,2},{2,3},{3,0},{4,5},{5,6},{6,7},{7,4},{8,9},{9,10},{10,1... | collective-permute-start | bytes 602120 | tf_op jit(solution)/shard_map/ppermute | solution.py:312
  54.4 15.8 %collective-permute-start.13 = (bf16[16,6272]{1,0:T(8,128)(2,1)S(1)}, bf16[16,6272]{1,0:T(8,128)(2,1)S(1)}, u32[]{:S(2)}, u32[]{:S(2)}) collective-permute-start(bf16[16,6272]{1,0:T(8,128)(2,1)S(1)} %get-tuple-element.71), channel_id=1, source_target_pairs={{0,1},{1,2},{2,3},{3,0},{4,5},{5,6},{6,7},{7,4},{8,9},{9,10},{10,1... | collective-permute-start | bytes 602120 | tf_op jit(solution)/shard_map/ppermute | solution.py:312
  56.4 13.8 %collective-permute-start.14 = (bf16[16,6272]{1,0:T(8,128)(2,1)S(1)}, bf16[16,6272]{1,0:T(8,128)(2,1)S(1)}, u32[]{:S(2)}, u32[]{:S(2)}) collective-permute-start(bf16[16,6272]{1,0:T(8,128)(2,1)S(1)} %get-tuple-element.72), channel_id=1, source_target_pairs={{0,2},{1,3},{2,0},{3,1},{4,6},{5,7},{6,4},{7,5},{8,10},{9,11},{10,... | collective-permute-start | bytes 602120 | tf_op jit(solution)/shard_map/ppermute | solution.py:312
  58.3 11.9 %collective-permute-start.15 = (bf16[16,6272]{1,0:T(8,128)(2,1)S(1)}, bf16[16,6272]{1,0:T(8,128)(2,1)S(1)}, u32[]{:S(2)}, u32[]{:S(2)}) collective-permute-start(bf16[16,6272]{1,0:T(8,128)(2,1)S(1)} %get-tuple-element.73), channel_id=1, source_target_pairs={{0,3},{1,0},{2,1},{3,2},{4,7},{5,4},{6,5},{7,6},{8,11},{9,8},{10,9... | collective-permute-start | bytes 602120 | tf_op jit(solution)/shard_map/ppermute | solution.py:312
  70.3 10.9 %collective-permute-start.18 = (bf16[16,6272]{1,0:T(8,128)(2,1)S(1)}, bf16[16,6272]{1,0:T(8,128)(2,1)S(1)}, u32[]{:S(2)}, u32[]{:S(2)}) collective-permute-start(bf16[16,6272]{1,0:T(8,128)(2,1)S(1)} %get-tuple-element.78), channel_id=1, source_target_pairs={{0,1},{1,2},{2,3},{3,0},{4,5},{5,6},{6,7},{7,4},{8,9},{9,10},{10,1... | collective-permute-start | bytes 602120 | tf_op jit(solution)/shard_map/ppermute | solution.py:312
  70.4 10.8 %collective-permute-start.19 = (bf16[16,6272]{1,0:T(8,128)(2,1)S(1)}, bf16[16,6272]{1,0:T(8,128)(2,1)S(1)}, u32[]{:S(2)}, u32[]{:S(2)}) collective-permute-start(bf16[16,6272]{1,0:T(8,128)(2,1)S(1)} %get-tuple-element.79), channel_id=1, source_target_pairs={{0,2},{1,3},{2,0},{3,1},{4,6},{5,7},{6,4},{7,5},{8,10},{9,11},{10,... | collective-permute-start | bytes 602120 | tf_op jit(solution)/shard_map/ppermute | solution.py:312
  71.9 9.9 %collective-permute-start.20 = (bf16[16,6272]{1,0:T(8,128)(2,1)S(1)}, bf16[16,6272]{1,0:T(8,128)(2,1)S(1)}, u32[]{:S(2)}, u32[]{:S(2)}) collective-permute-start(bf16[16,6272]{1,0:T(8,128)(2,1)S(1)} %get-tuple-element.80), channel_id=1, source_target_pairs={{0,3},{1,0},{2,1},{3,2},{4,7},{5,4},{6,5},{7,6},{8,11},{9,8},{10,9... | collective-permute-start | bytes 602120 | tf_op jit(solution)/shard_map/ppermute | solution.py:312
  73.6 8.3 %collective-permute-start.17 = (bf16[64,6272]{1,0:T(8,128)(2,1)S(1)}, bf16[64,6272]{1,0:T(8,128)(2,1)S(1)}, u32[]{:S(2)}, u32[]{:S(2)}) collective-permute-start(bf16[64,6272]{1,0:T(8,128)(2,1)S(1)} %get-tuple-element.76), channel_id=1, source_target_pairs={{0,8},{8,0},{16,24},{24,16},{32,40},{40,32},{48,56},{56,48},{64,72... | collective-permute-start | bytes 2408456 | tf_op jit(solution)/shard_map/ppermute | solution.py:315
  82.1 17.6 %copy-start.6 = (bf16[8,49,128]{2,0,1:T(8,128)(2,1)S(1)}, bf16[8,49,128]{2,0,1:T(8,128)(2,1)}, u32[]{:S(2)}) copy-start(bf16[8,49,128]{2,0,1:T(8,128)(2,1)} %param.17) | copy-start | bytes 301060
  82.1 24.1 %copy-start.5 = (bf16[8,49,128]{2,0,1:T(8,128)(2,1)S(1)}, bf16[8,49,128]{2,0,1:T(8,128)(2,1)}, u32[]{:S(2)}) copy-start(bf16[8,49,128]{2,0,1:T(8,128)(2,1)} %param.33) | copy-start | bytes 301060
  82.2 8.9 %collective-permute-start.21 = (bf16[16,6272]{1,0:T(8,128)(2,1)S(1)}, bf16[16,6272]{1,0:T(8,128)(2,1)S(1)}, u32[]{:S(2)}, u32[]{:S(2)}) collective-permute-start(bf16[16,6272]{1,0:T(8,128)(2,1)S(1)} %get-tuple-element.82), channel_id=1, source_target_pairs={{0,1},{1,2},{2,3},{3,0},{4,5},{5,6},{6,7},{7,4},{8,9},{9,10},{10,1... | collective-permute-start | bytes 602120 | tf_op jit(solution)/shard_map/ppermute | solution.py:312
  82.5 12.1 %collective-permute-start.22 = (bf16[16,6272]{1,0:T(8,128)(2,1)S(1)}, bf16[16,6272]{1,0:T(8,128)(2,1)S(1)}, u32[]{:S(2)}, u32[]{:S(2)}) collective-permute-start(bf16[16,6272]{1,0:T(8,128)(2,1)S(1)} %get-tuple-element.83), channel_id=1, source_target_pairs={{0,2},{1,3},{2,0},{3,1},{4,6},{5,7},{6,4},{7,5},{8,10},{9,11},{10,... | collective-permute-start | bytes 602120 | tf_op jit(solution)/shard_map/ppermute | solution.py:312
  86.1 8.5 %collective-permute-start.23 = (bf16[16,6272]{1,0:T(8,128)(2,1)S(1)}, bf16[16,6272]{1,0:T(8,128)(2,1)S(1)}, u32[]{:S(2)}, u32[]{:S(2)}) collective-permute-start(bf16[16,6272]{1,0:T(8,128)(2,1)S(1)} %get-tuple-element.84), channel_id=1, source_target_pairs={{0,3},{1,0},{2,1},{3,2},{4,7},{5,4},{6,5},{7,6},{8,11},{9,8},{10,9... | collective-permute-start | bytes 602120 | tf_op jit(solution)/shard_map/ppermute | solution.py:312
  86.1 9.3 %collective-permute-start.24 = (bf16[16,6272]{1,0:T(8,128)(2,1)S(1)}, bf16[16,6272]{1,0:T(8,128)(2,1)S(1)}, u32[]{:S(2)}, u32[]{:S(2)}) collective-permute-start(bf16[16,6272]{1,0:T(8,128)(2,1)S(1)} %add_convert_fusion.1), channel_id=1, source_target_pairs={{0,248},{8,16},{16,8},{24,32},{32,24},{40,48},{48,40},{56,64},{64,... | collective-permute-start | bytes 602120 | tf_op jit(solution)/shard_map/ppermute | solution.py:318
  86.1 13.6 %collective-permute-start.16 = (bf16[8,6272]{1,0:T(8,128)(2,1)S(1)}, bf16[8,6272]{1,0:T(8,128)(2,1)S(1)}, u32[]{:S(2)}, u32[]{:S(2)}) collective-permute-start(bf16[8,6272]{1,0:T(8,128)(2,1)S(1)} %slice.88), channel_id=1, source_target_pairs={{0,4},{1,5},{2,6},{3,7},{4,0},{5,1},{6,2},{7,3},{8,12},{9,13},{10,... | collective-permute-start | bytes 301064 | tf_op jit(solution)/shard_map/ppermute | solution.py:309
  95.6 10.7 %collective-permute-start.25 = (bf16[8,6272]{1,0:T(8,128)(2,1)S(1)}, bf16[8,6272]{1,0:T(8,128)(2,1)S(1)}, u32[]{:S(2)}, u32[]{:S(2)}) collective-permute-start(bf16[8,6272]{1,0:T(8,128)(2,1)S(1)} %slice.87), channel_id=1, source_target_pairs={{0,4},{1,5},{2,6},{3,7},{4,0},{5,1},{6,2},{7,3},{8,12},{9,13},{10,... | collective-permute-start | bytes 301064 | tf_op jit(solution)/shard_map/ppermute | solution.py:309
